TPU v7x, 128 devices: a whole 4x4x4 slice. The times are simulated.
128 devices in a mesh: exp: 8 (over y, z_hi), gy: 4 (over z_lo, core), gz: 4 (over x).
Axes of the slice: x: 4, y: 4, z: 4 (z_hi: 2, z_lo: 2; z = z_hi * 2 + z_lo), core: 2. Of those that a mesh axis runs over, the one named last changes fastest.
Arguments:
- adjoint_final: float32 [8, 128, 128, 1024], P('exp', None, 'gy', 'gz'), may hold values from -6 to 6
- concentration: bfloat16 [2, 8, 128, 128, 1024], P(None, 'exp', None, 'gy', 'gz'), may hold values from 0 to 1
- observed: bfloat16 [2, 8, 128, 128, 1024], P(None, 'exp', None, 'gy', 'gz'), may hold values from 0 to 1
- capacity: float32 [128, 128, 1024], P(None, 'gy', 'gz'), may hold values from 0.03 to 0.3
- pore_mask: int32 [128, 128, 1024], P(None, 'gy', 'gz'), may hold values 0 or 1
- feed_index: int32 [8], P('exp'), may hold values from 0 to 7
- feed_affinity: float32 [8], replicated, may hold values from 0.5 to 4
Outputs:
- adjoint_first: float32 [8, 128, 128, 1024], P('exp', None, 'gy', 'gz')
- capacity_grad: float32 [128, 128, 1024], P('exp', 'gy', 'gz')
All inputs are finite; a program needn't handle non-finite values. No bound on the sum of `pore_mask` on one device may be relied on, other than what follows from the above.
Results may differ from a plain program's by a relative error of at most 0.0003.
Values sent between devices are 32-bit elements; how exact they have to be, the bound alone decides.
No kernel may reach another device: no remote copies, remote signals or barrier semaphores. Data moves between devices by JAX's collectives and lax.ppermute only.
A program may use at most 128 MiB of HBM per device.

v0:
```python
import jax
import jax.numpy as jnp
from jax import lax
from jax.sharding import PartitionSpec as P


def padded(cells, sides, width):
    for axis, dim in sides:
        count = lax.axis_size(axis)
        ends = count - 1
        head = lax.slice_in_dim(cells, 0, width, axis=dim)
        tail = lax.slice_in_dim(cells, cells.shape[dim] - width, cells.shape[dim], axis=dim)
        cells = jnp.concatenate(
            [
                lax.ppermute(tail, axis, [(i, (i + 1) % count) for i in range(ends)]),
                cells,
                lax.ppermute(head, axis, [((i + 1) % count, i) for i in range(ends)]),
            ],
            axis=dim,
        )
    return cells


def face_flux(near_adj, near_pores, adjoint):
    return near_pores * (near_adj - adjoint)


def adjoint_update(adjoint_wide, pores_wide, capacity, affinity, filled_low, observed_low):
    adjoint = adjoint_wide[:, 1:-1, 1:-1]
    pores = pores_wide[:, 1:-1, 1:-1]
    adjoint_x = jnp.pad(adjoint, ((1, 1), (0, 0), (0, 0)))
    pores_x = jnp.pad(pores, ((1, 1), (0, 0), (0, 0)))
    dispersion = face_flux(adjoint_x[2:], pores_x[2:], adjoint) + face_flux(
        adjoint_x[:-2], pores_x[:-2], adjoint
    )
    dispersion = dispersion + face_flux(adjoint_wide[:, 2:, 1:-1], pores_wide[:, 2:, 1:-1], adjoint)
    dispersion = dispersion + face_flux(
        adjoint_wide[:, :-2, 1:-1], pores_wide[:, :-2, 1:-1], adjoint
    )
    dispersion = dispersion + face_flux(adjoint_wide[:, 1:-1, 2:], pores_wide[:, 1:-1, 2:], adjoint)
    dispersion = dispersion + face_flux(
        adjoint_wide[:, 1:-1, :-2], pores_wide[:, 1:-1, :-2], adjoint
    )
    pores_next = jnp.concatenate([pores[1:], jnp.ones_like(pores[:1])], 0)
    adjoint_next = jnp.concatenate([adjoint[1:], jnp.zeros_like(adjoint[:1])], 0)
    transport = pores_next * (adjoint_next - adjoint)
    filled = filled_low.astype(jnp.float32)
    saturation = 1.0 + affinity * filled
    uptake = capacity * affinity / (saturation * saturation)
    updated = pores * (
        adjoint
        + 0.1 * dispersion
        + 0.2 * transport
        - uptake * adjoint
        + (filled - observed_low.astype(jnp.float32))
    )
    gradient_term = -pores * affinity * filled / saturation * adjoint
    return (updated, gradient_term)


def shards(adjoint_final, concentration, observed, capacity, pore_mask, feed_index, feed_affinity):
    pores_wide = padded(pore_mask, (("gy", 1), ("gz", 2)), 1).astype(jnp.float32)
    feeds = jnp.arange(feed_affinity.shape[0], dtype=jnp.int32)
    affinity = jnp.sum(
        jnp.where(feeds == feed_index[0], feed_affinity, jnp.zeros_like(feed_affinity))
    )
    adjoint = adjoint_final[0]
    length = adjoint.shape[0]
    share = length // lax.axis_size("exp")
    gradient = jnp.zeros_like(adjoint)
    for moment in reversed(range(concentration.shape[0])):
        adjoint_wide = padded(adjoint, (("gy", 1), ("gz", 2)), 1)
        adjoint, gradient_term = adjoint_update(
            adjoint_wide,
            pores_wide,
            capacity,
            affinity,
            concentration[moment, 0],
            observed[moment, 0],
        )
        gradient = gradient + gradient_term
    summed = lax.psum(gradient, "exp")
    owned = lax.dynamic_slice_in_dim(summed, lax.axis_index("exp") * share, share, 0)
    return (adjoint[None], owned)


def solution(mesh):
    in_specs = (
        P("exp", None, "gy", "gz"),
        P(None, "exp", None, "gy", "gz"),
        P(None, "exp", None, "gy", "gz"),
        P(None, "gy", "gz"),
        P(None, "gy", "gz"),
        P("exp"),
        P(),
    )
    out_specs = (P("exp", None, "gy", "gz"), P("exp", "gy", "gz"))
    return jax.shard_map(shards, mesh=mesh, in_specs=in_specs, out_specs=out_specs, check_vma=False)
```

profile of v0, /device:TPU:1, one launch (start us, length us, event | category | flops | bytes accessed | tf_op | source)
XLA Modules:
  0.0 325.6 jit_solution(10019507288806775459)
XLA Ops:
  7.2 0.0 all-reduce.8.cloned.1.call-start
  7.2 1.7 fusion.66
  9.0 4.9 %collective-permute-start = (s32[128,1,256]{2,0,1:T(8,128)S(1)}, s32[128,1,256]{2,0,1:T(8,128)S(1)}, u32[]{:S(2)}, u32[]{:S(2)}) collective-permute-start(s32[128,1,256]{2,0,1:T(8,128)S(1)} %copy.35), channel_id=1, source_target_pairs={{0,4},{4,8},{8,12},{1,5},{5,9},{9,13},{2,6},{6,10},{10,14},{3,7},{... | collective-permute-start | bytes 393224 | tf_op jit(solution)/shard_map/ppermute | solution.py:15
  13.9 1.9 collective-permute-start.1
  15.9 6.0 %copy.14 = f32[1,128,32,256]{1,2,3,0:T(8,128)} copy(f32[1,128,32,256]{3,2,1,0:T(8,128)} %param.7) | data formatting | bytes 8388608 | tf_op args[0]
  21.8 1.7 fusion.64
  23.6 0.1 copy.15
  23.7 1.9 collective-permute-start.4
  25.6 0.1 copy.17
  25.7 0.0 copy-start.4
  25.7 3.9 %collective-permute-start.5 = (f32[128,1,256]{2,0,1:T(8,128)S(1)}, f32[128,1,256]{2,0,1:T(8,128)S(1)}, u32[]{:S(2)}, u32[]{:S(2)}) collective-permute-start(f32[128,1,256]{2,0,1:T(8,128)S(1)} %copy.17), channel_id=1, source_target_pairs={{0,4},{4,8},{8,12},{1,5},{5,9},{9,13},{2,6},{6,10},{10,14},{3,7},{... | collective-permute-start | bytes 393224 | tf_op jit(solution)/shard_map/ppermute | solution.py:15
  29.6 5.3 %slice_bitcast_fusion = f32[127,32,256]{0,1,2:T(8,128)} fusion(f32[1,128,32,256]{1,2,3,0:T(8,128)} %copy.14), kind=kLoop, calls=%fused_computation.72 | loop fusion | bytes 8323072 | tf_op jit(solution)/shard_map/slice | solution.py:45
  34.9 2.6 fusion.65
  37.5 1.1 copy-done.5
  38.6 1.8 fusion.62
  41.0 0.7 fusion.60
  41.7 5.9 %copy.12 = s32[128,32,256]{0,1,2:T(8,128)} copy(s32[128,32,256]{2,1,0:T(8,128)} %param.11) | data formatting | bytes 8388608 | tf_op args[4]
  47.6 5.2 %copy.39 = bf16[1,1,128,32,256]{2,3,4,1,0:T(8,128)(2,1)} copy(bf16[1,1,128,32,256]{4,3,2,1,0:T(8,128)(2,1)} %get-tuple-element.19) | data formatting | bytes 4194304
  52.8 5.2 %copy.37 = bf16[1,1,128,32,256]{2,3,4,1,0:T(8,128)(2,1)} copy(bf16[1,1,128,32,256]{4,3,2,1,0:T(8,128)(2,1)} %get-tuple-element.18) | data formatting | bytes 4194304
  57.9 4.0 %copy.38 = bf16[1,1,128,32,256]{2,3,4,1,0:T(8,128)(2,1)} copy(bf16[1,1,128,32,256]{4,3,2,1,0:T(8,128)(2,1)S(1)} %get-tuple-element.13) | data formatting | bytes 4194304
  62.0 6.0 %copy.22 = f32[128,32,256]{0,1,2:T(8,128)} copy(f32[128,32,256]{2,1,0:T(8,128)} %param.10) | data formatting | bytes 8388608 | tf_op args[3]
  67.9 0.0 collective-permute-done
  67.9 0.1 copy.11
  68.0 0.0 collective-permute-done.1
  68.0 0.1 copy.13
  68.1 0.8 pad_add_fusion.2
  68.9 3.1 collective-permute-start.2
  72.0 1.3 collective-permute-start.3
  73.3 0.0 collective-permute-done.4
  73.3 0.1 copy.16
  73.4 0.0 collective-permute-done.5
  73.4 0.1 copy.18
  73.5 0.0 copy-start.2
  73.5 0.9 pad_maximum_fusion.21
  74.4 1.4 collective-permute-start.6
  75.9 4.8 %collective-permute-start.7 = (f32[128,34,1]{0,1,2:T(8,128)S(1)}, f32[128,34,1]{0,1,2:T(8,128)S(1)}, u32[]{:S(2)}, u32[]{:S(2)}) collective-permute-start(f32[128,34,1]{0,1,2:T(8,128)S(1)} %get-tuple-element.9), channel_id=1, source_target_pairs={{0,1},{1,2},{2,3},{4,5},{5,6},{6,7},{8,9},{9,10},{10,11},{12,13},{... | collective-permute-start | bytes 52232 | tf_op jit(solution)/shard_map/ppermute | solution.py:15
  80.7 0.0 collective-permute-done.2
  80.7 0.0 collective-permute-done.3
  80.7 1.9 add_convert_fusion
  82.6 3.1 slice.173
  85.7 3.2 slice.180
  89.0 0.0 collective-permute-done.6
  89.0 32.2 %fusion.9 = (f32[128,32,256]{0,1,2:T(8,128)}, f32[128,32,256]{0,1,2:T(8,128)}) fusion(bf16[1,1,128,32,256]{2,3,4,1,0:T(8,128)(2,1)} %copy.39, bf16[1,1,128,32,256]{2,3,4,1,0:T(8,128)(2,1)} %copy.37, f32[]{:T(128)} %fusion.60, f32[1,128,32,256]{1,2,3,0:T(8,128)} %copy.14, f32[128,34,258]{0,1,2:T(8,128)S(1)} %add_convert_fusion, f32[128,32,256]{0,1,2:T(8,128)} %slice.173, ...), kind=kLoop, calls=%fused_computation.22 | loop fusion | flops 57671680 | bytes 61048836 | tf_op jit(solution)/shard_map/add | solution.py:81
  121.1 0.0 all-reduce.8.cloned.1.call-update
  121.2 1.7 fusion.63
  122.9 0.1 copy.25
  123.0 1.9 collective-permute-start.8
  124.9 0.1 copy.27
  125.0 3.6 %collective-permute-start.9 = (f32[128,1,256]{2,0,1:T(8,128)S(1)}, f32[128,1,256]{2,0,1:T(8,128)S(1)}, u32[]{:S(2)}, u32[]{:S(2)}) collective-permute-start(f32[128,1,256]{2,0,1:T(8,128)S(1)} %copy.27), channel_id=1, source_target_pairs={{0,4},{4,8},{8,12},{1,5},{5,9},{9,13},{2,6},{6,10},{10,14},{3,7},{... | collective-permute-start | bytes 393224 | tf_op jit(solution)/shard_map/ppermute | solution.py:15
  128.7 0.6 collective-permute-done.8
  129.3 0.1 copy.26
  129.4 1.2 collective-permute-done.9
  130.6 0.1 copy.28
  130.7 0.8 pad_maximum_fusion.18
  131.4 1.3 collective-permute-start.10
  132.7 4.2 %collective-permute-start.11 = (f32[128,34,1]{0,1,2:T(8,128)S(1)}, f32[128,34,1]{0,1,2:T(8,128)S(1)}, u32[]{:S(2)}, u32[]{:S(2)}) collective-permute-start(f32[128,34,1]{0,1,2:T(8,128)S(1)} %get-tuple-element.7), channel_id=1, source_target_pairs={{0,1},{1,2},{2,3},{4,5},{5,6},{6,7},{8,9},{9,10},{10,11},{12,13},{... | collective-permute-start | bytes 52232 | tf_op jit(solution)/shard_map/ppermute | solution.py:15
  137.0 0.0 slice-start
  137.0 5.4 %copy.40 = bf16[1,1,128,32,256]{2,3,4,1,0:T(8,128)(2,1)} copy(bf16[1,1,128,32,256]{4,3,2,1,0:T(8,128)(2,1)} %get-tuple-element.12) | data formatting | bytes 4194304
  142.3 5.6 %slice.184 = f32[127,32,256]{0,1,2:T(8,128)} slice(f32[128,32,256]{0,1,2:T(8,128)} %get-tuple-element.5), slice={[1:128], [0:32], [0:256]} | slice | bytes 8323072 | tf_op jit(solution)/shard_map/slice | solution.py:45
  148.0 18.8 %fusion.59 = f32[1,128,32,256]{1,2,3,0:T(8,128)} fusion(f32[128,32,256]{0,1,2:T(8,128)} %slice.173, f32[128,32,256]{0,1,2:T(8,128)S(1)} %copy-done.1, f32[127,32,256]{0,1,2:T(8,128)} %slice.184, f32[128,1,256]{0,1,2:T(1,128)S(1)} %copy.26, f32[128,1,256]{0,1,2:T(1,128)S(1)} %copy.28, f32[128,34,1]{0,1,2:T(8,128)S(1)} %collective-permute-done.11, ...), kind=kLoop, calls=%fused_computation.89 | loop fusion | flops 45088768 | bytes 46368772 | tf_op jit(solution)/shard_map/broadcast_in_dim | solution.py:84
  166.8 5.6 %copy.33 = f32[1,128,32,256]{3,2,1,0:T(8,128)} copy(f32[1,128,32,256]{1,2,3,0:T(8,128)} %fusion.59) | data formatting | bytes 8388608
  172.4 136.6 %all-reduce.8.cloned.1.call-done = f32[128,32,256]{0,1,2:T(8,128)} async-done(((f32[128,32,256]{0,1,2:T(8,128)}), f32[128,32,256]{0,1,2:T(8,128)}) %all-reduce.8.cloned.1.call-update) | async-done | bytes 4194320 | tf_op jit(solution)/shard_map/psum | solution.py:82
  309.0 5.3 %constant_dynamic-slice_fusion = f32[16,32,256]{0,1,2:T(8,128)} fusion(f32[128,32,256]{0,1,2:T(8,128)} %all-reduce.8.cloned.1.call-done, s32[]{:T(128)S(6)} %select_n.8), kind=kLoop, calls=%fused_computation.101 | loop fusion | bytes 1048580 | tf_op jit(solution)/shard_map/dynamic_slice | solution.py:83
  314.3 4.5 %copy.34 = f32[16,32,256]{2,1,0:T(8,128)} copy(f32[16,32,256]{0,1,2:T(8,128)} %constant_dynamic-slice_fusion) | data formatting | bytes 1048576
  (20 shorter events, 0.1 us)
Async XLA Ops:
  7.2 301.8 %all-reduce.8.cloned.1.call-start = ((), (), s32[]{:S(2)}) async-start(), calls=%async_computation | async-start | bytes 8388608 | tf_op jit(solution)/shard_map/psum | solution.py:82
  9.0 59.0 %collective-permute-start = (s32[128,1,256]{2,0,1:T(8,128)S(1)}, s32[128,1,256]{2,0,1:T(8,128)S(1)}, u32[]{:S(2)}, u32[]{:S(2)}) collective-permute-start(s32[128,1,256]{2,0,1:T(8,128)S(1)} %copy.35), channel_id=1, source_target_pairs={{0,4},{4,8},{8,12},{1,5},{5,9},{9,13},{2,6},{6,10},{10,14},{3,7},{... | collective-permute-start | bytes 393224 | tf_op jit(solution)/shard_map/ppermute | solution.py:15
  13.9 54.1 %collective-permute-start.1 = (s32[128,1,256]{2,0,1:T(8,128)S(1)}, s32[128,1,256]{2,0,1:T(8,128)S(1)}, u32[]{:S(2)}, u32[]{:S(2)}) collective-permute-start(s32[128,1,256]{2,0,1:T(8,128)S(1)} %copy.36), channel_id=1, source_target_pairs={{4,0},{8,4},{12,8},{5,1},{9,5},{13,9},{6,2},{10,6},{14,10},{7,3},{... | collective-permute-start | bytes 393224 | tf_op jit(solution)/shard_map/ppermute | solution.py:17
  23.7 49.6 %collective-permute-start.4 = (f32[128,1,256]{2,0,1:T(8,128)S(1)}, f32[128,1,256]{2,0,1:T(8,128)S(1)}, u32[]{:S(2)}, u32[]{:S(2)}) collective-permute-start(f32[128,1,256]{2,0,1:T(8,128)S(1)} %copy.15), channel_id=1, source_target_pairs={{4,0},{8,4},{12,8},{5,1},{9,5},{13,9},{6,2},{10,6},{14,10},{7,3},{... | collective-permute-start | bytes 393224 | tf_op jit(solution)/shard_map/ppermute | solution.py:17
  25.7 9.2 %copy-start.4 = (bf16[2,1,128,32,256]{4,3,2,1,0:T(8,128)(2,1)S(1)}, bf16[2,1,128,32,256]{4,3,2,1,0:T(8,128)(2,1)}, u32[]{:S(2)}) copy-start(bf16[2,1,128,32,256]{4,3,2,1,0:T(8,128)(2,1)} %param.8) | copy-start | bytes 12582916
  25.7 47.7 %collective-permute-start.5 = (f32[128,1,256]{2,0,1:T(8,128)S(1)}, f32[128,1,256]{2,0,1:T(8,128)S(1)}, u32[]{:S(2)}, u32[]{:S(2)}) collective-permute-start(f32[128,1,256]{2,0,1:T(8,128)S(1)} %copy.17), channel_id=1, source_target_pairs={{0,4},{4,8},{8,12},{1,5},{5,9},{9,13},{2,6},{6,10},{10,14},{3,7},{... | collective-permute-start | bytes 393224 | tf_op jit(solution)/shard_map/ppermute | solution.py:15
  34.9 3.7 %copy-start.5 = (bf16[2,1,128,32,256]{4,3,2,1,0:T(8,128)(2,1)S(1)}, bf16[2,1,128,32,256]{4,3,2,1,0:T(8,128)(2,1)}, u32[]{:S(2)}) copy-start(bf16[2,1,128,32,256]{4,3,2,1,0:T(8,128)(2,1)} %param.9) | copy-start | bytes 12582916
  38.6 2.4 copy-start.6
  68.9 11.8 %collective-permute-start.2 = (s32[128,34,1]{0,1,2:T(8,128)S(1)}, s32[128,34,1]{0,1,2:T(8,128)S(1)}, u32[]{:S(2)}, u32[]{:S(2)}) collective-permute-start(s32[128,34,1]{0,1,2:T(8,128)S(1)} %get-tuple-element.10), channel_id=1, source_target_pairs={{0,1},{1,2},{2,3},{4,5},{5,6},{6,7},{8,9},{9,10},{10,11},{12,13},{... | collective-permute-start | bytes 52232 | tf_op jit(solution)/shard_map/ppermute | solution.py:15
  72.0 8.7 %collective-permute-start.3 = (s32[128,34,1]{0,1,2:T(8,128)S(1)}, s32[128,34,1]{0,1,2:T(8,128)S(1)}, u32[]{:S(2)}, u32[]{:S(2)}) collective-permute-start(s32[128,34,1]{0,1,2:T(8,128)S(1)} %get-tuple-element.11), channel_id=1, source_target_pairs={{1,0},{2,1},{3,2},{5,4},{6,5},{7,6},{9,8},{10,9},{11,10},{13,12},{... | collective-permute-start | bytes 52232 | tf_op jit(solution)/shard_map/ppermute | solution.py:17
  73.5 7.2 %copy-start.2 = (s32[128,32,256]{0,1,2:T(8,128)S(1)}, s32[128,32,256]{0,1,2:T(8,128)}, u32[]{:S(2)}) copy-start(s32[128,32,256]{0,1,2:T(8,128)} %copy.12) | copy-start | bytes 12582916
  74.4 14.5 %collective-permute-start.6 = (f32[128,34,1]{0,1,2:T(8,128)S(1)}, f32[128,34,1]{0,1,2:T(8,128)S(1)}, u32[]{:S(2)}, u32[]{:S(2)}) collective-permute-start(f32[128,34,1]{0,1,2:T(8,128)S(1)} %get-tuple-element.8), channel_id=1, source_target_pairs={{1,0},{2,1},{3,2},{5,4},{6,5},{7,6},{9,8},{10,9},{11,10},{13,12},{... | collective-permute-start | bytes 52232 | tf_op jit(solution)/shard_map/ppermute | solution.py:17
  75.9 13.1 %collective-permute-start.7 = (f32[128,34,1]{0,1,2:T(8,128)S(1)}, f32[128,34,1]{0,1,2:T(8,128)S(1)}, u32[]{:S(2)}, u32[]{:S(2)}) collective-permute-start(f32[128,34,1]{0,1,2:T(8,128)S(1)} %get-tuple-element.9), channel_id=1, source_target_pairs={{0,1},{1,2},{2,3},{4,5},{5,6},{6,7},{8,9},{9,10},{10,11},{12,13},{... | collective-permute-start | bytes 52232 | tf_op jit(solution)/shard_map/ppermute | solution.py:15
  82.6 6.3 %copy-start = (f32[128,34,258]{0,1,2:T(8,128)}, f32[128,34,258]{0,1,2:T(8,128)S(1)}, u32[]{:S(2)}) copy-start(f32[128,34,258]{0,1,2:T(8,128)S(1)} %add_convert_fusion) | copy-start | bytes 13473796
  123.0 6.3 %collective-permute-start.8 = (f32[128,1,256]{2,0,1:T(8,128)S(1)}, f32[128,1,256]{2,0,1:T(8,128)S(1)}, u32[]{:S(2)}, u32[]{:S(2)}) collective-permute-start(f32[128,1,256]{2,0,1:T(8,128)S(1)} %copy.25), channel_id=1, source_target_pairs={{4,0},{8,4},{12,8},{5,1},{9,5},{13,9},{6,2},{10,6},{14,10},{7,3},{... | collective-permute-start | bytes 393224 | tf_op jit(solution)/shard_map/ppermute | solution.py:17
  125.0 5.6 %collective-permute-start.9 = (f32[128,1,256]{2,0,1:T(8,128)S(1)}, f32[128,1,256]{2,0,1:T(8,128)S(1)}, u32[]{:S(2)}, u32[]{:S(2)}) collective-permute-start(f32[128,1,256]{2,0,1:T(8,128)S(1)} %copy.27), channel_id=1, source_target_pairs={{0,4},{4,8},{8,12},{1,5},{5,9},{9,13},{2,6},{6,10},{10,14},{3,7},{... | collective-permute-start | bytes 393224 | tf_op jit(solution)/shard_map/ppermute | solution.py:15
  131.4 16.5 %collective-permute-start.10 = (f32[128,34,1]{0,1,2:T(8,128)S(1)}, f32[128,34,1]{0,1,2:T(8,128)S(1)}, u32[]{:S(2)}, u32[]{:S(2)}) collective-permute-start(f32[128,34,1]{0,1,2:T(8,128)S(1)} %get-tuple-element.6), channel_id=1, source_target_pairs={{1,0},{2,1},{3,2},{5,4},{6,5},{7,6},{9,8},{10,9},{11,10},{13,12},{... | collective-permute-start | bytes 52232 | tf_op jit(solution)/shard_map/ppermute | solution.py:17
  132.7 15.2 %collective-permute-start.11 = (f32[128,34,1]{0,1,2:T(8,128)S(1)}, f32[128,34,1]{0,1,2:T(8,128)S(1)}, u32[]{:S(2)}, u32[]{:S(2)}) collective-permute-start(f32[128,34,1]{0,1,2:T(8,128)S(1)} %get-tuple-element.7), channel_id=1, source_target_pairs={{0,1},{1,2},{2,3},{4,5},{5,6},{6,7},{8,9},{9,10},{10,11},{12,13},{... | collective-permute-start | bytes 52232 | tf_op jit(solution)/shard_map/ppermute | solution.py:15
  137.0 11.0 %slice-start = ((s8[5283840]{0:T(1024)(128)(4,1)}), s8[1089536]{0:T(1024)(128)(4,1)S(1)}, s32[]{:S(2)}) async-start(s8[5283840]{0:T(1024)(128)(4,1)} %bitcast.24), calls=%async_computation.1 | async-start | bytes 2179072
  137.0 11.0 %copy-start.3 = (bf16[1,1,128,32,256]{2,3,4,1,0:T(8,128)(2,1)S(1)}, bf16[1,1,128,32,256]{2,3,4,1,0:T(8,128)(2,1)}, u32[]{:S(2)}) copy-start(bf16[1,1,128,32,256]{2,3,4,1,0:T(8,128)(2,1)} %copy.39) | copy-start | bytes 6291460
  142.3 5.6 %slice-start.1 = ((s8[5283840]{0:T(1024)(128)(4,1)}), s8[4194304]{0:T(1024)(128)(4,1)S(1)}, s32[]{:S(2)}) async-start(s8[5283840]{0:T(1024)(128)(4,1)} %bitcast.24), calls=%async_computation.2 | async-start | bytes 8388608
  142.3 5.6 %copy-start.1 = (f32[128,32,256]{0,1,2:T(8,128)S(1)}, f32[128,32,256]{0,1,2:T(8,128)}, u32[]{:S(2)}) copy-start(f32[128,32,256]{0,1,2:T(8,128)} %get-tuple-element.5) | copy-start | bytes 12582916
Sparse Core Ops, SparseCore 0:
  121.3 187.6 all-reduce.7
where the time goes:
time: 329 us; the launch traced here: 326 us
  waiting for transfers between devices  138 us (42%)
  local copies, waits for them, and re-layouts  81.7 us (25%)
  other arithmetic  56 us (17%)
  starting transfers between devices  34.4 us (10%)
  between operations  15 us (5%)
    psum x1, waiting for transfers between devices, shards(): summed = lax.psum(gradient, 'exp')  137 us
    unnamed x29, local copies, waits for them, and re-layouts  48.8 us
    add x1, other arithmetic, shards(): gradient = gradient + gradient_term  32.2 us
    ppermute x6, starting transfers between devices, padded(): lax.ppermute(tail, axis, [(i, (i + 1) % count) for i in range(ends)])  24.6 us
    broadcast_in_dim x1, other arithmetic, shards(): return (adjoint[None], owned)  18.8 us
    slice x2, local copies, waits for them, and re-layouts, adjoint_update(): adjoint[1:]  10.9 us
    ppermute x6, starting transfers between devices, padded(): lax.ppermute(head, axis, [((i + 1) % count, i) for i in range(ends)])  9.75 us
  transfers between devices with their start and end apart: 13, of which 3 were waited for; matrix products, arithmetic and copies ran while one was open for 29% of the time, Pallas kernels for 0%

commit v1 on v0

v1 whole, which is shorter than its diff:
```python
import functools

import jax
import jax.numpy as jnp
from jax import lax
from jax.experimental import pallas as pl
from jax.experimental.pallas import tpu as pltpu
from jax.sharding import PartitionSpec as P

F32 = jnp.float32
VMEM_LIMIT = 40 * 1024 * 1024


def reciprocal(value):
    guess = pl.reciprocal(value, approx=True)
    return guess * (2.0 - value * guess)


def lane_to(values, source, target):
    lanes = values.shape[1]
    shift = target - source
    if isinstance(shift, int):
        return pltpu.roll(values, shift % lanes, 1)
    return pltpu.roll(values, lax.rem(shift + lanes, lanes), 1)


def beside_sum(centre, y_low, y_high, z_low, z_high):
    ny, nz = centre.shape
    row = lax.broadcasted_iota(jnp.int32, (ny, nz), 0)
    col = lax.broadcasted_iota(jnp.int32, (ny, nz), 1)
    reps = nz // z_low.shape[1]
    z_low = jnp.concatenate([z_low] * reps, 1)
    z_high = jnp.concatenate([z_high] * reps, 1)
    total = jnp.where(row == 0, y_low, pltpu.roll(centre, 1, 0))
    total = total + jnp.where(row == ny - 1, y_high, pltpu.roll(centre, ny - 1, 0))
    total = total + jnp.where(col == 0, z_low, pltpu.roll(centre, 1, 1))
    return total + jnp.where(col == nz - 1, z_high, pltpu.roll(centre, nz - 1, 1))


def window(start, planes, nx):
    return jnp.clip(start - 1, 0, nx - planes - 2)


def gather_window(start, planes, nx, adj_ref, pore_ref, m_scr, p_scr, masked):
    base = window(start, planes, nx)

    def body(j, _):
        x = start - 1 + j
        at = jnp.clip(x - base, 0, planes + 1)
        inside = jnp.logical_and(x >= 0, x < nx).astype(F32)
        pores = pore_ref[at].astype(F32) * inside
        p_scr[j] = pores
        m_scr[j] = adj_ref[at] * (inside if masked else pores)
        return 0

    lax.fori_loop(0, planes + 2, body, 0)


def halo_column(ref, part, rows, x, target):
    values = ref[part * rows : (part + 1) * rows, :]
    return lane_to(values, x, target)


def couplings(i, x, nx, m_scr, p_scr, m_halo, p_halo):
    m_c = m_scr[i + 1]
    p_c = p_scr[i + 1]
    m_sum = m_scr[i] + 3.0 * m_scr[i + 2] + beside_sum(m_c, *m_halo)
    p_sum = p_scr[i] + 3.0 * p_scr[i + 2] + beside_sum(p_c, *p_halo)
    kept = jnp.where(x == nx - 1, 0.8, 1.0)
    return m_c, p_c, 0.1 * m_sum, kept - 0.1 * p_sum


def halos(x, ny, part_m, y_low, y_high, z_low, z_high):
    lanes = z_low.shape[1]
    return (
        y_low[part_m, pl.ds(x, 1), :],
        y_high[part_m, pl.ds(x, 1), :],
        halo_column(z_low, part_m, ny, x, 0),
        halo_column(z_high, part_m, ny, x, lanes - 1),
    )


def faces_kernel(adj_ref, pore_ref, y_low, y_high, z_low, z_high):
    planes, ny, nz = adj_ref.shape
    nx = z_low.shape[1]
    step = pl.program_id(0)
    lane = lax.broadcasted_iota(jnp.int32, (ny, nx), 1)

    def body(i, carry):
        x = step * planes + i
        pores = pore_ref[i].astype(F32)
        out = list(carry)
        for part, value in enumerate((adj_ref[i] * pores, pores)):
            y_low[part, pl.ds(x, 1), :] = value[:1]
            y_high[part, pl.ds(x, 1), :] = value[ny - 1 :]
            out[part] = jnp.where(lane == x, lane_to(value[:, :nx], 0, x), out[part])
            out[2 + part] = jnp.where(lane == x, lane_to(value[:, nz - nx :], nx - 1, x), out[2 + part])
        return tuple(out)

    parts = [z_low[:ny], z_low[ny:], z_high[:ny], z_high[ny:]]
    parts = lax.fori_loop(0, planes, body, tuple(parts))
    z_low[:ny], z_low[ny:], z_high[:ny], z_high[ny:] = parts


def faces(adjoint, pores, planes=16):
    nx, ny, nz = adjoint.shape
    block = pl.BlockSpec((planes, ny, nz), lambda t: (t, 0, 0))
    y_spec = pl.BlockSpec((2, nx, nz), lambda t: (0, 0, 0))
    z_spec = pl.BlockSpec((2 * ny, nx), lambda t: (0, 0))
    y_shape = jax.ShapeDtypeStruct((2, nx, nz), F32)
    z_shape = jax.ShapeDtypeStruct((2 * ny, nx), F32)
    return pl.pallas_call(
        faces_kernel,
        grid=(nx // planes,),
        in_specs=[block, block],
        out_specs=[y_spec, y_spec, z_spec, z_spec],
        out_shape=[y_shape, y_shape, z_shape, z_shape],
        compiler_params=pltpu.CompilerParams(vmem_limit_bytes=VMEM_LIMIT),
        cost_estimate=pl.CostEstimate(flops=nx * ny * nz, bytes_accessed=8 * nx * ny * nz, transcendentals=0),
        name="faces",
    )(adjoint, pores)


def stage_kernel(first, count, planes, nx, split, has_prior, *refs):
    (table, which, affinities, adj, pore, cap, f_late, f_early, o_late, y_low, y_high, z_low, z_high), refs = refs[:13], refs[13:]
    prior = ()
    if has_prior:
        prior, refs = refs[1:5], refs[5:]
    next_adj, *next_faces = refs[:5]
    outs, (m_scr, p_scr) = refs[5:-2], refs[-2:]
    ny, nz = cap.shape[1:]
    step = pl.program_id(0)
    start = table[first + step]
    affinity = affinities[which[0]]
    out_y_low, out_y_high, out_z_low, out_z_high = next_faces

    if has_prior:

        @pl.when(step == 0)
        def _():
            for new, old in zip(next_faces, prior):
                new[...] = old[...]

    gather_window(start, planes, nx, adj, pore, m_scr, p_scr, False)
    lane = lax.broadcasted_iota(jnp.int32, (ny, nx), 1)

    def run(grad_ref):
        def body(i, carry):
            low, high = carry
            x = start + i
            m_halo = halos(x, ny, 0, y_low, y_high, z_low, z_high)
            p_halo = halos(x, ny, 1, y_low, y_high, z_low, z_high)
            m_c, p_c, inflow, kept = couplings(i, x, nx, m_scr, p_scr, m_halo, p_halo)
            filled = f_late[i].astype(F32)
            late = reciprocal(1.0 + affinity * filled)
            kept = kept - cap[i] * (affinity * late * late)
            updated = m_c * kept + p_c * (inflow + (filled - o_late[i].astype(F32)))
            next_adj[i] = updated
            early = reciprocal(1.0 + affinity * f_early[i].astype(F32))
            grad_ref[i] = (late - 1.0) * m_c + (early - 1.0) * updated
            out_y_low[pl.ds(x, 1), :] = updated[:1]
            out_y_high[pl.ds(x, 1), :] = updated[ny - 1 :]
            low = jnp.where(lane == x, lane_to(updated[:, :nx], 0, x), low)
            high = jnp.where(lane == x, lane_to(updated[:, nz - nx :], nx - 1, x), high)
            return low, high

        low, high = lax.fori_loop(0, planes, body, (out_z_low[...], out_z_high[...]))
        out_z_low[...] = low
        out_z_high[...] = high

    if split:
        for k, grad_ref in enumerate(outs):
            pl.when(step == k)(functools.partial(run, grad_ref))
    else:
        run(outs[0])


def stage(scalars, fields, halo, prior, first, count, planes, split, name):
    adjoint, pores, capacity, filled, seen = fields
    nx, ny, nz = adjoint.shape
    el = pl.Element
    full = (el(ny), el(nz))

    def at(moment):
        return pl.BlockSpec((el(planes), *full), lambda t, table, *_: (table[first + t] + moment * nx, 0, 0))

    wide = pl.BlockSpec((el(planes + 2), *full), lambda t, table, *_: (window(table[first + t], planes, nx), 0, 0))

    def whole(shape):
        return pl.BlockSpec(shape, lambda t, *_: (0,) * len(shape))

    face_shapes = [(nx, nz), (nx, nz), (ny, nx), (ny, nx)]
    in_specs = [wide, wide, at(0), at(1), at(0), at(1)] + [whole(h.shape) for h in halo]
    operands = [adjoint, pores, capacity, filled, filled, seen, *halo]
    aliases = {}
    if prior is not None:
        aliases = {len(scalars) + len(operands): 0}
        in_specs += [pl.BlockSpec(memory_space=pl.ANY)] + [whole(s) for s in face_shapes]
        operands += list(prior)
    out_specs = [at(0)] + [whole(s) for s in face_shapes]
    out_shape = [jax.ShapeDtypeStruct((nx, ny, nz), F32)] + [jax.ShapeDtypeStruct(s, F32) for s in face_shapes]
    if split:
        out_specs += [whole((planes, ny, nz))] * count
        out_shape += [jax.ShapeDtypeStruct((planes, ny, nz), F32)] * count
    else:
        out_specs += [pl.BlockSpec((planes, ny, nz), lambda t, *_: (t, 0, 0))]
        out_shape += [jax.ShapeDtypeStruct((count * planes, ny, nz), F32)]
    voxels = count * planes * ny * nz
    results = pl.pallas_call(
        functools.partial(stage_kernel, first, count, planes, nx, split, prior is not None),
        grid_spec=pltpu.PrefetchScalarGridSpec(
            num_scalar_prefetch=len(scalars),
            grid=(count,),
            in_specs=in_specs,
            out_specs=out_specs,
            scratch_shapes=[pltpu.VMEM((planes + 2, ny, nz), F32)] * 2,
        ),
        out_shape=out_shape,
        input_output_aliases=aliases,
        compiler_params=pltpu.CompilerParams(vmem_limit_bytes=VMEM_LIMIT),
        cost_estimate=pl.CostEstimate(flops=50 * voxels, bytes_accessed=28 * voxels, transcendentals=2 * voxels),
        name=name,
    )(*scalars, *operands)
    return results[:5], results[5:]


def last_kernel(nx, which, affinities, adj, pore, cap, f_early, o_early, m_yl, m_yh, m_zl, m_zh, y_low, y_high, z_low, z_high, out, m_scr, p_scr):
    planes, ny, _ = cap.shape
    start = pl.program_id(0) * planes
    affinity = affinities[which[0]]
    gather_window(start, planes, nx, adj, pore, m_scr, p_scr, True)

    def body(i, _):
        x = start + i
        lanes = m_zl.shape[1]
        m_halo = (
            m_yl[pl.ds(x, 1), :],
            m_yh[pl.ds(x, 1), :],
            halo_column(m_zl, 0, ny, x, 0),
            halo_column(m_zh, 0, ny, x, lanes - 1),
        )
        p_halo = halos(x, ny, 1, y_low, y_high, z_low, z_high)
        m_c, p_c, inflow, kept = couplings(i, x, nx, m_scr, p_scr, m_halo, p_halo)
        filled = f_early[i].astype(F32)
        early = reciprocal(1.0 + affinity * filled)
        kept = kept - cap[i] * (affinity * early * early)
        out[i] = m_c * kept + p_c * (inflow + (filled - o_early[i].astype(F32)))
        return 0

    lax.fori_loop(0, planes, body, 0)


def last_step(scalars, fields, halo, face_halo, planes=16):
    adjoint, pores, capacity, filled, seen = fields
    nx, ny, nz = adjoint.shape
    el = pl.Element

    block = pl.BlockSpec((planes, ny, nz), lambda t, *_: (t, 0, 0))
    wide = pl.BlockSpec((el(planes + 2), el(ny), el(nz)), lambda t, *_: (window(t * planes, planes, nx), 0, 0))

    def whole(shape):
        return pl.BlockSpec(shape, lambda t, *_: (0,) * len(shape))

    voxels = nx * ny * nz
    return pl.pallas_call(
        functools.partial(last_kernel, nx),
        grid_spec=pltpu.PrefetchScalarGridSpec(
            num_scalar_prefetch=len(scalars),
            grid=(nx // planes,),
            in_specs=[wide, wide, block, block, block] + [whole(h.shape) for h in (*face_halo, *halo)],
            out_specs=block,
            scratch_shapes=[pltpu.VMEM((planes + 2, ny, nz), F32)] * 2,
        ),
        out_shape=jax.ShapeDtypeStruct((nx, ny, nz), F32),
        compiler_params=pltpu.CompilerParams(vmem_limit_bytes=VMEM_LIMIT),
        cost_estimate=pl.CostEstimate(flops=40 * voxels, bytes_accessed=20 * voxels, transcendentals=voxels),
        name="last_step",
    )(*scalars, adjoint, pores, capacity, filled, seen, *face_halo, *halo)


def exchange(y_low, y_high, z_low, z_high):
    received = []
    for axis, low, high in (("gy", y_low, y_high), ("gz", z_low, z_high)):
        count = lax.axis_size(axis)
        up = [(i, i + 1) for i in range(count - 1)]
        down = [(i + 1, i) for i in range(count - 1)]
        received += [lax.ppermute(high, axis, up), lax.ppermute(low, axis, down)]
    return tuple(received)


def shards(ring, adjoint_final, concentration, observed, capacity, pore_mask, feed_index, feed_affinity):
    ranks = lax.axis_size("exp")
    pairs = ranks // ring
    adjoint = adjoint_final[0]
    nx, ny, nz = adjoint.shape
    share = nx // ranks
    size_p = (share * 5) // 8
    size_q = share - size_p
    filled = concentration.reshape(-1, ny, nz)
    seen = observed.reshape(-1, ny, nz)

    rank = lax.axis_index("exp")
    row, half = rank // pairs, rank % pairs

    def send(value, turn, swap):
        perm = [
            (r * pairs + h, ((r + turn) % ring) * pairs + (h + swap) % pairs) for r in range(ring) for h in range(pairs)
        ]
        return lax.ppermute(value, "exp", perm)

    def owner(turn, swap):
        return ((row + turn) % ring) * pairs + (half + swap) % pairs

    order = [(2, 1, 0), (2, 0, 0)]
    order += [(turn, 1, size_p) for turn in range(ring)]
    order += [(1, 0, 0), (3, 1, 0), (1, 1, 0), (3, 0, 0), (0, 1, 0), (0, 0, 0)]
    order += [(turn, 0, size_p) for turn in range(ring)]
    table = jnp.stack([owner(turn, swap) * share + offset for turn, swap, offset in order]).astype(jnp.int32)
    scalars = (table, feed_index, feed_affinity)

    halo = exchange(*faces(adjoint, pore_mask))
    fields = (adjoint, pore_mask, capacity, filled, seen)
    state, (far_s, far_k) = stage(scalars, fields, halo, None, 0, 2, size_p, True, "far")
    got_s, got_k = send(far_s, 1, 0), send(far_k, 3, 0)
    state, (cross,) = stage(scalars, fields, halo, state, 2, 4, size_q, False, "cross")
    crossed = send(cross, 0, 1)
    state, (up_k, dn_s, up_s, dn_k, own_s, own_k) = stage(scalars, fields, halo, state, 6, 6, size_p, True, "near")
    from_low_k, from_high_s = send(up_k, 1, 0), send(dn_s, 3, 0)
    state, (kept,) = stage(scalars, fields, halo, state, 12, 4, size_q, False, "kept")

    next_adjoint, *next_faces = state
    face_halo = exchange(*next_faces)

    from_low_s, from_high_k = send(up_s + got_s, 1, 0), send(dn_k + got_k, 3, 0)
    sums = (kept + crossed).reshape(ring, size_q, ny, nz)
    part_2, part_1, part_3 = send(sums[2], 2, 0), send(sums[1], 1, 0), send(sums[3], 3, 0)
    last_p = send(own_s + from_low_s + from_high_s, 0, 1)

    adjoint_first = last_step((feed_index, feed_affinity), (next_adjoint, pore_mask, capacity, filled, seen), halo, face_halo)

    total_p = own_k + from_low_k + from_high_k + last_p
    total_q = sums[0] + part_1 + part_2 + part_3
    return adjoint_first[None], jnp.concatenate([total_p, total_q], 0)


def solution(mesh):
    in_specs = (
        P("exp", None, "gy", "gz"),
        P(None, "exp", None, "gy", "gz"),
        P(None, "exp", None, "gy", "gz"),
        P(None, "gy", "gz"),
        P(None, "gy", "gz"),
        P("exp"),
        P(),
    )
    out_specs = (P("exp", None, "gy", "gz"), P("exp", "gy", "gz"))
    return jax.shard_map(
        functools.partial(shards, 4), mesh=mesh, in_specs=in_specs, out_specs=out_specs, check_vma=False
    )
```

time: 329 us -> 127 us (0.39)
  waiting for transfers between devices: 138 us -> 3.99 us
  local copies, waits for them, and re-layouts: 81.7 us -> 8.89 us
  Pallas kernels: 0 us -> 68.4 us
  other arithmetic: 56 us -> 1.29 us
  between operations: 15 us -> 1.67 us
  starting transfers between devices: 34.4 us -> 41.8 us
    psum x1 -> x0, waiting for transfers between devices: 137 us -> none  [shards(): summed = lax.psum(gradient, 'exp')]
    pallas_call x0 -> x6, Pallas kernels: none -> 68.4 us  [the longest x4 35.7 us: stage(): pl.pallas_call(functools.partial(stage_kernel, first, count, planes, nx,...]
    unnamed x29 -> x14, local copies, waits for them, and re-layouts: 48.8 us -> 8.75 us
    add x1 -> x6, other arithmetic: 32.2 us -> 0.45 us  [the longest x1 0.13 us: shards(): sums = (kept + crossed).reshape(ring, size_q, ny, nz)]
    slice x13 -> x1, local copies, waits for them, and re-layouts: 27.1 us -> 0.05 us  [shards(): sums[1]]
    broadcast_in_dim x1 -> x0, other arithmetic: 18.8 us -> none  [shards(): return (adjoint[None], owned)]
    ppermute x12 -> x19, starting transfers between devices: 34.4 us -> 41.8 us  [the longest x8 23.9 us: exchange(): received += [lax.ppermute(high, axis, up), lax.ppermute(low, axis, down)]]
    dynamic_slice x1 -> x0, local copies, waits for them, and re-layouts: 5.29 us -> none  [shards(): lax.dynamic_slice_in_dim(summed, lax.axis_index('exp') * share, share, 0)]
  transfers between devices with their start and end apart: 13 -> 19, of which waited for: 3 -> 2; matrix products, arithmetic and copies ran while one was open for 29% -> 0% of each run, Pallas kernels for 0% -> 35%
where the time goes in v1:
time: 127 us; the launch traced here: 126 us
  Pallas kernels  68.4 us (54%)
  starting transfers between devices  41.8 us (33%)
  local copies, waits for them, and re-layouts  8.89 us (7%)
  waiting for transfers between devices  3.99 us (3%)
  between operations  1.67 us (1%)
  other arithmetic  1.29 us (1%)
    pallas_call x4, Pallas kernels, stage(): pl.pallas_call(functools.partial(stage_kernel, first, count, planes, nx,...  35.7 us
    ppermute x8, starting transfers between devices, exchange(): received += [lax.ppermute(high, axis, up), lax.ppermute(low, axis, down)]  23.9 us
    pallas_call x1, Pallas kernels, last_step(): pl.pallas_call(functools.partial(last_kernel, nx), grid_spec=pltpu.Prefet...  21.4 us
    ppermute x11, starting transfers between devices, send(): return lax.ppermute(value, 'exp', perm)  17.9 us
    pallas_call x1, Pallas kernels, faces(): pl.pallas_call(faces_kernel, grid=(nx // planes,), in_specs=[block, block...  11.3 us
    unnamed x14, local copies, waits for them, and re-layouts  8.75 us
  transfers between devices with their start and end apart: 19, of which 2 were waited for; matrix products, arithmetic and copies ran while one was open for 0% of the time, Pallas kernels for 35%

profile of v1, /device:TPU:1, one launch (start us, length us, event | category | flops | bytes accessed | tf_op | source)
XLA Modules:
  0.0 126.0 jit_solution(1968846100828737795)
XLA Ops:
  0.6 0.0 copy-start
  0.6 2.2 %copy-done = s32[128,32,256]{2,1,0:T(8,128)S(1)} copy-done((s32[128,32,256]{2,1,0:T(8,128)S(1)}, s32[128,32,256]{2,1,0:T(8,128)}, u32[]{:S(2)}) %copy-start) | copy-done | bytes 4194328
  2.8 0.0 copy-start.3
  2.8 2.2 %copy-done.3 = f32[1,128,32,256]{3,2,1,0:T(8,128)S(1)} copy-done((f32[1,128,32,256]{3,2,1,0:T(8,128)S(1)}, f32[1,128,32,256]{3,2,1,0:T(8,128)}, u32[]{:S(2)}) %copy-start.3) | copy-done | bytes 4194328
  5.0 0.0 copy-start.6
  5.0 11.3 %faces.1 = (f32[2,128,256]{2,1,0:T(8,128)S(1)}, f32[2,128,256]{2,1,0:T(8,128)S(1)}, f32[64,128]{1,0:T(8,128)S(1)}, f32[64,128]{1,0:T(8,128)S(1)}) custom-call(f32[128,32,256]{2,1,0:T(8,128)S(1)} %bitcast.20, s32[128,32,256]{2,1,0:T(8,128)S(1)} %copy-done), custom_call_target="tpu_custom_call" | custom-call | flops 1048576 | bytes 8388608 | tf_op jit(solution)/shard_map/faces/pallas_call | solution.py:112
  16.3 4.9 %collective-permute-start = (f32[2,128,256]{2,1,0:T(8,128)S(1)}, f32[2,128,256]{2,1,0:T(8,128)S(1)}, u32[]{:S(2)}, u32[]{:S(2)}) collective-permute-start(f32[2,128,256]{2,1,0:T(8,128)S(1)} %get-tuple-element.36), channel_id=1, source_target_pairs={{0,4},{4,8},{8,12},{1,5},{5,9},{9,13},{2,6},{6,10},{10,14},{3,7},{... | collective-permute-start | bytes 786440 | tf_op jit(solution)/shard_map/ppermute | solution.py:287
  21.3 1.9 %collective-permute-start.1 = (f32[2,128,256]{2,1,0:T(8,128)S(1)}, f32[2,128,256]{2,1,0:T(8,128)S(1)}, u32[]{:S(2)}, u32[]{:S(2)}) collective-permute-start(f32[2,128,256]{2,1,0:T(8,128)S(1)} %get-tuple-element.37), channel_id=1, source_target_pairs={{4,0},{8,4},{12,8},{5,1},{9,5},{13,9},{6,2},{10,6},{14,10},{7,3},{... | collective-permute-start | bytes 786440 | tf_op jit(solution)/shard_map/ppermute | solution.py:287
  23.2 3.1 %collective-permute-start.2 = (f32[64,128]{1,0:T(8,128)S(1)}, f32[64,128]{1,0:T(8,128)S(1)}, u32[]{:S(2)}, u32[]{:S(2)}) collective-permute-start(f32[64,128]{1,0:T(8,128)S(1)} %get-tuple-element.38), channel_id=1, source_target_pairs={{0,1},{1,2},{2,3},{4,5},{5,6},{6,7},{8,9},{9,10},{10,11},{12,13},{... | collective-permute-start | bytes 98312 | tf_op jit(solution)/shard_map/ppermute | solution.py:287
  26.3 1.3 %collective-permute-start.3 = (f32[64,128]{1,0:T(8,128)S(1)}, f32[64,128]{1,0:T(8,128)S(1)}, u32[]{:S(2)}, u32[]{:S(2)}) collective-permute-start(f32[64,128]{1,0:T(8,128)S(1)} %get-tuple-element.39), channel_id=1, source_target_pairs={{1,0},{2,1},{3,2},{5,4},{6,5},{7,6},{9,8},{10,9},{11,10},{13,12},{... | collective-permute-start | bytes 98312 | tf_op jit(solution)/shard_map/ppermute | solution.py:287
  28.4 0.1 stack.67.refs_0_
  28.5 0.0 collective-permute-done.2.refs_11_.z_low
  28.5 2.5 %collective-permute-done.3.refs_12_.z_high = f32[64,128]{1,0:T(8,128)S(1)} collective-permute-done((f32[64,128]{1,0:T(8,128)S(1)}, f32[64,128]{1,0:T(8,128)S(1)}, u32[]{:S(2)}, u32[]{:S(2)}) %collective-permute-start.3) | collective-permute-done | bytes 32800 | tf_op jit(solution)/shard_map/ppermute | solution.py:287
  31.0 0.0 collective-permute-done.refs_9_.y_low
  31.0 0.0 collective-permute-done.1.refs_10_.y_high
  31.0 0.0 copy-done.6
  31.0 0.0 copy-start.1
  31.0 2.2 %copy-done.1 = s32[128,32,256]{2,1,0:T(8,128)S(1)} copy-done((s32[128,32,256]{2,1,0:T(8,128)S(1)}, s32[128,32,256]{2,1,0:T(8,128)}, u32[]{:S(2)}) %copy-start.1) | copy-done | bytes 4194328
  33.2 0.0 copy-start.4
  33.2 2.2 %copy-done.4 = f32[1,128,32,256]{3,2,1,0:T(8,128)S(1)} copy-done((f32[1,128,32,256]{3,2,1,0:T(8,128)S(1)}, f32[1,128,32,256]{3,2,1,0:T(8,128)}, u32[]{:S(2)}) %copy-start.4) | copy-done | bytes 4194328
  35.4 6.1 %far.1 = (f32[128,32,256]{2,1,0:T(8,128)S(1)}, f32[128,256]{1,0:T(8,128)S(1)}, f32[128,256]{1,0:T(8,128)S(1)}, f32[32,128]{1,0:T(8,128)S(1)}, f32[32,128]{1,0:T(...) custom-call(s32[16]{0:T(128)S(1)} %stack.67.refs_0_, s32[1]{0:T(128)S(6)} %copy.15.refs_1_.which, ...), custom_call_target="tpu_custom_call" | custom-call | flops 8192000 | bytes 4587520 | tf_op jit(solution)/shard_map/far/pallas_call | solution.py:209
  41.5 7.0 %cross.1 = (f32[128,32,256]{2,1,0:T(8,128)S(1)}, f32[128,256]{1,0:T(8,128)S(1)}, f32[128,256]{1,0:T(8,128)S(1)}, f32[32,128]{1,0:T(8,128)S(1)}, f32[32,128]{1,0:T(8,128)S(1)}, /*index=5*/f32[24,32,256]{2,1,0:T(8,128)S(1)}) custom-call(s32[16]{0:T(128)S(1)} %stack.67.refs_0_, s32[1]{0:T(128)S(6)} %copy.15.refs_1_.which, ...), custom_call_target="tpu_custom_call", output_to_operand_aliasing={{0}: (13, {})} | custom-call | flops 9830400 | bytes 5505024 | tf_op jit(solution)/shard_map/cross/pallas_call | solution.py:209
  48.5 3.4 %collective-permute-start.15 = (f32[24,32,256]{2,1,0:T(8,128)S(1)}, f32[24,32,256]{2,1,0:T(8,128)S(1)}, u32[]{:S(2)}, u32[]{:S(2)}) collective-permute-start(f32[24,32,256]{2,1,0:T(8,128)S(1)} %get-tuple-element.69), channel_id=1, source_target_pairs={{0,16},{16,0},{32,48},{48,32},{64,80},{80,64},{96,112},{112,96},{1... | collective-permute-start | bytes 2359304 | tf_op jit(solution)/shard_map/ppermute | solution.py:309
  51.9 1.3 %collective-permute-start.11 = (f32[10,32,256]{2,1,0:T(8,128)S(1)}, f32[10,32,256]{2,1,0:T(8,128)S(1)}, u32[]{:S(2)}, u32[]{:S(2)}) collective-permute-start(f32[10,32,256]{2,1,0:T(8,128)S(1)} %get-tuple-element.66), channel_id=1, source_target_pairs={{0,32},{16,48},{32,64},{48,80},{64,96},{80,112},{96,0},{112,16},{1... | collective-permute-start | bytes 983048 | tf_op jit(solution)/shard_map/ppermute | solution.py:309
  53.2 1.4 %collective-permute-start.9 = (f32[10,32,256]{2,1,0:T(8,128)S(1)}, f32[10,32,256]{2,1,0:T(8,128)S(1)}, u32[]{:S(2)}, u32[]{:S(2)}) collective-permute-start(f32[10,32,256]{2,1,0:T(8,128)S(1)} %get-tuple-element.63), channel_id=1, source_target_pairs={{0,96},{16,112},{32,0},{48,16},{64,32},{80,48},{96,64},{112,80},{1... | collective-permute-start | bytes 983048 | tf_op jit(solution)/shard_map/ppermute | solution.py:309
  54.6 15.6 %near.1 = (f32[128,32,256]{2,1,0:T(8,128)S(1)}, f32[128,256]{1,0:T(8,128)S(1)}, f32[128,256]{1,0:T(8,128)S(1)}, f32[32,128]{1,0:T(8,128)S(1)}, f32[32,128]{1,0:T...) custom-call(s32[16]{0:T(128)S(1)} %stack.67.refs_0_, ...), custom_call_target="tpu_custom_call", output_to_operand_aliasing={{0}: (13, {})} | custom-call | flops 24576000 | bytes 13762560 | tf_op jit(solution)/shard_map/near/pallas_call | solution.py:209
  70.2 1.5 %collective-permute-start.13 = (f32[10,32,256]{2,1,0:T(8,128)S(1)}, f32[10,32,256]{2,1,0:T(8,128)S(1)}, u32[]{:S(2)}, u32[]{:S(2)}) collective-permute-start(f32[10,32,256]{2,1,0:T(8,128)S(1)} %get-tuple-element.67), channel_id=1, source_target_pairs={{0,96},{16,112},{32,0},{48,16},{64,32},{80,48},{96,64},{112,80},{1... | collective-permute-start | bytes 983048 | tf_op jit(solution)/shard_map/ppermute | solution.py:309
  71.8 0.0 collective-permute-done.11
  71.8 0.1 collective-permute-start.12
  71.9 0.0 copy-done.2
  71.9 7.0 %kept.1 = (f32[128,32,256]{2,1,0:T(8,128)S(1)}, f32[128,256]{1,0:T(8,128)S(1)}, f32[128,256]{1,0:T(8,128)S(1)}, f32[32,128]{1,0:T(8,128)S(1)}, f32[32,128]{1,0:T(8,128)S(1)}, /*index=5*/f32[24,32,256]{2,1,0:T(8,128)S(1)}) custom-call(s32[16]{0:T(128)S(1)} %stack.67.refs_0_, s32[1]{0:T(128)S(6)} %copy.15.refs_1_.which, ...), custom_call_target="tpu_custom_call", output_to_operand_aliasing={{0}: (13, {})} | custom-call | flops 9830400 | bytes 5505024 | tf_op jit(solution)/shard_map/kept/pallas_call | solution.py:209
  78.9 0.0 copy-start.5
  78.9 3.4 %collective-permute-start.6 = (f32[32,128]{1,0:T(8,128)S(1)}, f32[32,128]{1,0:T(8,128)S(1)}, u32[]{:S(2)}, u32[]{:S(2)}) collective-permute-start(f32[32,128]{1,0:T(8,128)S(1)} %get-tuple-element.58), channel_id=1, source_target_pairs={{0,1},{1,2},{2,3},{4,5},{5,6},{6,7},{8,9},{9,10},{10,11},{12,13},{... | collective-permute-start | bytes 49160 | tf_op jit(solution)/shard_map/ppermute | solution.py:287
  82.3 0.0 collective-permute-done.9
  82.3 1.3 %collective-permute-start.7 = (f32[32,128]{1,0:T(8,128)S(1)}, f32[32,128]{1,0:T(8,128)S(1)}, u32[]{:S(2)}, u32[]{:S(2)}) collective-permute-start(f32[32,128]{1,0:T(8,128)S(1)} %get-tuple-element.59), channel_id=1, source_target_pairs={{1,0},{2,1},{3,2},{5,4},{6,5},{7,6},{9,8},{10,9},{11,10},{13,12},{... | collective-permute-start | bytes 49160 | tf_op jit(solution)/shard_map/ppermute | solution.py:287
  83.6 0.1 add.194
  83.7 0.0 collective-permute-done.15
  83.7 6.0 %collective-permute-start.4 = (f32[128,256]{1,0:T(8,128)S(1)}, f32[128,256]{1,0:T(8,128)S(1)}, u32[]{:S(2)}, u32[]{:S(2)}) collective-permute-start(f32[128,256]{1,0:T(8,128)S(1)} %get-tuple-element.56), channel_id=1, source_target_pairs={{0,4},{4,8},{8,12},{1,5},{5,9},{9,13},{2,6},{6,10},{10,14},{3,7},{... | collective-permute-start | bytes 393224 | tf_op jit(solution)/shard_map/ppermute | solution.py:287
  89.8 0.1 add.200
  89.9 0.0 collective-permute-done.6.m_zl
  90.0 1.9 %collective-permute-start.5 = (f32[128,256]{1,0:T(8,128)S(1)}, f32[128,256]{1,0:T(8,128)S(1)}, u32[]{:S(2)}, u32[]{:S(2)}) collective-permute-start(f32[128,256]{1,0:T(8,128)S(1)} %get-tuple-element.57), channel_id=1, source_target_pairs={{4,0},{8,4},{12,8},{5,1},{9,5},{13,9},{6,2},{10,6},{14,10},{7,3},{... | collective-permute-start | bytes 393224 | tf_op jit(solution)/shard_map/ppermute | solution.py:287
  91.9 0.0 collective-permute-done.7.m_zh
  91.9 0.2 collective-permute-start.16
  92.1 0.0 collective-permute-done.13
  92.1 2.7 %collective-permute-start.18 = (f32[6,32,256]{2,1,0:T(8,128)S(1)}, f32[6,32,256]{2,1,0:T(8,128)S(1)}, u32[]{:S(2)}, u32[]{:S(2)}) collective-permute-start(f32[6,32,256]{2,1,0:T(8,128)S(1)} %get-tuple-element.71), channel_id=1, source_target_pairs={{0,96},{16,112},{32,0},{48,16},{64,32},{80,48},{96,64},{112,80},{1... | collective-permute-start | bytes 589832 | tf_op jit(solution)/shard_map/ppermute | solution.py:309
  94.8 0.0 collective-permute-done.12
  94.8 1.2 collective-permute-start.17
  96.0 0.1 add_add_fusion
  96.0 0.0 collective-permute-done.4.m_yl
  96.1 0.8 collective-permute-start.8
  96.9 0.0 collective-permute-done.5.m_yh
  96.9 2.4 %collective-permute-start.10 = (f32[10,32,256]{2,1,0:T(8,128)S(1)}, f32[10,32,256]{2,1,0:T(8,128)S(1)}, u32[]{:S(2)}, u32[]{:S(2)}) collective-permute-start(f32[10,32,256]{2,1,0:T(8,128)S(1)} %add.194), channel_id=1, source_target_pairs={{0,96},{16,112},{32,0},{48,16},{64,32},{80,48},{96,64},{112,80},{1... | collective-permute-start | bytes 983048 | tf_op jit(solution)/shard_map/ppermute | solution.py:309
  99.3 1.5 %collective-permute-done.16 = f32[6,32,256]{2,1,0:T(8,128)S(1)} collective-permute-done((f32[6,32,256]{2,1,0:T(8,128)S(1)}, f32[6,32,256]{2,1,0:T(8,128)S(1)}, u32[]{:S(2)}, u32[]{:S(2)}) %collective-permute-start.16) | collective-permute-done | bytes 196640 | tf_op jit(solution)/shard_map/ppermute | solution.py:309
  100.7 2.9 %collective-permute-start.14 = (f32[10,32,256]{2,1,0:T(8,128)S(1)}, f32[10,32,256]{2,1,0:T(8,128)S(1)}, u32[]{:S(2)}, u32[]{:S(2)}) collective-permute-start(f32[10,32,256]{2,1,0:T(8,128)S(1)} %add_add_fusion), channel_id=1, source_target_pairs={{0,16},{16,0},{32,48},{48,32},{64,80},{80,64},{96,112},{112,96},{1... | collective-permute-start | bytes 983048 | tf_op jit(solution)/shard_map/ppermute | solution.py:309
  103.6 0.0 copy-done.5
  103.6 21.4 %last_step.1 = f32[128,32,256]{2,1,0:T(8,128)} custom-call(s32[1]{0:T(128)S(6)} %copy.15.refs_1_.which, f32[8]{0:T(128)S(1)} %copy-done.6, f32[128,32,256]{2,1,0:T(8,128)S(1)} %get-tuple-element.55.adj, s32[128,32,256]{2,1,0:T(8,128)S(1)} %copy-done.2, f32[128,32,256]{2,1,0:T(8,128)S(1)} %copy-done.5, bf16[256,32,256]{2,1,0:T(8,128)(2,1)} %bitcast.33, ...), custom_call_target="tpu_custom_call" | custom-call | flops 41943040 | bytes 20971520 | tf_op jit(solution)/shard_map/last_step/pallas_call | solution.py:265
  125.0 0.0 collective-permute-done.18
  125.0 0.0 collective-permute-done.17
  125.0 0.1 fusion.1
  125.0 0.0 collective-permute-done.8
  125.1 0.0 collective-permute-done.10
  125.1 0.0 collective-permute-done.14
  125.1 0.1 add_add_fusion.1
  125.2 0.8 pad_maximum_fusion
  (3 shorter events, 0.1 us)
Async XLA Ops:
  0.6 2.2 %copy-start = (s32[128,32,256]{2,1,0:T(8,128)S(1)}, s32[128,32,256]{2,1,0:T(8,128)}, u32[]{:S(2)}) copy-start(s32[128,32,256]{2,1,0:T(8,128)} %pore.1) | copy-start | bytes 12582916
  2.8 2.2 %copy-start.3 = (f32[1,128,32,256]{3,2,1,0:T(8,128)S(1)}, f32[1,128,32,256]{3,2,1,0:T(8,128)}, u32[]{:S(2)}) copy-start(f32[1,128,32,256]{3,2,1,0:T(8,128)} %param.7) | copy-start | bytes 12582916
  5.0 26.0 %copy-start.6 = (f32[8]{0:T(128)S(1)}, f32[8]{0:T(128)}, u32[]{:S(2)}) copy-start(f32[8]{0:T(128)} %affinities.1) | copy-start | bytes 100
  16.3 14.7 %collective-permute-start = (f32[2,128,256]{2,1,0:T(8,128)S(1)}, f32[2,128,256]{2,1,0:T(8,128)S(1)}, u32[]{:S(2)}, u32[]{:S(2)}) collective-permute-start(f32[2,128,256]{2,1,0:T(8,128)S(1)} %get-tuple-element.36), channel_id=1, source_target_pairs={{0,4},{4,8},{8,12},{1,5},{5,9},{9,13},{2,6},{6,10},{10,14},{3,7},{... | collective-permute-start | bytes 786440 | tf_op jit(solution)/shard_map/ppermute | solution.py:287
  21.3 9.7 %collective-permute-start.1 = (f32[2,128,256]{2,1,0:T(8,128)S(1)}, f32[2,128,256]{2,1,0:T(8,128)S(1)}, u32[]{:S(2)}, u32[]{:S(2)}) collective-permute-start(f32[2,128,256]{2,1,0:T(8,128)S(1)} %get-tuple-element.37), channel_id=1, source_target_pairs={{4,0},{8,4},{12,8},{5,1},{9,5},{13,9},{6,2},{10,6},{14,10},{7,3},{... | collective-permute-start | bytes 786440 | tf_op jit(solution)/shard_map/ppermute | solution.py:287
  23.2 5.3 %collective-permute-start.2 = (f32[64,128]{1,0:T(8,128)S(1)}, f32[64,128]{1,0:T(8,128)S(1)}, u32[]{:S(2)}, u32[]{:S(2)}) collective-permute-start(f32[64,128]{1,0:T(8,128)S(1)} %get-tuple-element.38), channel_id=1, source_target_pairs={{0,1},{1,2},{2,3},{4,5},{5,6},{6,7},{8,9},{9,10},{10,11},{12,13},{... | collective-permute-start | bytes 98312 | tf_op jit(solution)/shard_map/ppermute | solution.py:287
  26.3 4.7 %collective-permute-start.3 = (f32[64,128]{1,0:T(8,128)S(1)}, f32[64,128]{1,0:T(8,128)S(1)}, u32[]{:S(2)}, u32[]{:S(2)}) collective-permute-start(f32[64,128]{1,0:T(8,128)S(1)} %get-tuple-element.39), channel_id=1, source_target_pairs={{1,0},{2,1},{3,2},{5,4},{6,5},{7,6},{9,8},{10,9},{11,10},{13,12},{... | collective-permute-start | bytes 98312 | tf_op jit(solution)/shard_map/ppermute | solution.py:287
  31.0 2.2 %copy-start.1 = (s32[128,32,256]{2,1,0:T(8,128)S(1)}, s32[128,32,256]{2,1,0:T(8,128)}, u32[]{:S(2)}) copy-start(s32[128,32,256]{2,1,0:T(8,128)} %pore.1) | copy-start | bytes 12582916
  33.2 2.2 %copy-start.4 = (f32[1,128,32,256]{3,2,1,0:T(8,128)S(1)}, f32[1,128,32,256]{3,2,1,0:T(8,128)}, u32[]{:S(2)}) copy-start(f32[1,128,32,256]{3,2,1,0:T(8,128)} %param.7) | copy-start | bytes 12582916
  48.5 35.2 %collective-permute-start.15 = (f32[24,32,256]{2,1,0:T(8,128)S(1)}, f32[24,32,256]{2,1,0:T(8,128)S(1)}, u32[]{:S(2)}, u32[]{:S(2)}) collective-permute-start(f32[24,32,256]{2,1,0:T(8,128)S(1)} %get-tuple-element.69), channel_id=1, source_target_pairs={{0,16},{16,0},{32,48},{48,32},{64,80},{80,64},{96,112},{112,96},{1... | collective-permute-start | bytes 2359304 | tf_op jit(solution)/shard_map/ppermute | solution.py:309
  51.9 19.9 %collective-permute-start.11 = (f32[10,32,256]{2,1,0:T(8,128)S(1)}, f32[10,32,256]{2,1,0:T(8,128)S(1)}, u32[]{:S(2)}, u32[]{:S(2)}) collective-permute-start(f32[10,32,256]{2,1,0:T(8,128)S(1)} %get-tuple-element.66), channel_id=1, source_target_pairs={{0,32},{16,48},{32,64},{48,80},{64,96},{80,112},{96,0},{112,16},{1... | collective-permute-start | bytes 983048 | tf_op jit(solution)/shard_map/ppermute | solution.py:309
  53.2 29.2 %collective-permute-start.9 = (f32[10,32,256]{2,1,0:T(8,128)S(1)}, f32[10,32,256]{2,1,0:T(8,128)S(1)}, u32[]{:S(2)}, u32[]{:S(2)}) collective-permute-start(f32[10,32,256]{2,1,0:T(8,128)S(1)} %get-tuple-element.63), channel_id=1, source_target_pairs={{0,96},{16,112},{32,0},{48,16},{64,32},{80,48},{96,64},{112,80},{1... | collective-permute-start | bytes 983048 | tf_op jit(solution)/shard_map/ppermute | solution.py:309
  54.6 17.3 %copy-start.2 = (s32[128,32,256]{2,1,0:T(8,128)S(1)}, s32[128,32,256]{2,1,0:T(8,128)}, u32[]{:S(2)}) copy-start(s32[128,32,256]{2,1,0:T(8,128)} %pore.1) | copy-start | bytes 12582916
  70.2 21.8 %collective-permute-start.13 = (f32[10,32,256]{2,1,0:T(8,128)S(1)}, f32[10,32,256]{2,1,0:T(8,128)S(1)}, u32[]{:S(2)}, u32[]{:S(2)}) collective-permute-start(f32[10,32,256]{2,1,0:T(8,128)S(1)} %get-tuple-element.67), channel_id=1, source_target_pairs={{0,96},{16,112},{32,0},{48,16},{64,32},{80,48},{96,64},{112,80},{1... | collective-permute-start | bytes 983048 | tf_op jit(solution)/shard_map/ppermute | solution.py:309
  71.8 23.0 %collective-permute-start.12 = (f32[10,32,256]{2,1,0:T(8,128)S(1)}, f32[10,32,256]{2,1,0:T(8,128)S(1)}, u32[]{:S(2)}, u32[]{:S(2)}) collective-permute-start(f32[10,32,256]{2,1,0:T(8,128)S(1)} %add.196), channel_id=1, source_target_pairs={{0,32},{16,48},{32,64},{48,80},{64,96},{80,112},{96,0},{112,16},{1... | collective-permute-start | bytes 983048 | tf_op jit(solution)/shard_map/ppermute | solution.py:309
  78.9 24.7 %copy-start.5 = (f32[128,32,256]{2,1,0:T(8,128)S(1)}, f32[128,32,256]{2,1,0:T(8,128)}, u32[]{:S(2)}) copy-start(f32[128,32,256]{2,1,0:T(8,128)} %cap.1) | copy-start | bytes 12582916
  78.9 11.0 %collective-permute-start.6 = (f32[32,128]{1,0:T(8,128)S(1)}, f32[32,128]{1,0:T(8,128)S(1)}, u32[]{:S(2)}, u32[]{:S(2)}) collective-permute-start(f32[32,128]{1,0:T(8,128)S(1)} %get-tuple-element.58), channel_id=1, source_target_pairs={{0,1},{1,2},{2,3},{4,5},{5,6},{6,7},{8,9},{9,10},{10,11},{12,13},{... | collective-permute-start | bytes 49160 | tf_op jit(solution)/shard_map/ppermute | solution.py:287
  82.3 9.6 %collective-permute-start.7 = (f32[32,128]{1,0:T(8,128)S(1)}, f32[32,128]{1,0:T(8,128)S(1)}, u32[]{:S(2)}, u32[]{:S(2)}) collective-permute-start(f32[32,128]{1,0:T(8,128)S(1)} %get-tuple-element.59), channel_id=1, source_target_pairs={{1,0},{2,1},{3,2},{5,4},{6,5},{7,6},{9,8},{10,9},{11,10},{13,12},{... | collective-permute-start | bytes 49160 | tf_op jit(solution)/shard_map/ppermute | solution.py:287
  83.7 12.3 %collective-permute-start.4 = (f32[128,256]{1,0:T(8,128)S(1)}, f32[128,256]{1,0:T(8,128)S(1)}, u32[]{:S(2)}, u32[]{:S(2)}) collective-permute-start(f32[128,256]{1,0:T(8,128)S(1)} %get-tuple-element.56), channel_id=1, source_target_pairs={{0,4},{4,8},{8,12},{1,5},{5,9},{9,13},{2,6},{6,10},{10,14},{3,7},{... | collective-permute-start | bytes 393224 | tf_op jit(solution)/shard_map/ppermute | solution.py:287
  90.0 6.9 %collective-permute-start.5 = (f32[128,256]{1,0:T(8,128)S(1)}, f32[128,256]{1,0:T(8,128)S(1)}, u32[]{:S(2)}, u32[]{:S(2)}) collective-permute-start(f32[128,256]{1,0:T(8,128)S(1)} %get-tuple-element.57), channel_id=1, source_target_pairs={{4,0},{8,4},{12,8},{5,1},{9,5},{13,9},{6,2},{10,6},{14,10},{7,3},{... | collective-permute-start | bytes 393224 | tf_op jit(solution)/shard_map/ppermute | solution.py:287
  91.9 8.8 %collective-permute-start.16 = (f32[6,32,256]{2,1,0:T(8,128)S(1)}, f32[6,32,256]{2,1,0:T(8,128)S(1)}, u32[]{:S(2)}, u32[]{:S(2)}) collective-permute-start(f32[6,32,256]{2,1,0:T(8,128)S(1)} %get-tuple-element.70), channel_id=1, source_target_pairs={{0,32},{16,48},{32,64},{48,80},{64,96},{80,112},{96,0},{112,16},{1... | collective-permute-start | bytes 589832 | tf_op jit(solution)/shard_map/ppermute | solution.py:309
  92.1 32.9 %collective-permute-start.18 = (f32[6,32,256]{2,1,0:T(8,128)S(1)}, f32[6,32,256]{2,1,0:T(8,128)S(1)}, u32[]{:S(2)}, u32[]{:S(2)}) collective-permute-start(f32[6,32,256]{2,1,0:T(8,128)S(1)} %get-tuple-element.71), channel_id=1, source_target_pairs={{0,96},{16,112},{32,0},{48,16},{64,32},{80,48},{96,64},{112,80},{1... | collective-permute-start | bytes 589832 | tf_op jit(solution)/shard_map/ppermute | solution.py:309
  94.8 30.2 %collective-permute-start.17 = (f32[6,32,256]{2,1,0:T(8,128)S(1)}, f32[6,32,256]{2,1,0:T(8,128)S(1)}, u32[]{:S(2)}, u32[]{:S(2)}) collective-permute-start(f32[6,32,256]{2,1,0:T(8,128)S(1)} %get-tuple-element.72), channel_id=1, source_target_pairs={{0,64},{16,80},{32,96},{48,112},{64,0},{80,16},{96,32},{112,48},{1... | collective-permute-start | bytes 589832 | tf_op jit(solution)/shard_map/ppermute | solution.py:309
  96.1 29.0 %collective-permute-start.8 = (f32[10,32,256]{2,1,0:T(8,128)S(1)}, f32[10,32,256]{2,1,0:T(8,128)S(1)}, u32[]{:S(2)}, u32[]{:S(2)}) collective-permute-start(f32[10,32,256]{2,1,0:T(8,128)S(1)} %get-tuple-element.61), channel_id=1, source_target_pairs={{0,32},{16,48},{32,64},{48,80},{64,96},{80,112},{96,0},{112,16},{1... | collective-permute-start | bytes 983048 | tf_op jit(solution)/shard_map/ppermute | solution.py:309
  96.9 28.2 %collective-permute-start.10 = (f32[10,32,256]{2,1,0:T(8,128)S(1)}, f32[10,32,256]{2,1,0:T(8,128)S(1)}, u32[]{:S(2)}, u32[]{:S(2)}) collective-permute-start(f32[10,32,256]{2,1,0:T(8,128)S(1)} %add.194), channel_id=1, source_target_pairs={{0,96},{16,112},{32,0},{48,16},{64,32},{80,48},{96,64},{112,80},{1... | collective-permute-start | bytes 983048 | tf_op jit(solution)/shard_map/ppermute | solution.py:309
  100.7 24.3 %collective-permute-start.14 = (f32[10,32,256]{2,1,0:T(8,128)S(1)}, f32[10,32,256]{2,1,0:T(8,128)S(1)}, u32[]{:S(2)}, u32[]{:S(2)}) collective-permute-start(f32[10,32,256]{2,1,0:T(8,128)S(1)} %add_add_fusion), channel_id=1, source_target_pairs={{0,16},{16,0},{32,48},{48,32},{64,80},{80,64},{96,112},{112,96},{1... | collective-permute-start | bytes 983048 | tf_op jit(solution)/shard_map/ppermute | solution.py:309

commit v2 on v0

v2 whole, which is shorter than its diff:
```python
import functools

import jax
import jax.numpy as jnp
from jax import lax
from jax.experimental import pallas as pl
from jax.experimental.pallas import tpu as pltpu
from jax.sharding import PartitionSpec as P

F32 = jnp.float32
SOLID = float("inf")
VMEM_LIMIT = 16 * 1024 * 1024
LANES = 128
ROWS = 8
VMEM = pl.BlockSpec(memory_space=pltpu.VMEM)
SMEM = pl.BlockSpec(memory_space=pltpu.SMEM)
HBM = pl.BlockSpec(memory_space=pltpu.HBM)


def reciprocal(value):
    guess = pl.reciprocal(value, approx=True)
    return guess * (2.0 - value * guess)


def lane_to(values, source, target):
    shift = target - source
    if isinstance(shift, int):
        return pltpu.roll(values, shift % LANES, 1)
    return pltpu.roll(values, lax.rem(shift + LANES, LANES), 1)


def in_hbm(*arrays):
    return [pltpu.with_memory_space_constraint(a, pltpu.HBM) for a in arrays]


def in_vmem(*arrays):
    return [pltpu.with_memory_space_constraint(a, pltpu.VMEM) for a in arrays]


def over(planes, unroll, body, carry=()):
    def some(k, carry):
        for u in range(unroll):
            carry = body(k * unroll + u, carry)
        return carry

    return lax.fori_loop(0, planes // unroll, some, carry)


def run(h):
    return slice(h * LANES, (h + 1) * LANES)


def padded_shape(nx, ny, nz):
    return (nz // LANES, nx + 2, ny + 2 * ROWS, LANES)


def halo_rows(wide, x, low, high):
    ny = wide.shape[2] - 2 * ROWS
    for h in range(wide.shape[0]):
        wide[h, x + 1, ROWS - 1 : ROWS, :] = low[:, run(h)]
        wide[h, x + 1, ROWS + ny : ROWS + ny + 1, :] = high[:, run(h)]


def weighted(wide, at, lane, z_low, z_high):
    count, _, rows, _ = wide.shape
    ny = rows - 2 * ROWS
    inner = slice(ROWS, ROWS + ny)
    centre = [wide[h, at, inner, :] for h in range(count)]
    ups = [pltpu.roll(c, 1, 1) for c in centre]
    downs = [pltpu.roll(c, LANES - 1, 1) for c in centre]
    sums = []
    for h in range(count):
        total = wide[h, at, ROWS - 1 : ROWS - 1 + ny, :] + wide[h, at, ROWS + 1 : ROWS + 1 + ny, :]
        total = total + (wide[h, at - 1, inner, :] + 3.0 * wide[h, at + 1, inner, :])
        left = jnp.where(lane == 0, ups[h - 1] if h else z_low, ups[h])
        right = jnp.where(lane == LANES - 1, downs[h + 1] if h + 1 < count else z_high, downs[h])
        sums.append(total + (left + right))
    return centre, sums


def rotating(steps, copies, body):
    for copy in copies(0, 0):
        copy.start()
    for t in range(steps):
        slot = t % 2
        if t + 1 < steps:
            for copy in copies(t + 1, 1 - slot):
                copy.start()
        for copy in copies(t, slot):
            copy.wait()
        body(t, slot)


def prepare_kernel(planes, unroll, adj_hbm, pore_hbm, masked, kept, y_low, y_high, z_low, z_high, adj, pore, wide, sem):
    nx, ny, nz = adj_hbm.shape
    count = nz // LANES
    lane = lax.broadcasted_iota(jnp.int32, (ny, LANES), 1)
    steps = nx // planes

    for h in range(count):
        for x in (0, nx + 1):
            masked[h, x] = jnp.zeros_like(masked[h, x])
            wide[h, x] = jnp.zeros_like(wide[h, x])

    def clear(x, carry):
        for h in range(count):
            wide[h, x + 1, :ROWS, :] = jnp.zeros((ROWS, LANES), F32)
            wide[h, x + 1, ROWS + ny :, :] = jnp.zeros((ROWS, LANES), F32)
        return carry

    def copies(t, slot):
        at = pl.ds(t * planes, planes)
        return [
            pltpu.make_async_copy(adj_hbm.at[at], adj.at[slot], sem.at[slot, 0]),
            pltpu.make_async_copy(pore_hbm.at[at], pore.at[slot], sem.at[slot, 1]),
        ]

    def body(t, slot):
        def load(i, carry):
            x = t * planes + i
            here = lane == x
            out = list(carry)
            clear(x, ())
            pores = pore[slot, i].astype(F32)
            for part, value in enumerate((adj[slot, i] * pores, pores)):
                halves = [value[:, run(h)] for h in range(count)]
                for h in range(count):
                    (wide if part else masked)[h, x + 1, ROWS : ROWS + ny, :] = halves[h]
                y_low[part, pl.ds(x, 1), :] = value[:1]
                y_high[part, pl.ds(x, 1), :] = value[ny - 1 :]
                out[part] = jnp.where(here, lane_to(halves[0], 0, x), out[part])
                out[2 + part] = jnp.where(here, lane_to(halves[-1], LANES - 1, x), out[2 + part])
            return tuple(out)

        parts = (z_low[:ny], z_low[ny:], z_high[:ny], z_high[ny:])
        z_low[:ny], z_low[ny:], z_high[:ny], z_high[ny:] = over(planes, unroll, load, parts)

        def weigh(i, carry):
            x = t * planes + i - 1 if t else i
            zero = jnp.zeros((ny, LANES), F32)
            pores, sums = weighted(wide, x + 1, lane, zero, zero)
            outer = jnp.where(x == nx - 1, 0.8, 1.0)
            for h in range(count):
                kept[h, x] = jnp.where(pores[h] > 0.0, outer - 0.1 * sums[h], SOLID)
            return carry

        over(planes if t else planes - 1, unroll if t else 1, weigh)
        if t == steps - 1:
            weigh(planes, ())

    rotating(steps, copies, body)


def prepare(adjoint, pores, planes=16, unroll=4):
    nx, ny, nz = adjoint.shape
    y_shape = jax.ShapeDtypeStruct((2, nx, nz), F32)
    z_shape = jax.ShapeDtypeStruct((2 * ny, nx), F32)
    wide = padded_shape(nx, ny, nz)
    return pl.pallas_call(
        functools.partial(prepare_kernel, planes, unroll),
        in_specs=[HBM, HBM],
        out_specs=[VMEM] * 6,
        out_shape=[
            pltpu.VMEM(wide, F32),
            pltpu.VMEM((nz // LANES, nx, ny, LANES), F32),
            y_shape,
            y_shape,
            z_shape,
            z_shape,
        ],
        scratch_shapes=[
            pltpu.VMEM((2, planes, ny, nz), F32),
            pltpu.VMEM((2, planes, ny, nz), jnp.int32),
            pltpu.VMEM(wide, F32),
            pltpu.SemaphoreType.DMA((2, 2)),
        ],
        compiler_params=pltpu.CompilerParams(vmem_limit_bytes=VMEM_LIMIT),
        cost_estimate=pl.CostEstimate(flops=14 * nx * ny * nz, bytes_accessed=8 * nx * ny * nz, transcendentals=0),
        name="prepare",
    )(*in_hbm(adjoint, pores))


def stage_kernel(places, counts, planes, unroll, fresh, *refs):
    which, affinities, cap_hbm, filled_hbm, seen_hbm, y_low, y_high, z_low, z_high = refs[:9]
    refs = refs[9 + (2 if fresh else 7) :]
    (masked, kept, adj, out_y_low, out_y_high, out_z_low, out_z_high), refs = refs[:7], refs[7:]
    outs, (cap, late_f, early_f, late_o, sem) = refs[:-5], refs[-5:]
    count, nx, ny, _ = kept.shape
    lane = lax.broadcasted_iota(jnp.int32, (ny, LANES), 1)
    starts = places()
    inverse = 1.0 / jnp.full((1, LANES), affinities[which[0]], F32)

    if fresh:
        for h in range(count):
            for x in (0, nx + 1):
                adj[h, x] = jnp.zeros_like(adj[h, x])

    def copies(t, slot):
        start = starts[t]
        pairs = [
            (cap_hbm, start, cap),
            (filled_hbm, start + nx, late_f),
            (filled_hbm, start, early_f),
            (seen_hbm, start + nx, late_o),
        ]
        return [
            pltpu.make_async_copy(src.at[pl.ds(at, planes)], dst.at[slot], sem.at[slot, k])
            for k, (src, at, dst) in enumerate(pairs)
        ]

    targets = [(out, k) for out, n in zip(outs, counts) for k in range(n)]

    def body(t, slot):
        start = starts[t]
        grad, block = targets[t]
        m_low, p_low = z_low[:ny], 0.1 * z_low[ny:]
        m_high, p_high = z_high[:ny], 0.1 * z_high[ny:]

        def ends(i, carry):
            x = start + i
            row = pl.ds(x, 1)
            halo_rows(masked, x, y_low[0, row, :], y_high[0, row, :])
            low, high = 0.1 * y_low[1, row, :], 0.1 * y_high[1, row, :]
            for h in range(count):
                kept[h, x, :1, :] = kept[h, x, :1, :] - low[:, run(h)]
                kept[h, x, ny - 1 :, :] = kept[h, x, ny - 1 :, :] - high[:, run(h)]
            return carry

        over(planes, unroll, ends)

        def plane(i, carry):
            low, high = carry
            x = start + i
            m_c, m_sum = weighted(masked, x + 1, lane, lane_to(m_low, x, 0), lane_to(m_high, x, LANES - 1))
            values = []
            for h in range(count):
                filled = late_f[slot, i, :, run(h)].astype(F32)
                early = early_f[slot, i, :, run(h)].astype(F32)
                source = filled - late_o[slot, i, :, run(h)].astype(F32)
                late_r = reciprocal(-inverse - filled)
                early_r = reciprocal(-inverse - early)
                weight = kept[h, x]
                if h == 0:
                    weight = weight - jnp.where(lane == 0, lane_to(p_low, x, 0), 0.0)
                if h == count - 1:
                    weight = weight - jnp.where(lane == LANES - 1, lane_to(p_high, x, LANES - 1), 0.0)
                pore = weight != SOLID
                uptake = cap[slot, i, :, run(h)] * inverse
                updated = m_c[h] * (weight - uptake * (late_r * late_r)) + (0.1 * m_sum[h] + source)
                updated = jnp.where(pore, updated, 0.0)
                kept[h, x] = jnp.where(pore, weight - uptake * (early_r * early_r), SOLID)
                grad[block * planes + i, :, run(h)] = (filled * late_r) * m_c[h] + (early * early_r) * updated
                adj[h, x + 1, ROWS : ROWS + ny, :] = updated
                values.append(updated)
            out_y_low[pl.ds(x, 1), :] = jnp.concatenate([v[:1] for v in values], 1)
            out_y_high[pl.ds(x, 1), :] = jnp.concatenate([v[ny - 1 :] for v in values], 1)
            low = jnp.where(lane == x, lane_to(values[0], 0, x), low)
            high = jnp.where(lane == x, lane_to(values[-1], LANES - 1, x), high)
            return low, high

        out_z_low[...], out_z_high[...] = over(planes, unroll, plane, (out_z_low[...], out_z_high[...]))

    rotating(sum(counts), copies, body)


def stage(scalars, fields, halo, state, places, counts, planes, unroll, name):
    capacity, filled, seen = fields
    nx, ny, nz = capacity.shape
    runs = sum(counts)
    operands = [*scalars, *in_hbm(capacity, filled, seen), *halo, *in_vmem(*state)]
    base = len(operands) - len(state)
    shapes = [padded_shape(nx, ny, nz), (nz // LANES, nx, ny, LANES), padded_shape(nx, ny, nz), (nx, nz), (nx, nz), (ny, nx), (ny, nx)]
    shapes += [(n * planes, ny, nz) for n in counts]
    block = (2, planes, ny, nz)
    voxels = runs * planes * ny * nz
    results = pl.pallas_call(
        functools.partial(stage_kernel, places, counts, planes, unroll, len(state) == 2),
        in_specs=[SMEM] * 2 + [HBM] * 3 + [VMEM] * (4 + len(state)),
        out_specs=[VMEM] * len(shapes),
        out_shape=[pltpu.VMEM(s, F32) for s in shapes[:7]] + [jax.ShapeDtypeStruct(s, F32) for s in shapes[7:]],
        scratch_shapes=[
            pltpu.VMEM(block, F32),
            pltpu.VMEM(block, jnp.bfloat16),
            pltpu.VMEM(block, jnp.bfloat16),
            pltpu.VMEM(block, jnp.bfloat16),
            pltpu.SemaphoreType.DMA((2, 4)),
        ],
        input_output_aliases={base + k: k for k in range(len(state))},
        compiler_params=pltpu.CompilerParams(vmem_limit_bytes=VMEM_LIMIT),
        cost_estimate=pl.CostEstimate(flops=40 * voxels, bytes_accessed=10 * voxels, transcendentals=2 * voxels),
        name=name,
    )(*operands)
    return results[:7], results[7:]


def last_kernel(planes, unroll, f_hbm, o_hbm, kept, y_low, y_high, z_low, z_high, _, out_hbm, adj, filled, seen, out, sem, out_sem):
    count, nx, ny, _ = kept.shape
    lane = lax.broadcasted_iota(jnp.int32, (ny, LANES), 1)
    steps = nx // planes

    def copies(t, slot):
        at = pl.ds(t * planes, planes)
        return [
            pltpu.make_async_copy(f_hbm.at[at], filled.at[slot], sem.at[slot, 0]),
            pltpu.make_async_copy(o_hbm.at[at], seen.at[slot], sem.at[slot, 1]),
        ]

    def writing(t):
        return pltpu.make_async_copy(out.at[t % 2], out_hbm.at[pl.ds(t * planes, planes)], out_sem.at[t % 2])

    def body(t, slot):
        if t >= 2:
            writing(t - 2).wait()

        def ends(i, carry):
            x = t * planes + i
            row = pl.ds(x, 1)
            halo_rows(adj, x, y_low[row, :], y_high[row, :])
            return carry

        over(planes, unroll, ends)

        def plane(i, carry):
            x = t * planes + i
            centre, sums = weighted(adj, x + 1, lane, lane_to(z_low[...], x, 0), lane_to(z_high[...], x, LANES - 1))
            for h in range(count):
                weight = kept[h, x]
                source = filled[slot, i, :, run(h)].astype(F32) - seen[slot, i, :, run(h)].astype(F32)
                value = centre[h] * weight + (0.1 * sums[h] + source)
                out[slot, i, :, run(h)] = jnp.where(weight == SOLID, 0.0, value)
            return carry

        over(planes, unroll, plane)
        writing(t).start()

    rotating(steps, copies, body)
    writing(steps - 2).wait()
    writing(steps - 1).wait()


def last_step(adjoint, kept, filled, seen, halo, planes=16, unroll=4):
    count, nx, ny, lanes = kept.shape
    nz = count * lanes
    voxels = nx * ny * nz
    return pl.pallas_call(
        functools.partial(last_kernel, planes, unroll),
        in_specs=[HBM, HBM] + [VMEM] * 6,
        out_specs=[HBM, VMEM],
        out_shape=[jax.ShapeDtypeStruct((nx, ny, nz), F32), pltpu.VMEM(adjoint.shape, F32)],
        scratch_shapes=[
            pltpu.VMEM((2, planes, ny, nz), jnp.bfloat16),
            pltpu.VMEM((2, planes, ny, nz), jnp.bfloat16),
            pltpu.VMEM((2, planes, ny, nz), F32),
            pltpu.SemaphoreType.DMA((2, 2)),
            pltpu.SemaphoreType.DMA((2,)),
        ],
        input_output_aliases={7: 1},
        compiler_params=pltpu.CompilerParams(vmem_limit_bytes=VMEM_LIMIT),
        cost_estimate=pl.CostEstimate(flops=20 * voxels, bytes_accessed=8 * voxels, transcendentals=0),
        name="last_step",
    )(*in_hbm(filled, seen), *in_vmem(kept), *halo, *in_vmem(adjoint))[0]


def exchange(y_low, y_high, z_low, z_high):
    received = []
    for axis, low, high in (("gy", y_low, y_high), ("gz", z_low, z_high)):
        count = lax.axis_size(axis)
        up = [(i, i + 1) for i in range(count - 1)]
        down = [(i + 1, i) for i in range(count - 1)]
        received += [lax.ppermute(high, axis, up), lax.ppermute(low, axis, down)]
    return tuple(received)


def places(ring, pairs, share, order):
    rank = lax.axis_index("exp")
    row, half = rank // pairs, rank % pairs
    return [
        (((row + turn) % ring) * pairs + (half + swap) % pairs) * share + part * (share // 2)
        for turn, swap, part in order
    ]


def orders(ring):
    cross = [(turn, 1, 1) for turn in range(ring)]
    along = [(turn, swap, 0) for turn in (2, 1, 3) for swap in (1, 0)]
    own = [(0, 1, 0), (0, 0, 0)] + [(turn, 0, 1) for turn in range(ring)]
    return cross, along, own


def shards(ring, adjoint_final, concentration, observed, capacity, pore_mask, feed_index, feed_affinity):
    ranks = lax.axis_size("exp")
    pairs = ranks // ring
    adjoint = adjoint_final[0]
    nx, ny, nz = adjoint.shape
    share = nx // ranks
    planes = share // 2
    filled = concentration.reshape(-1, ny, nz)
    seen = observed.reshape(-1, ny, nz)

    def send(value, turn, swap):
        perm = [
            (r * pairs + h, ((r + turn) % ring) * pairs + (h + swap) % pairs) for r in range(ring) for h in range(pairs)
        ]
        return lax.ppermute(value, "exp", perm)

    scalars = (feed_index, feed_affinity)
    at = [functools.partial(places, ring, pairs, share, order) for order in orders(ring)]
    fields = (capacity, filled, seen)

    *state, y_low, y_high, z_low, z_high = prepare(adjoint, pore_mask)
    halo = exchange(y_low, y_high, z_low, z_high)
    state, (cross,) = stage(scalars, fields, halo, state, at[0], (4,), planes, 2, "cross")
    crossed = send(cross, 0, 1)
    state, along = stage(scalars, fields, halo, state, at[1], (2, 2, 2), planes, 2, "along")
    parts_p = [send(value, turn, 0) for value, turn in zip(along, (2, 1, 3))]
    (_, kept, next_adjoint, *next_faces), (own_p, own_q) = stage(scalars, fields, halo, state, at[2], (2, 4), planes, 2, "own")
    face_halo = exchange(*next_faces)

    total_p = own_p + parts_p[0] + parts_p[1] + parts_p[2]
    last_p = send(total_p[:planes], 0, 1)
    total_q = (own_q + crossed).reshape(ring, planes, ny, nz)
    parts_q = [send(total_q[turn], turn, 0) for turn in (2, 1, 3)]

    adjoint_first = last_step(next_adjoint, kept, filled, seen, face_halo)

    sum_p = total_p[planes:] + last_p
    sum_q = total_q[0] + parts_q[0] + parts_q[1] + parts_q[2]
    return adjoint_first[None], jnp.concatenate([sum_p, sum_q], 0)


def solution(mesh):
    in_specs = (
        P("exp", None, "gy", "gz"),
        P(None, "exp", None, "gy", "gz"),
        P(None, "exp", None, "gy", "gz"),
        P(None, "gy", "gz"),
        P(None, "gy", "gz"),
        P("exp"),
        P(),
    )
    out_specs = (P("exp", None, "gy", "gz"), P("exp", "gy", "gz"))
    return jax.shard_map(
        functools.partial(shards, 4), mesh=mesh, in_specs=in_specs, out_specs=out_specs, check_vma=False
    )
```

time: 329 us -> 92.6 us (0.28)
  waiting for transfers between devices: 138 us -> 13 us
  local copies, waits for them, and re-layouts: 81.7 us -> 0.09 us
  other arithmetic: 56 us -> 1.25 us
  Pallas kernels: 0 us -> 42.6 us
  between operations: 15 us -> 1.5 us
    psum x1 -> x0, waiting for transfers between devices: 137 us -> none  [shards(): summed = lax.psum(gradient, 'exp')]
    unnamed x29 -> x2, local copies, waits for them, and re-layouts: 48.8 us -> 0.01 us
    pallas_call x0 -> x5, Pallas kernels: none -> 42.6 us  [the longest x3 21.5 us: stage(): pl.pallas_call(functools.partial(stage_kernel, places, counts, planes, un...]
    add x1 -> x4, other arithmetic: 32.2 us -> 0.42 us  [the longest x1 0.16 us: shards(): total_q = (own_q + crossed).reshape(ring, planes, ny, nz)]
    slice x13 -> x2, local copies, waits for them, and re-layouts: 27.1 us -> 0.09 us  [the longest x1 0.07 us: shards(): parts_q = [send(total_q[turn], turn, 0) for turn in (2, 1, 3)]]
    broadcast_in_dim x1 -> x0, other arithmetic: 18.8 us -> none  [shards(): return (adjoint[None], owned)]
    ppermute x12 -> x16, waiting for transfers between devices: 1.86 us -> 13 us  [the longest x8 9.53 us: send(): return lax.ppermute(value, 'exp', perm)]
    dynamic_slice x1 -> x0, local copies, waits for them, and re-layouts: 5.29 us -> none  [shards(): lax.dynamic_slice_in_dim(summed, lax.axis_index('exp') * share, share, 0)]
  transfers between devices with their start and end apart: 13 -> 16, of which waited for: 3 -> 4; matrix products, arithmetic and copies ran while one was open for 29% -> 0% of each run, Pallas kernels for 0% -> 28%
where the time goes in v2:
time: 92.6 us; the launch traced here: 91.7 us
  Pallas kernels  42.6 us (46%)
  starting transfers between devices  33.3 us (36%)
  waiting for transfers between devices  13 us (14%)
  between operations  1.5 us (2%)
  other arithmetic  1.25 us (1%)
    pallas_call x3, Pallas kernels, stage(): pl.pallas_call(functools.partial(stage_kernel, places, counts, planes, un...  21.5 us
    ppermute x8, starting transfers between devices, exchange(): received += [lax.ppermute(high, axis, up), lax.ppermute(low, axis, down)]  20 us
    ppermute x8, starting transfers between devices, send(): return lax.ppermute(value, 'exp', perm)  13.3 us
    pallas_call x1, Pallas kernels, prepare(): pl.pallas_call(functools.partial(prepare_kernel, planes, unroll), in_spec...  11.3 us
    pallas_call x1, Pallas kernels, last_step(): pl.pallas_call(functools.partial(last_kernel, planes, unroll), in_specs=[...  9.78 us
    ppermute x8, waiting for transfers between devices, send(): return lax.ppermute(value, 'exp', perm)  9.53 us
    ppermute x8, waiting for transfers between devices, exchange(): received += [lax.ppermute(high, axis, up), lax.ppermute(low, axis, down)]  3.51 us
  transfers between devices with their start and end apart: 16, of which 4 were waited for; matrix products, arithmetic and copies ran while one was open for 0% of the time, Pallas kernels for 28%

profile of v2, /device:TPU:1, one launch (start us, length us, event | category | flops | bytes accessed | tf_op | source)
XLA Modules:
  0.0 91.7 jit_solution(6570013098512852985)
XLA Ops:
  0.6 0.0 copy-start
  0.6 11.3 %prepare.1 = (f32[2,130,48,128]{3,2,1,0:T(8,128)S(1)}, f32[2,128,32,128]{3,2,1,0:T(8,128)S(1)}, f32[2,128,256]{2,1,0:T(8,128)S(1)}, f32[2,128,256]{2,1,0:T(8,128...) custom-call(f32[128,32,256]{2,1,0:T(8,128)} %bitcast.12, s32[128,32,256]{2,1,0:T(8,128)} %pore_hbm.1), custom_call_target="tpu_custom_call" | custom-call | flops 14680064 | bytes 8388608 | tf_op jit(solution)/shard_map/prepare/pallas_call | solution.py:159
  11.9 4.9 %collective-permute-start = (f32[2,128,256]{2,1,0:T(8,128)S(1)}, f32[2,128,256]{2,1,0:T(8,128)S(1)}, u32[]{:S(2)}, u32[]{:S(2)}) collective-permute-start(f32[2,128,256]{2,1,0:T(8,128)S(1)} %get-tuple-element.35), channel_id=1, source_target_pairs={{0,4},{4,8},{8,12},{1,5},{5,9},{9,13},{2,6},{6,10},{10,14},{3,7},{... | collective-permute-start | bytes 786440 | tf_op jit(solution)/shard_map/ppermute | solution.py:370
  16.8 1.9 %collective-permute-start.1 = (f32[2,128,256]{2,1,0:T(8,128)S(1)}, f32[2,128,256]{2,1,0:T(8,128)S(1)}, u32[]{:S(2)}, u32[]{:S(2)}) collective-permute-start(f32[2,128,256]{2,1,0:T(8,128)S(1)} %get-tuple-element.36), channel_id=1, source_target_pairs={{4,0},{8,4},{12,8},{5,1},{9,5},{13,9},{6,2},{10,6},{14,10},{7,3},{... | collective-permute-start | bytes 786440 | tf_op jit(solution)/shard_map/ppermute | solution.py:370
  18.8 3.1 %collective-permute-start.2 = (f32[64,128]{1,0:T(8,128)S(1)}, f32[64,128]{1,0:T(8,128)S(1)}, u32[]{:S(2)}, u32[]{:S(2)}) collective-permute-start(f32[64,128]{1,0:T(8,128)S(1)} %get-tuple-element.37), channel_id=1, source_target_pairs={{0,1},{1,2},{2,3},{4,5},{5,6},{6,7},{8,9},{9,10},{10,11},{12,13},{... | collective-permute-start | bytes 98312 | tf_op jit(solution)/shard_map/ppermute | solution.py:370
  21.9 1.3 %collective-permute-start.3 = (f32[64,128]{1,0:T(8,128)S(1)}, f32[64,128]{1,0:T(8,128)S(1)}, u32[]{:S(2)}, u32[]{:S(2)}) collective-permute-start(f32[64,128]{1,0:T(8,128)S(1)} %get-tuple-element.38), channel_id=1, source_target_pairs={{1,0},{2,1},{3,2},{5,4},{6,5},{7,6},{9,8},{10,9},{11,10},{13,12},{... | collective-permute-start | bytes 98312 | tf_op jit(solution)/shard_map/ppermute | solution.py:370
  23.8 0.0 collective-permute-done.2.refs_7_
  23.9 2.7 %collective-permute-done.3.refs_8_ = f32[64,128]{1,0:T(8,128)S(1)} collective-permute-done((f32[64,128]{1,0:T(8,128)S(1)}, f32[64,128]{1,0:T(8,128)S(1)}, u32[]{:S(2)}, u32[]{:S(2)}) %collective-permute-start.3) | collective-permute-done | bytes 32800 | tf_op jit(solution)/shard_map/ppermute | solution.py:370
  26.6 0.0 collective-permute-done.refs_5_
  26.6 0.0 collective-permute-done.1.refs_6_
  26.6 0.0 copy-done
  26.6 5.9 %cross.1 = (f32[2,130,48,128]{3,2,1,0:T(8,128)S(1)}, f32[2,128,32,128]{3,2,1,0:T(8,128)S(1)}, f32[2,130,48,128]{3,2,1,0:T(8,128)S(1)}, f32[128,256]{1,0:T(8,128)...) custom-call(s32[1]{0:T(128)S(6)} %copy.43.refs_0_, ...), custom_call_target="tpu_custom_call", output_to_operand_aliasing={{0}: (9, {}), {1}: (10, {})} | custom-call | flops 10485760 | bytes 2621440 | tf_op jit(solution)/shard_map/cross/pallas_call | solution.py:276
  32.4 3.4 %collective-permute-start.12 = (f32[32,32,256]{2,1,0:T(8,128)S(1)}, f32[32,32,256]{2,1,0:T(8,128)S(1)}, u32[]{:S(2)}, u32[]{:S(2)}) collective-permute-start(f32[32,32,256]{2,1,0:T(8,128)S(1)} %get-tuple-element.67), channel_id=1, source_target_pairs={{0,16},{16,0},{32,48},{48,32},{64,80},{80,64},{96,112},{112,96},{1... | collective-permute-start | bytes 3145736 | tf_op jit(solution)/shard_map/ppermute | solution.py:404
  35.8 7.8 %along.1 = (f32[2,130,48,128]{3,2,1,0:T(8,128)S(1)}, f32[2,128,32,128]{3,2,1,0:T(8,128)S(1)}, f32[2,130,48,128]{3,2,1,0:T(8,128)S(1)}, f32[128,256]{1,0:T(8,128)...) custom-call(s32[1]{0:T(128)S(6)} %copy.43.refs_0_, ...), custom_call_target="tpu_custom_call", output_to_operand_aliasing={{0}: (9, {}), {1}: (10, {}), {2}: (11, {}), {3}: (12, {}), ... | custom-call | flops 15728640 | bytes 3932160 | tf_op jit(solution)/shard_map/along/pallas_call | solution.py:276
  43.6 3.0 %collective-permute-start.8 = (f32[16,32,256]{2,1,0:T(8,128)S(1)}, f32[16,32,256]{2,1,0:T(8,128)S(1)}, u32[]{:S(2)}, u32[]{:S(2)}) collective-permute-start(f32[16,32,256]{2,1,0:T(8,128)S(1)} %get-tuple-element.63), channel_id=1, source_target_pairs={{0,64},{16,80},{32,96},{48,112},{64,0},{80,16},{96,32},{112,48},{1... | collective-permute-start | bytes 1572872 | tf_op jit(solution)/shard_map/ppermute | solution.py:404
  46.6 0.4 collective-permute-start.9
  47.0 2.3 %collective-permute-start.10 = (f32[16,32,256]{2,1,0:T(8,128)S(1)}, f32[16,32,256]{2,1,0:T(8,128)S(1)}, u32[]{:S(2)}, u32[]{:S(2)}) collective-permute-start(f32[16,32,256]{2,1,0:T(8,128)S(1)} %get-tuple-element.65), channel_id=1, source_target_pairs={{0,96},{16,112},{32,0},{48,16},{64,32},{80,48},{96,64},{112,80},{1... | collective-permute-start | bytes 1572872 | tf_op jit(solution)/shard_map/ppermute | solution.py:404
  49.3 7.9 %own.1 = (f32[2,130,48,128]{3,2,1,0:T(8,128)S(1)}, f32[2,128,32,128]{3,2,1,0:T(8,128)S(1)}, f32[2,130,48,128]{3,2,1,0:T(8,128)S(1)}, f32[128,256]{1,0:T(8,128)S(...) custom-call(s32[1]{0:T(128)S(6)} %copy.43.refs_0_, ...), custom_call_target="tpu_custom_call", output_to_operand_aliasing={{0}: (9, {}), {1}: (10, {}), {2}: (11, {}), {3}: (12, {}), ... | custom-call | flops 15728640 | bytes 3932160 | tf_op jit(solution)/shard_map/own/pallas_call | solution.py:276
  57.2 3.1 %collective-permute-start.6 = (f32[32,128]{1,0:T(8,128)S(1)}, f32[32,128]{1,0:T(8,128)S(1)}, u32[]{:S(2)}, u32[]{:S(2)}) collective-permute-start(f32[32,128]{1,0:T(8,128)S(1)} %get-tuple-element.58), channel_id=1, source_target_pairs={{0,1},{1,2},{2,3},{4,5},{5,6},{6,7},{8,9},{9,10},{10,11},{12,13},{... | collective-permute-start | bytes 49160 | tf_op jit(solution)/shard_map/ppermute | solution.py:370
  60.3 0.0 collective-permute-done.8
  60.3 1.3 %collective-permute-start.7 = (f32[32,128]{1,0:T(8,128)S(1)}, f32[32,128]{1,0:T(8,128)S(1)}, u32[]{:S(2)}, u32[]{:S(2)}) collective-permute-start(f32[32,128]{1,0:T(8,128)S(1)} %get-tuple-element.59), channel_id=1, source_target_pairs={{1,0},{2,1},{3,2},{5,4},{6,5},{7,6},{9,8},{10,9},{11,10},{13,12},{... | collective-permute-start | bytes 49160 | tf_op jit(solution)/shard_map/ppermute | solution.py:370
  61.6 8.8 %collective-permute-done.9 = f32[16,32,256]{2,1,0:T(8,128)S(1)} collective-permute-done((f32[16,32,256]{2,1,0:T(8,128)S(1)}, f32[16,32,256]{2,1,0:T(8,128)S(1)}, u32[]{:S(2)}, u32[]{:S(2)}) %collective-permute-start.9) | collective-permute-done | bytes 524320 | tf_op jit(solution)/shard_map/ppermute | solution.py:404
  70.4 1.9 %collective-permute-start.4 = (f32[128,256]{1,0:T(8,128)S(1)}, f32[128,256]{1,0:T(8,128)S(1)}, u32[]{:S(2)}, u32[]{:S(2)}) collective-permute-start(f32[128,256]{1,0:T(8,128)S(1)} %get-tuple-element.56), channel_id=1, source_target_pairs={{0,4},{4,8},{8,12},{1,5},{5,9},{9,13},{2,6},{6,10},{10,14},{3,7},{... | collective-permute-start | bytes 393224 | tf_op jit(solution)/shard_map/ppermute | solution.py:370
  72.3 0.0 collective-permute-done.10
  72.3 2.4 %collective-permute-start.5 = (f32[128,256]{1,0:T(8,128)S(1)}, f32[128,256]{1,0:T(8,128)S(1)}, u32[]{:S(2)}, u32[]{:S(2)}) collective-permute-start(f32[128,256]{1,0:T(8,128)S(1)} %get-tuple-element.57), channel_id=1, source_target_pairs={{4,0},{8,4},{12,8},{5,1},{9,5},{13,9},{6,2},{10,6},{14,10},{7,3},{... | collective-permute-start | bytes 393224 | tf_op jit(solution)/shard_map/ppermute | solution.py:370
  74.7 0.2 add_add_fusion
  74.9 0.0 collective-permute-done.12
  74.9 0.3 collective-permute-start.11
  75.2 0.2 add.28
  75.4 0.1 fusion.2
  75.4 0.0 collective-permute-done.6.z_low
  75.4 2.2 %collective-permute-start.13 = (f32[8,32,256]{2,1,0:T(8,128)S(1)}, f32[8,32,256]{2,1,0:T(8,128)S(1)}, u32[]{:S(2)}, u32[]{:S(2)}) collective-permute-start(f32[8,32,256]{2,1,0:T(8,128)S(1)} %get-tuple-element.68), channel_id=1, source_target_pairs={{0,64},{16,80},{32,96},{48,112},{64,0},{80,16},{96,32},{112,48},{1... | collective-permute-start | bytes 786440 | tf_op jit(solution)/shard_map/ppermute | solution.py:404
  77.7 0.0 collective-permute-done.7.z_high
  77.7 1.7 %collective-permute-start.15 = (f32[8,32,256]{2,1,0:T(8,128)S(1)}, f32[8,32,256]{2,1,0:T(8,128)S(1)}, u32[]{:S(2)}, u32[]{:S(2)}) collective-permute-start(f32[8,32,256]{2,1,0:T(8,128)S(1)} %get-tuple-element.69), channel_id=1, source_target_pairs={{0,96},{16,112},{32,0},{48,16},{64,32},{80,48},{96,64},{112,80},{1... | collective-permute-start | bytes 786440 | tf_op jit(solution)/shard_map/ppermute | solution.py:404
  79.4 0.0 collective-permute-done.4.y_low
  79.4 0.0 collective-permute-start.14
  79.4 0.8 collective-permute-done.5.y_high
  80.2 9.8 %last_step.1 = (f32[128,32,256]{2,1,0:T(8,128)}, f32[2,130,48,128]{3,2,1,0:T(8,128)S(1)}) custom-call(bf16[256,32,256]{2,1,0:T(8,128)(2,1)} %bitcast.7, bf16[256,32,256]{2,1,0:T(8,128)(2,1)} %bitcast.11, f32[2,128,32,128]{3,2,1,0:T(8,128)S(1)} %get-tuple-element.55.kept, ...), custom_call_target="tpu_custom_call", output_to_operand_aliasing={{1}: (7, {})} | custom-call | flops 20971520 | bytes 8388608 | tf_op jit(solution)/shard_map/last_step/pallas_call | solution.py:345
  90.0 0.0 collective-permute-done.11
  90.0 0.0 collective-permute-done.13
  90.0 0.0 collective-permute-done.15
  90.0 0.8 collective-permute-done.14
  90.8 0.1 fusion.1
  90.9 0.8 pad_maximum_fusion
  (2 shorter events, 0.1 us)
Async XLA Ops:
  0.6 25.9 %copy-start = (f32[8]{0:T(128)S(1)}, f32[8]{0:T(128)}, u32[]{:S(2)}) copy-start(f32[8]{0:T(128)} %refs_1_.5) | copy-start | bytes 100
  11.9 14.7 %collective-permute-start = (f32[2,128,256]{2,1,0:T(8,128)S(1)}, f32[2,128,256]{2,1,0:T(8,128)S(1)}, u32[]{:S(2)}, u32[]{:S(2)}) collective-permute-start(f32[2,128,256]{2,1,0:T(8,128)S(1)} %get-tuple-element.35), channel_id=1, source_target_pairs={{0,4},{4,8},{8,12},{1,5},{5,9},{9,13},{2,6},{6,10},{10,14},{3,7},{... | collective-permute-start | bytes 786440 | tf_op jit(solution)/shard_map/ppermute | solution.py:370
  16.8 9.7 %collective-permute-start.1 = (f32[2,128,256]{2,1,0:T(8,128)S(1)}, f32[2,128,256]{2,1,0:T(8,128)S(1)}, u32[]{:S(2)}, u32[]{:S(2)}) collective-permute-start(f32[2,128,256]{2,1,0:T(8,128)S(1)} %get-tuple-element.36), channel_id=1, source_target_pairs={{4,0},{8,4},{12,8},{5,1},{9,5},{13,9},{6,2},{10,6},{14,10},{7,3},{... | collective-permute-start | bytes 786440 | tf_op jit(solution)/shard_map/ppermute | solution.py:370
  18.8 5.1 %collective-permute-start.2 = (f32[64,128]{1,0:T(8,128)S(1)}, f32[64,128]{1,0:T(8,128)S(1)}, u32[]{:S(2)}, u32[]{:S(2)}) collective-permute-start(f32[64,128]{1,0:T(8,128)S(1)} %get-tuple-element.37), channel_id=1, source_target_pairs={{0,1},{1,2},{2,3},{4,5},{5,6},{6,7},{8,9},{9,10},{10,11},{12,13},{... | collective-permute-start | bytes 98312 | tf_op jit(solution)/shard_map/ppermute | solution.py:370
  21.9 4.7 %collective-permute-start.3 = (f32[64,128]{1,0:T(8,128)S(1)}, f32[64,128]{1,0:T(8,128)S(1)}, u32[]{:S(2)}, u32[]{:S(2)}) collective-permute-start(f32[64,128]{1,0:T(8,128)S(1)} %get-tuple-element.38), channel_id=1, source_target_pairs={{1,0},{2,1},{3,2},{5,4},{6,5},{7,6},{9,8},{10,9},{11,10},{13,12},{... | collective-permute-start | bytes 98312 | tf_op jit(solution)/shard_map/ppermute | solution.py:370
  32.4 42.5 %collective-permute-start.12 = (f32[32,32,256]{2,1,0:T(8,128)S(1)}, f32[32,32,256]{2,1,0:T(8,128)S(1)}, u32[]{:S(2)}, u32[]{:S(2)}) collective-permute-start(f32[32,32,256]{2,1,0:T(8,128)S(1)} %get-tuple-element.67), channel_id=1, source_target_pairs={{0,16},{16,0},{32,48},{48,32},{64,80},{80,64},{96,112},{112,96},{1... | collective-permute-start | bytes 3145736 | tf_op jit(solution)/shard_map/ppermute | solution.py:404
  43.6 16.7 %collective-permute-start.8 = (f32[16,32,256]{2,1,0:T(8,128)S(1)}, f32[16,32,256]{2,1,0:T(8,128)S(1)}, u32[]{:S(2)}, u32[]{:S(2)}) collective-permute-start(f32[16,32,256]{2,1,0:T(8,128)S(1)} %get-tuple-element.63), channel_id=1, source_target_pairs={{0,64},{16,80},{32,96},{48,112},{64,0},{80,16},{96,32},{112,48},{1... | collective-permute-start | bytes 1572872 | tf_op jit(solution)/shard_map/ppermute | solution.py:404
  46.6 23.7 %collective-permute-start.9 = (f32[16,32,256]{2,1,0:T(8,128)S(1)}, f32[16,32,256]{2,1,0:T(8,128)S(1)}, u32[]{:S(2)}, u32[]{:S(2)}) collective-permute-start(f32[16,32,256]{2,1,0:T(8,128)S(1)} %get-tuple-element.64), channel_id=1, source_target_pairs={{0,32},{16,48},{32,64},{48,80},{64,96},{80,112},{96,0},{112,16},{1... | collective-permute-start | bytes 1572872 | tf_op jit(solution)/shard_map/ppermute | solution.py:404
  47.0 25.3 %collective-permute-start.10 = (f32[16,32,256]{2,1,0:T(8,128)S(1)}, f32[16,32,256]{2,1,0:T(8,128)S(1)}, u32[]{:S(2)}, u32[]{:S(2)}) collective-permute-start(f32[16,32,256]{2,1,0:T(8,128)S(1)} %get-tuple-element.65), channel_id=1, source_target_pairs={{0,96},{16,112},{32,0},{48,16},{64,32},{80,48},{96,64},{112,80},{1... | collective-permute-start | bytes 1572872 | tf_op jit(solution)/shard_map/ppermute | solution.py:404
  57.2 18.3 %collective-permute-start.6 = (f32[32,128]{1,0:T(8,128)S(1)}, f32[32,128]{1,0:T(8,128)S(1)}, u32[]{:S(2)}, u32[]{:S(2)}) collective-permute-start(f32[32,128]{1,0:T(8,128)S(1)} %get-tuple-element.58), channel_id=1, source_target_pairs={{0,1},{1,2},{2,3},{4,5},{5,6},{6,7},{8,9},{9,10},{10,11},{12,13},{... | collective-permute-start | bytes 49160 | tf_op jit(solution)/shard_map/ppermute | solution.py:370
  60.3 17.4 %collective-permute-start.7 = (f32[32,128]{1,0:T(8,128)S(1)}, f32[32,128]{1,0:T(8,128)S(1)}, u32[]{:S(2)}, u32[]{:S(2)}) collective-permute-start(f32[32,128]{1,0:T(8,128)S(1)} %get-tuple-element.59), channel_id=1, source_target_pairs={{1,0},{2,1},{3,2},{5,4},{6,5},{7,6},{9,8},{10,9},{11,10},{13,12},{... | collective-permute-start | bytes 49160 | tf_op jit(solution)/shard_map/ppermute | solution.py:370
  70.4 9.0 %collective-permute-start.4 = (f32[128,256]{1,0:T(8,128)S(1)}, f32[128,256]{1,0:T(8,128)S(1)}, u32[]{:S(2)}, u32[]{:S(2)}) collective-permute-start(f32[128,256]{1,0:T(8,128)S(1)} %get-tuple-element.56), channel_id=1, source_target_pairs={{0,4},{4,8},{8,12},{1,5},{5,9},{9,13},{2,6},{6,10},{10,14},{3,7},{... | collective-permute-start | bytes 393224 | tf_op jit(solution)/shard_map/ppermute | solution.py:370
  72.3 7.9 %collective-permute-start.5 = (f32[128,256]{1,0:T(8,128)S(1)}, f32[128,256]{1,0:T(8,128)S(1)}, u32[]{:S(2)}, u32[]{:S(2)}) collective-permute-start(f32[128,256]{1,0:T(8,128)S(1)} %get-tuple-element.57), channel_id=1, source_target_pairs={{4,0},{8,4},{12,8},{5,1},{9,5},{13,9},{6,2},{10,6},{14,10},{7,3},{... | collective-permute-start | bytes 393224 | tf_op jit(solution)/shard_map/ppermute | solution.py:370
  74.9 15.1 %collective-permute-start.11 = (f32[8,32,256]{2,1,0:T(8,128)S(1)}, f32[8,32,256]{2,1,0:T(8,128)S(1)}, u32[]{:S(2)}, u32[]{:S(2)}) collective-permute-start(f32[8,32,256]{2,1,0:T(8,128)S(1)} %slice.29), channel_id=1, source_target_pairs={{0,16},{16,0},{32,48},{48,32},{64,80},{80,64},{96,112},{112,96},{1... | collective-permute-start | bytes 786440 | tf_op jit(solution)/shard_map/ppermute | solution.py:404
  75.4 14.6 %collective-permute-start.13 = (f32[8,32,256]{2,1,0:T(8,128)S(1)}, f32[8,32,256]{2,1,0:T(8,128)S(1)}, u32[]{:S(2)}, u32[]{:S(2)}) collective-permute-start(f32[8,32,256]{2,1,0:T(8,128)S(1)} %get-tuple-element.68), channel_id=1, source_target_pairs={{0,64},{16,80},{32,96},{48,112},{64,0},{80,16},{96,32},{112,48},{1... | collective-permute-start | bytes 786440 | tf_op jit(solution)/shard_map/ppermute | solution.py:404
  77.7 12.4 %collective-permute-start.15 = (f32[8,32,256]{2,1,0:T(8,128)S(1)}, f32[8,32,256]{2,1,0:T(8,128)S(1)}, u32[]{:S(2)}, u32[]{:S(2)}) collective-permute-start(f32[8,32,256]{2,1,0:T(8,128)S(1)} %get-tuple-element.69), channel_id=1, source_target_pairs={{0,96},{16,112},{32,0},{48,16},{64,32},{80,48},{96,64},{112,80},{1... | collective-permute-start | bytes 786440 | tf_op jit(solution)/shard_map/ppermute | solution.py:404
  79.4 11.4 %collective-permute-start.14 = (f32[8,32,256]{2,1,0:T(8,128)S(1)}, f32[8,32,256]{2,1,0:T(8,128)S(1)}, u32[]{:S(2)}, u32[]{:S(2)}) collective-permute-start(f32[8,32,256]{2,1,0:T(8,128)S(1)} %get-tuple-element.70), channel_id=1, source_target_pairs={{0,32},{16,48},{32,64},{48,80},{64,96},{80,112},{96,0},{112,16},{1... | collective-permute-start | bytes 786440 | tf_op jit(solution)/shard_map/ppermute | solution.py:404

commit v3 on v2

--- a/solution.py
+++ b/solution.py
@@ -12,14 +12,11 @@
 VMEM_LIMIT = 16 * 1024 * 1024
 LANES = 128
 ROWS = 8
+UNROLL = (8, 4)
 VMEM = pl.BlockSpec(memory_space=pltpu.VMEM)
+ANY = pl.BlockSpec(memory_space=pl.ANY)
 SMEM = pl.BlockSpec(memory_space=pltpu.SMEM)
 HBM = pl.BlockSpec(memory_space=pltpu.HBM)
-
-
-def reciprocal(value):
-    guess = pl.reciprocal(value, approx=True)
-    return guess * (2.0 - value * guess)
 
 
 def lane_to(values, source, target):
@@ -39,10 +36,16 @@
 
 def over(planes, unroll, body, carry=()):
     def some(k, carry):
+        stores = []
         for u in range(unroll):
-            carry = body(k * unroll + u, carry)
+            carry, more = body(k * unroll + u, carry)
+            stores += more
+        for ref, index, value in stores:
+            ref[index] = value
         return carry
 
+    if unroll == planes:
+        return some(0, carry)
     return lax.fori_loop(0, planes // unroll, some, carry)
 
 
@@ -56,9 +59,23 @@
 
 def halo_rows(wide, x, low, high):
     ny = wide.shape[2] - 2 * ROWS
+    stores = []
     for h in range(wide.shape[0]):
-        wide[h, x + 1, ROWS - 1 : ROWS, :] = low[:, run(h)]
-        wide[h, x + 1, ROWS + ny : ROWS + ny + 1, :] = high[:, run(h)]
+        stores.append((wide, (h, x + 1, slice(ROWS - 1, ROWS)), low[:, run(h)]))
+        stores.append((wide, (h, x + 1, slice(ROWS + ny, ROWS + ny + 1)), high[:, run(h)]))
+    return stores
+
+
+def face_rows(wide, x, row):
+    count, planes, rows, _ = wide.shape
+    flat = wide.reshape(count, planes * rows, LANES)
+    return [flat[h, pl.ds((x + 1) * rows + ROWS + row, ROWS, stride=rows), :] for h in range(count)]
+
+
+def store_rows(face, x, values, *lead):
+    at = pl.ds(pl.multiple_of(x, ROWS), ROWS)
+    for h, value in enumerate(values):
+        face[(*lead, at, run(h))] = value
 
 
 def weighted(wide, at, lane, z_low, z_high):
@@ -91,7 +108,7 @@
         body(t, slot)
 
 
-def prepare_kernel(planes, unroll, adj_hbm, pore_hbm, masked, kept, y_low, y_high, z_low, z_high, adj, pore, wide, sem):
+def faces_kernel(planes, unroll, adj_hbm, pore_hbm, masked, wide, y_low, y_high, z_low, z_high, adj, pore, sem):
     nx, ny, nz = adj_hbm.shape
     count = nz // LANES
     lane = lax.broadcasted_iota(jnp.int32, (ny, LANES), 1)
@@ -101,12 +118,6 @@
         for x in (0, nx + 1):
             masked[h, x] = jnp.zeros_like(masked[h, x])
             wide[h, x] = jnp.zeros_like(wide[h, x])
-
-    def clear(x, carry):
-        for h in range(count):
-            wide[h, x + 1, :ROWS, :] = jnp.zeros((ROWS, LANES), F32)
-            wide[h, x + 1, ROWS + ny :, :] = jnp.zeros((ROWS, LANES), F32)
-        return carry
 
     def copies(t, slot):
         at = pl.ds(t * planes, planes)
@@ -120,71 +131,86 @@
             x = t * planes + i
             here = lane == x
             out = list(carry)
-            clear(x, ())
-            pores = pore[slot, i].astype(F32)
-            for part, value in enumerate((adj[slot, i] * pores, pores)):
-                halves = [value[:, run(h)] for h in range(count)]
-                for h in range(count):
-                    (wide if part else masked)[h, x + 1, ROWS : ROWS + ny, :] = halves[h]
-                y_low[part, pl.ds(x, 1), :] = value[:1]
-                y_high[part, pl.ds(x, 1), :] = value[ny - 1 :]
-                out[part] = jnp.where(here, lane_to(halves[0], 0, x), out[part])
-                out[2 + part] = jnp.where(here, lane_to(halves[-1], LANES - 1, x), out[2 + part])
-            return tuple(out)
+            stores = []
+            for h in range(count):
+                pores = pore[slot, i, :, run(h)].astype(F32)
+                for part, (array, value) in enumerate(((masked, adj[slot, i, :, run(h)] * pores), (wide, pores))):
+                    stores.append((array, (h, x + 1, slice(ROWS, ROWS + ny)), value))
+                    if h == 0:
+                        out[part] = jnp.where(here, lane_to(value, 0, x), out[part])
+                    if h == count - 1:
+                        out[2 + part] = jnp.where(here, lane_to(value, LANES - 1, x), out[2 + part])
+                for rows in (slice(0, ROWS), slice(ROWS + ny, 2 * ROWS + ny)):
+                    stores.append((wide, (h, x + 1, rows), jnp.zeros((ROWS, LANES), F32)))
+            return tuple(out), stores
 
         parts = (z_low[:ny], z_low[ny:], z_high[:ny], z_high[ny:])
         z_low[:ny], z_low[ny:], z_high[:ny], z_high[ny:] = over(planes, unroll, load, parts)
 
-        def weigh(i, carry):
-            x = t * planes + i - 1 if t else i
-            zero = jnp.zeros((ny, LANES), F32)
-            pores, sums = weighted(wide, x + 1, lane, zero, zero)
-            outer = jnp.where(x == nx - 1, 0.8, 1.0)
-            for h in range(count):
-                kept[h, x] = jnp.where(pores[h] > 0.0, outer - 0.1 * sums[h], SOLID)
-            return carry
-
-        over(planes if t else planes - 1, unroll if t else 1, weigh)
-        if t == steps - 1:
-            weigh(planes, ())
+        for x in range(t * planes, (t + 1) * planes, ROWS):
+            for part, array in enumerate((masked, wide)):
+                store_rows(y_low, x, face_rows(array, x, 0), part)
+                store_rows(y_high, x, face_rows(array, x, ny - 1), part)
 
     rotating(steps, copies, body)
 
 
-def prepare(adjoint, pores, planes=16, unroll=4):
+def faces(adjoint, pores, planes=16, unroll=16):
     nx, ny, nz = adjoint.shape
     y_shape = jax.ShapeDtypeStruct((2, nx, nz), F32)
     z_shape = jax.ShapeDtypeStruct((2 * ny, nx), F32)
     wide = padded_shape(nx, ny, nz)
     return pl.pallas_call(
-        functools.partial(prepare_kernel, planes, unroll),
+        functools.partial(faces_kernel, planes, unroll),
         in_specs=[HBM, HBM],
         out_specs=[VMEM] * 6,
-        out_shape=[
-            pltpu.VMEM(wide, F32),
-            pltpu.VMEM((nz // LANES, nx, ny, LANES), F32),
-            y_shape,
-            y_shape,
-            z_shape,
-            z_shape,
-        ],
+        out_shape=[pltpu.VMEM(wide, F32), pltpu.VMEM(wide, F32), y_shape, y_shape, z_shape, z_shape],
         scratch_shapes=[
             pltpu.VMEM((2, planes, ny, nz), F32),
             pltpu.VMEM((2, planes, ny, nz), jnp.int32),
-            pltpu.VMEM(wide, F32),
             pltpu.SemaphoreType.DMA((2, 2)),
         ],
         compiler_params=pltpu.CompilerParams(vmem_limit_bytes=VMEM_LIMIT),
-        cost_estimate=pl.CostEstimate(flops=14 * nx * ny * nz, bytes_accessed=8 * nx * ny * nz, transcendentals=0),
-        name="prepare",
+        cost_estimate=pl.CostEstimate(flops=4 * nx * ny * nz, bytes_accessed=8 * nx * ny * nz, transcendentals=0),
+        name="faces",
     )(*in_hbm(adjoint, pores))
+
+
+def weigh_kernel(unroll, wide, kept):
+    count, nx, ny, _ = kept.shape
+    lane = lax.broadcasted_iota(jnp.int32, (ny, LANES), 1)
+    zero = jnp.zeros((ny, LANES), F32)
+
+    def body(x, carry):
+        pores, sums = weighted(wide, x + 1, lane, zero, zero)
+        outer = jnp.where(x == nx - 1, 0.8, 1.0)
+        return carry, [
+            (kept, (h, x), jnp.where(pores[h] > 0.0, outer - 0.1 * sums[h], SOLID)) for h in range(count)
+        ]
+
+    over(nx, unroll, body)
+
+
+def weigh(wide, unroll=32):
+    count, nx, rows, lanes = wide.shape
+    shape = (count, nx - 2, rows - 2 * ROWS, lanes)
+    voxels = shape[0] * shape[1] * shape[2] * shape[3]
+    return pl.pallas_call(
+        functools.partial(weigh_kernel, unroll),
+        in_specs=[VMEM],
+        out_specs=VMEM,
+        out_shape=pltpu.VMEM(shape, F32),
+        compiler_params=pltpu.CompilerParams(vmem_limit_bytes=VMEM_LIMIT),
+        cost_estimate=pl.CostEstimate(flops=12 * voxels, bytes_accessed=12 * voxels, transcendentals=0),
+        name="weigh",
+    )(*in_vmem(wide))
 
 
 def stage_kernel(places, counts, planes, unroll, fresh, *refs):
     which, affinities, cap_hbm, filled_hbm, seen_hbm, y_low, y_high, z_low, z_high = refs[:9]
     refs = refs[9 + (2 if fresh else 7) :]
     (masked, kept, adj, out_y_low, out_y_high, out_z_low, out_z_high), refs = refs[:7], refs[7:]
-    outs, (cap, late_f, early_f, late_o, sem) = refs[:-5], refs[-5:]
+    outs, (cap, late_f, early_f, late_o, inflow, sem) = refs[:-6], refs[-6:]
     count, nx, ny, _ = kept.shape
     lane = lax.broadcasted_iota(jnp.int32, (ny, LANES), 1)
     starts = places()
@@ -219,26 +245,33 @@
         def ends(i, carry):
             x = start + i
             row = pl.ds(x, 1)
-            halo_rows(masked, x, y_low[0, row, :], y_high[0, row, :])
+            stores = halo_rows(masked, x, y_low[0, row, :], y_high[0, row, :])
             low, high = 0.1 * y_low[1, row, :], 0.1 * y_high[1, row, :]
             for h in range(count):
-                kept[h, x, :1, :] = kept[h, x, :1, :] - low[:, run(h)]
-                kept[h, x, ny - 1 :, :] = kept[h, x, ny - 1 :, :] - high[:, run(h)]
-            return carry
-
-        over(planes, unroll, ends)
+                for rows, value in ((slice(0, 1), low), (slice(ny - 1, ny), high)):
+                    stores.append((kept, (h, x, rows), kept[h, x, rows, :] - value[:, run(h)]))
+            return carry, stores
+
+        over(planes, planes, ends)
+
+        def gather(i, carry):
+            x = start + i
+            _, sums = weighted(masked, x + 1, lane, lane_to(m_low, x, 0), lane_to(m_high, x, LANES - 1))
+            return carry, [(inflow, (h, i), 0.1 * sums[h]) for h in range(count)]
+
+        over(planes, unroll[0], gather)
 
         def plane(i, carry):
             low, high = carry
             x = start + i
-            m_c, m_sum = weighted(masked, x + 1, lane, lane_to(m_low, x, 0), lane_to(m_high, x, LANES - 1))
-            values = []
+            stores = []
             for h in range(count):
+                centre = masked[h, x + 1, ROWS : ROWS + ny, :]
                 filled = late_f[slot, i, :, run(h)].astype(F32)
                 early = early_f[slot, i, :, run(h)].astype(F32)
                 source = filled - late_o[slot, i, :, run(h)].astype(F32)
-                late_r = reciprocal(-inverse - filled)
-                early_r = reciprocal(-inverse - early)
+                late_r = pl.reciprocal(-inverse - filled, approx=True)
+                early_r = pl.reciprocal(-inverse - early, approx=True)
                 weight = kept[h, x]
                 if h == 0:
                     weight = weight - jnp.where(lane == 0, lane_to(p_low, x, 0), 0.0)
@@ -246,19 +279,22 @@
                     weight = weight - jnp.where(lane == LANES - 1, lane_to(p_high, x, LANES - 1), 0.0)
                 pore = weight != SOLID
                 uptake = cap[slot, i, :, run(h)] * inverse
-                updated = m_c[h] * (weight - uptake * (late_r * late_r)) + (0.1 * m_sum[h] + source)
+                updated = centre * (weight - uptake * (late_r * late_r)) + (inflow[h, i] + source)
                 updated = jnp.where(pore, updated, 0.0)
-                kept[h, x] = jnp.where(pore, weight - uptake * (early_r * early_r), SOLID)
-                grad[block * planes + i, :, run(h)] = (filled * late_r) * m_c[h] + (early * early_r) * updated
-                adj[h, x + 1, ROWS : ROWS + ny, :] = updated
-                values.append(updated)
-            out_y_low[pl.ds(x, 1), :] = jnp.concatenate([v[:1] for v in values], 1)
-            out_y_high[pl.ds(x, 1), :] = jnp.concatenate([v[ny - 1 :] for v in values], 1)
-            low = jnp.where(lane == x, lane_to(values[0], 0, x), low)
-            high = jnp.where(lane == x, lane_to(values[-1], LANES - 1, x), high)
-            return low, high
-
-        out_z_low[...], out_z_high[...] = over(planes, unroll, plane, (out_z_low[...], out_z_high[...]))
+                stores.append((kept, (h, x), jnp.where(pore, weight - uptake * (early_r * early_r), SOLID)))
+                term = (filled * late_r) * centre + (early * early_r) * updated
+                stores.append((grad, (block * planes + i, slice(None), run(h)), term))
+                stores.append((adj, (h, x + 1, slice(ROWS, ROWS + ny)), updated))
+                if h == 0:
+                    low = jnp.where(lane == x, lane_to(updated, 0, x), low)
+                if h == count - 1:
+                    high = jnp.where(lane == x, lane_to(updated, LANES - 1, x), high)
+            return (low, high), stores
+
+        out_z_low[...], out_z_high[...] = over(planes, unroll[1], plane, (out_z_low[...], out_z_high[...]))
+        for at in range(0, planes, ROWS):
+            store_rows(out_y_low, start + at, face_rows(adj, start + at, 0))
+            store_rows(out_y_high, start + at, face_rows(adj, start + at, ny - 1))
 
     rotating(sum(counts), copies, body)
 
@@ -283,6 +319,7 @@
             pltpu.VMEM(block, jnp.bfloat16),
             pltpu.VMEM(block, jnp.bfloat16),
             pltpu.VMEM(block, jnp.bfloat16),
+            pltpu.VMEM((nz // LANES, planes, ny, LANES), F32),
             pltpu.SemaphoreType.DMA((2, 4)),
         ],
         input_output_aliases={base + k: k for k in range(len(state))},
@@ -293,7 +330,7 @@
     return results[:7], results[7:]
 
 
-def last_kernel(planes, unroll, f_hbm, o_hbm, kept, y_low, y_high, z_low, z_high, _, out_hbm, adj, filled, seen, out, sem, out_sem):
+def last_kernel(planes, unroll, f_hbm, o_hbm, kept, y_low, y_high, z_low, z_high, _, _after, out_hbm, adj, filled, seen, out, sem, out_sem):
     count, nx, ny, _ = kept.shape
     lane = lax.broadcasted_iota(jnp.int32, (ny, LANES), 1)
     steps = nx // planes
@@ -315,20 +352,20 @@
         def ends(i, carry):
             x = t * planes + i
             row = pl.ds(x, 1)
-            halo_rows(adj, x, y_low[row, :], y_high[row, :])
-            return carry
-
-        over(planes, unroll, ends)
+            return carry, halo_rows(adj, x, y_low[row, :], y_high[row, :])
+
+        over(planes, planes, ends)
 
         def plane(i, carry):
             x = t * planes + i
             centre, sums = weighted(adj, x + 1, lane, lane_to(z_low[...], x, 0), lane_to(z_high[...], x, LANES - 1))
+            stores = []
             for h in range(count):
                 weight = kept[h, x]
                 source = filled[slot, i, :, run(h)].astype(F32) - seen[slot, i, :, run(h)].astype(F32)
                 value = centre[h] * weight + (0.1 * sums[h] + source)
-                out[slot, i, :, run(h)] = jnp.where(weight == SOLID, 0.0, value)
-            return carry
+                stores.append((out, (slot, i, slice(None), run(h)), jnp.where(weight == SOLID, 0.0, value)))
+            return carry, stores
 
         over(planes, unroll, plane)
         writing(t).start()
@@ -338,13 +375,13 @@
     writing(steps - 1).wait()
 
 
-def last_step(adjoint, kept, filled, seen, halo, planes=16, unroll=4):
+def last_step(adjoint, kept, filled, seen, halo, after, planes=16, unroll=16):
     count, nx, ny, lanes = kept.shape
     nz = count * lanes
     voxels = nx * ny * nz
     return pl.pallas_call(
         functools.partial(last_kernel, planes, unroll),
-        in_specs=[HBM, HBM] + [VMEM] * 6,
+        in_specs=[HBM, HBM] + [VMEM] * 6 + [ANY],
         out_specs=[HBM, VMEM],
         out_shape=[jax.ShapeDtypeStruct((nx, ny, nz), F32), pltpu.VMEM(adjoint.shape, F32)],
         scratch_shapes=[
@@ -358,7 +395,38 @@
         compiler_params=pltpu.CompilerParams(vmem_limit_bytes=VMEM_LIMIT),
         cost_estimate=pl.CostEstimate(flops=20 * voxels, bytes_accessed=8 * voxels, transcendentals=0),
         name="last_step",
-    )(*in_hbm(filled, seen), *in_vmem(kept), *halo, *in_vmem(adjoint))[0]
+    )(*in_hbm(filled, seen), *in_vmem(kept), *halo, *in_vmem(adjoint), after)[0]
+
+
+def add_kernel(n_parts, n_after, unroll, *refs):
+    parts, outs = refs[:n_parts], refs[n_parts + n_after :]
+    planes = outs[0].shape[0]
+
+    def body(i, carry):
+        stores = []
+        for k, out in enumerate(outs):
+            total = parts[0][k * planes + i]
+            for part in parts[1:]:
+                total = total + part[k * planes + i]
+            stores.append((out, (i,), total))
+        return carry, stores
+
+    over(planes, unroll, body)
+
+
+def add(parts, after, pieces, name, unroll=2):
+    planes, ny, nz = parts[0].shape
+    shape = jax.ShapeDtypeStruct((planes // pieces, ny, nz), F32)
+    size = planes * ny * nz
+    return pl.pallas_call(
+        functools.partial(add_kernel, len(parts), len(after), unroll),
+        in_specs=[VMEM] * len(parts) + [ANY] * len(after),
+        out_specs=[VMEM] * pieces,
+        out_shape=[shape] * pieces,
+        compiler_params=pltpu.CompilerParams(vmem_limit_bytes=VMEM_LIMIT),
+        cost_estimate=pl.CostEstimate(flops=size * len(parts), bytes_accessed=4 * size, transcendentals=0),
+        name=name,
+    )(*parts, *after)
 
 
 def exchange(y_low, y_high, z_low, z_high):
@@ -407,25 +475,24 @@
     at = [functools.partial(places, ring, pairs, share, order) for order in orders(ring)]
     fields = (capacity, filled, seen)
 
-    *state, y_low, y_high, z_low, z_high = prepare(adjoint, pore_mask)
-    halo = exchange(y_low, y_high, z_low, z_high)
-    state, (cross,) = stage(scalars, fields, halo, state, at[0], (4,), planes, 2, "cross")
+    masked, wide, *outer = faces(adjoint, pore_mask)
+    halo = exchange(*outer)
+    state = (masked, weigh(wide))
+    state, (cross,) = stage(scalars, fields, halo, state, at[0], (4,), planes, UNROLL, "cross")
     crossed = send(cross, 0, 1)
-    state, along = stage(scalars, fields, halo, state, at[1], (2, 2, 2), planes, 2, "along")
+    state, along = stage(scalars, fields, halo, state, at[1], (2, 2, 2), planes, UNROLL, "along")
     parts_p = [send(value, turn, 0) for value, turn in zip(along, (2, 1, 3))]
-    (_, kept, next_adjoint, *next_faces), (own_p, own_q) = stage(scalars, fields, halo, state, at[2], (2, 4), planes, 2, "own")
+    (_, kept, next_adjoint, *next_faces), (own_p, own_q) = stage(scalars, fields, halo, state, at[2], (2, 4), planes, UNROLL, "own")
     face_halo = exchange(*next_faces)
 
-    total_p = own_p + parts_p[0] + parts_p[1] + parts_p[2]
-    last_p = send(total_p[:planes], 0, 1)
-    total_q = (own_q + crossed).reshape(ring, planes, ny, nz)
-    parts_q = [send(total_q[turn], turn, 0) for turn in (2, 1, 3)]
-
-    adjoint_first = last_step(next_adjoint, kept, filled, seen, face_halo)
-
-    sum_p = total_p[planes:] + last_p
-    sum_q = total_q[0] + parts_q[0] + parts_q[1] + parts_q[2]
-    return adjoint_first[None], jnp.concatenate([sum_p, sum_q], 0)
+    totals_q = add([own_q, crossed], face_halo, ring, "add_q")
+    parts_q = [send(totals_q[turn], turn, 0) for turn in (2, 1, 3)]
+    total_s, total_k = add([own_p, *parts_p], totals_q[:1], 2, "add_p")
+    last_p = send(total_s, 0, 1)
+    adjoint_first = last_step(next_adjoint, kept, filled, seen, face_halo, total_k)
+
+    sum_q = totals_q[0] + parts_q[0] + parts_q[1] + parts_q[2]
+    return adjoint_first[None], jnp.concatenate([total_k + last_p, sum_q], 0)
 
 
 def solution(mesh):

time: 92.6 us -> 88.5 us (0.956)
  Pallas kernels: 42.6 us -> 35.7 us
  starting transfers between devices: 33.3 us -> 37.3 us
    ppermute x8, waiting for transfers between devices: 9.53 us -> 0.02 us  [send(): return lax.ppermute(value, 'exp', perm)]
    ppermute x8, waiting for transfers between devices: 3.51 us -> 12.1 us  [exchange(): received += [lax.ppermute(high, axis, up), lax.ppermute(low, axis, down)]]
    ppermute x8, starting transfers between devices: 20 us -> 24.6 us  [exchange(): received += [lax.ppermute(high, axis, up), lax.ppermute(low, axis, down)]]
    pallas_call x3, Pallas kernels: 21.5 us -> 18.5 us  [stage(): pl.pallas_call(functools.partial(stage_kernel, places, counts, planes, un...]
    pallas_call x1 -> x4, Pallas kernels: 11.3 us -> 9.13 us  [the longest x1 6.45 us: faces(): pl.pallas_call(functools.partial(faces_kernel, planes, unroll), in_specs=...]
    pallas_call x1, Pallas kernels: 9.78 us -> 8.08 us  [last_step(): pl.pallas_call(functools.partial(last_kernel, planes, unroll), in_specs=[...]
  transfers between devices with their start and end apart: 16 -> 16, of which waited for: 4 -> 5; matrix products, arithmetic and copies ran while one was open for 0% -> 0% of each run, Pallas kernels for 28% -> 28%
where the time goes in v3:
time: 88.5 us; the launch traced here: 87.7 us
  starting transfers between devices  37.3 us (42%)
  Pallas kernels  35.7 us (40%)
  waiting for transfers between devices  12.1 us (14%)
  between operations  1.5 us (2%)
  other arithmetic  0.95 us (1%)
    ppermute x8, starting transfers between devices, exchange(): received += [lax.ppermute(high, axis, up), lax.ppermute(low, axis, down)]  24.6 us
    pallas_call x3, Pallas kernels, stage(): pl.pallas_call(functools.partial(stage_kernel, places, counts, planes, un...  18.5 us
    ppermute x8, starting transfers between devices, send(): return lax.ppermute(value, 'exp', perm)  12.8 us
    ppermute x8, waiting for transfers between devices, exchange(): received += [lax.ppermute(high, axis, up), lax.ppermute(low, axis, down)]  12.1 us
    pallas_call x1, Pallas kernels, last_step(): pl.pallas_call(functools.partial(last_kernel, planes, unroll), in_specs=[...  8.08 us
    pallas_call x1, Pallas kernels, faces(): pl.pallas_call(functools.partial(faces_kernel, planes, unroll), in_specs=...  6.45 us
    pallas_call x1, Pallas kernels, weigh(): pl.pallas_call(functools.partial(weigh_kernel, unroll), in_specs=[VMEM],...  2.45 us
  transfers between devices with their start and end apart: 16, of which 5 were waited for; matrix products, arithmetic and copies ran while one was open for 0% of the time, Pallas kernels for 28%

profile of v3, /device:TPU:1, one launch (start us, length us, event | category | flops | bytes accessed | tf_op | source)
XLA Modules:
  0.0 87.7 jit_solution(13071401847694970035)
XLA Ops:
  0.6 6.5 %faces.1 = (f32[2,130,48,128]{3,2,1,0:T(8,128)S(1)}, f32[2,130,48,128]{3,2,1,0:T(8,128)S(1)}, f32[2,128,256]{2,1,0:T(8,128)S(1)}, f32[2,128,256]{2,1,0:T(8,128)S...) custom-call(f32[128,32,256]{2,1,0:T(8,128)} %bitcast.12, s32[128,32,256]{2,1,0:T(8,128)} %pore_hbm.1), custom_call_target="tpu_custom_call" | custom-call | flops 4194304 | bytes 8388608 | tf_op jit(solution)/shard_map/faces/pallas_call | solution.py:163
  7.1 4.9 %collective-permute-start = (f32[2,128,256]{2,1,0:T(8,128)S(1)}, f32[2,128,256]{2,1,0:T(8,128)S(1)}, u32[]{:S(2)}, u32[]{:S(2)}) collective-permute-start(f32[2,128,256]{2,1,0:T(8,128)S(1)} %get-tuple-element.41), channel_id=1, source_target_pairs={{0,4},{4,8},{8,12},{1,5},{5,9},{9,13},{2,6},{6,10},{10,14},{3,7},{... | collective-permute-start | bytes 786440 | tf_op jit(solution)/shard_map/ppermute | solution.py:438
  12.0 1.9 %collective-permute-start.1 = (f32[2,128,256]{2,1,0:T(8,128)S(1)}, f32[2,128,256]{2,1,0:T(8,128)S(1)}, u32[]{:S(2)}, u32[]{:S(2)}) collective-permute-start(f32[2,128,256]{2,1,0:T(8,128)S(1)} %get-tuple-element.42), channel_id=1, source_target_pairs={{4,0},{8,4},{12,8},{5,1},{9,5},{13,9},{6,2},{10,6},{14,10},{7,3},{... | collective-permute-start | bytes 786440 | tf_op jit(solution)/shard_map/ppermute | solution.py:438
  14.0 3.1 %collective-permute-start.2 = (f32[64,128]{1,0:T(8,128)S(1)}, f32[64,128]{1,0:T(8,128)S(1)}, u32[]{:S(2)}, u32[]{:S(2)}) collective-permute-start(f32[64,128]{1,0:T(8,128)S(1)} %get-tuple-element.43), channel_id=1, source_target_pairs={{0,1},{1,2},{2,3},{4,5},{5,6},{6,7},{8,9},{9,10},{10,11},{12,13},{... | collective-permute-start | bytes 98312 | tf_op jit(solution)/shard_map/ppermute | solution.py:438
  17.1 1.3 %collective-permute-start.3 = (f32[64,128]{1,0:T(8,128)S(1)}, f32[64,128]{1,0:T(8,128)S(1)}, u32[]{:S(2)}, u32[]{:S(2)}) collective-permute-start(f32[64,128]{1,0:T(8,128)S(1)} %get-tuple-element.44), channel_id=1, source_target_pairs={{1,0},{2,1},{3,2},{5,4},{6,5},{7,6},{9,8},{10,9},{11,10},{13,12},{... | collective-permute-start | bytes 98312 | tf_op jit(solution)/shard_map/ppermute | solution.py:438
  19.0 0.0 copy-start
  19.0 2.4 %weigh.1.refs_10_ = f32[2,128,32,128]{3,2,1,0:T(8,128)S(1)} custom-call(f32[2,130,48,128]{3,2,1,0:T(8,128)S(1)} %get-tuple-element.46.wide), custom_call_target="tpu_custom_call" | custom-call | flops 12582912 | bytes 12582912 | tf_op jit(solution)/shard_map/weigh/pallas_call | solution.py:198
  21.5 0.0 collective-permute-done.2.refs_7_
  21.5 0.2 collective-permute-done.3.refs_8_
  21.7 0.0 collective-permute-done.refs_5_
  21.7 0.0 collective-permute-done.1.refs_6_
  21.8 0.0 copy-done
  21.8 5.0 %cross.1 = (f32[2,130,48,128]{3,2,1,0:T(8,128)S(1)}, f32[2,128,32,128]{3,2,1,0:T(8,128)S(1)}, f32[2,130,48,128]{3,2,1,0:T(8,128)S(1)}, f32[128,256]{1,0:T(8,128)...) custom-call(s32[1]{0:T(128)S(6)} %copy.43.refs_0_, ...), custom_call_target="tpu_custom_call", output_to_operand_aliasing={{0}: (9, {}), {1}: (10, {})} | custom-call | flops 10485760 | bytes 2621440 | tf_op jit(solution)/shard_map/cross/pallas_call | solution.py:312
  26.8 3.4 %collective-permute-start.11 = (f32[32,32,256]{2,1,0:T(8,128)S(1)}, f32[32,32,256]{2,1,0:T(8,128)S(1)}, u32[]{:S(2)}, u32[]{:S(2)}) collective-permute-start(f32[32,32,256]{2,1,0:T(8,128)S(1)} %get-tuple-element.72), channel_id=1, source_target_pairs={{0,16},{16,0},{32,48},{48,32},{64,80},{80,64},{96,112},{112,96},{1... | collective-permute-start | bytes 3145736 | tf_op jit(solution)/shard_map/ppermute | solution.py:472
  30.2 6.7 %along.1 = (f32[2,130,48,128]{3,2,1,0:T(8,128)S(1)}, f32[2,128,32,128]{3,2,1,0:T(8,128)S(1)}, f32[2,130,48,128]{3,2,1,0:T(8,128)S(1)}, f32[128,256]{1,0:T(8,128)...) custom-call(s32[1]{0:T(128)S(6)} %copy.43.refs_0_, ...), custom_call_target="tpu_custom_call", output_to_operand_aliasing={{0}: (9, {}), {1}: (10, {}), {2}: (11, {}), {3}: (12, {}), ... | custom-call | flops 15728640 | bytes 3932160 | tf_op jit(solution)/shard_map/along/pallas_call | solution.py:312
  36.9 3.0 %collective-permute-start.8 = (f32[16,32,256]{2,1,0:T(8,128)S(1)}, f32[16,32,256]{2,1,0:T(8,128)S(1)}, u32[]{:S(2)}, u32[]{:S(2)}) collective-permute-start(f32[16,32,256]{2,1,0:T(8,128)S(1)} %get-tuple-element.68), channel_id=1, source_target_pairs={{0,64},{16,80},{32,96},{48,112},{64,0},{80,16},{96,32},{112,48},{1... | collective-permute-start | bytes 1572872 | tf_op jit(solution)/shard_map/ppermute | solution.py:472
  39.9 0.4 collective-permute-start.9
  40.3 2.3 %collective-permute-start.10 = (f32[16,32,256]{2,1,0:T(8,128)S(1)}, f32[16,32,256]{2,1,0:T(8,128)S(1)}, u32[]{:S(2)}, u32[]{:S(2)}) collective-permute-start(f32[16,32,256]{2,1,0:T(8,128)S(1)} %get-tuple-element.70), channel_id=1, source_target_pairs={{0,96},{16,112},{32,0},{48,16},{64,32},{80,48},{96,64},{112,80},{1... | collective-permute-start | bytes 1572872 | tf_op jit(solution)/shard_map/ppermute | solution.py:472
  42.6 6.8 %own.1 = (f32[2,130,48,128]{3,2,1,0:T(8,128)S(1)}, f32[2,128,32,128]{3,2,1,0:T(8,128)S(1)}, f32[2,130,48,128]{3,2,1,0:T(8,128)S(1)}, f32[128,256]{1,0:T(8,128)S(...) custom-call(s32[1]{0:T(128)S(6)} %copy.43.refs_0_, ...), custom_call_target="tpu_custom_call", output_to_operand_aliasing={{0}: (9, {}), {1}: (10, {}), {2}: (11, {}), {3}: (12, {}), ... | custom-call | flops 15728640 | bytes 3932160 | tf_op jit(solution)/shard_map/own/pallas_call | solution.py:312
  49.3 3.8 %collective-permute-start.6 = (f32[32,128]{1,0:T(8,128)S(1)}, f32[32,128]{1,0:T(8,128)S(1)}, u32[]{:S(2)}, u32[]{:S(2)}) collective-permute-start(f32[32,128]{1,0:T(8,128)S(1)} %get-tuple-element.64), channel_id=1, source_target_pairs={{0,1},{1,2},{2,3},{4,5},{5,6},{6,7},{8,9},{9,10},{10,11},{12,13},{... | collective-permute-start | bytes 49160 | tf_op jit(solution)/shard_map/ppermute | solution.py:438
  53.1 0.9 collective-permute-done.6.refs_4_.z_low
  54.0 1.3 %collective-permute-start.7 = (f32[32,128]{1,0:T(8,128)S(1)}, f32[32,128]{1,0:T(8,128)S(1)}, u32[]{:S(2)}, u32[]{:S(2)}) collective-permute-start(f32[32,128]{1,0:T(8,128)S(1)} %get-tuple-element.65), channel_id=1, source_target_pairs={{1,0},{2,1},{3,2},{5,4},{6,5},{7,6},{9,8},{10,9},{11,10},{13,12},{... | collective-permute-start | bytes 49160 | tf_op jit(solution)/shard_map/ppermute | solution.py:438
  55.3 4.0 %collective-permute-done.7.refs_5_.z_high = f32[32,128]{1,0:T(8,128)S(1)} collective-permute-done((f32[32,128]{1,0:T(8,128)S(1)}, f32[32,128]{1,0:T(8,128)S(1)}, u32[]{:S(2)}, u32[]{:S(2)}) %collective-permute-start.7) | collective-permute-done | bytes 16416 | tf_op jit(solution)/shard_map/ppermute | solution.py:438
  59.3 6.3 %collective-permute-start.4 = (f32[128,256]{1,0:T(8,128)S(1)}, f32[128,256]{1,0:T(8,128)S(1)}, u32[]{:S(2)}, u32[]{:S(2)}) collective-permute-start(f32[128,256]{1,0:T(8,128)S(1)} %get-tuple-element.62), channel_id=1, source_target_pairs={{0,4},{4,8},{8,12},{1,5},{5,9},{9,13},{2,6},{6,10},{10,14},{3,7},{... | collective-permute-start | bytes 393224 | tf_op jit(solution)/shard_map/ppermute | solution.py:438
  65.6 1.9 %collective-permute-done.4.refs_2_.y_low = f32[128,256]{1,0:T(8,128)S(1)} collective-permute-done((f32[128,256]{1,0:T(8,128)S(1)}, f32[128,256]{1,0:T(8,128)S(1)}, u32[]{:S(2)}, u32[]{:S(2)}) %collective-permute-start.4) | collective-permute-done | bytes 131104 | tf_op jit(solution)/shard_map/ppermute | solution.py:438
  67.6 1.9 %collective-permute-start.5 = (f32[128,256]{1,0:T(8,128)S(1)}, f32[128,256]{1,0:T(8,128)S(1)}, u32[]{:S(2)}, u32[]{:S(2)}) collective-permute-start(f32[128,256]{1,0:T(8,128)S(1)} %get-tuple-element.63), channel_id=1, source_target_pairs={{4,0},{8,4},{12,8},{5,1},{9,5},{13,9},{6,2},{10,6},{14,10},{7,3},{... | collective-permute-start | bytes 393224 | tf_op jit(solution)/shard_map/ppermute | solution.py:438
  69.5 5.1 %collective-permute-done.5.refs_3_.y_high = f32[128,256]{1,0:T(8,128)S(1)} collective-permute-done((f32[128,256]{1,0:T(8,128)S(1)}, f32[128,256]{1,0:T(8,128)S(1)}, u32[]{:S(2)}, u32[]{:S(2)}) %collective-permute-start.5) | collective-permute-done | bytes 131104 | tf_op jit(solution)/shard_map/ppermute | solution.py:438
  74.6 0.0 collective-permute-done.11.refs_1_
  74.6 0.1 add_q.1
  74.7 0.1 collective-permute-start.13
  74.8 0.0 collective-permute-done.8.refs_1_
  74.8 0.0 collective-permute-done.9.refs_2_
  74.8 0.0 collective-permute-done.10.refs_3_
  74.8 0.1 add_p.1
  74.9 1.0 %collective-permute-start.12 = (f32[8,32,256]{2,1,0:T(8,128)S(1)}, f32[8,32,256]{2,1,0:T(8,128)S(1)}, u32[]{:S(2)}, u32[]{:S(2)}) collective-permute-start(f32[8,32,256]{2,1,0:T(8,128)S(1)} %get-tuple-element.76), channel_id=1, source_target_pairs={{0,16},{16,0},{32,48},{48,32},{64,80},{80,64},{96,112},{112,96},{1... | collective-permute-start | bytes 786440 | tf_op jit(solution)/shard_map/ppermute | solution.py:472
  75.9 0.3 collective-permute-start.14
  76.2 2.4 %collective-permute-start.15 = (f32[8,32,256]{2,1,0:T(8,128)S(1)}, f32[8,32,256]{2,1,0:T(8,128)S(1)}, u32[]{:S(2)}, u32[]{:S(2)}) collective-permute-start(f32[8,32,256]{2,1,0:T(8,128)S(1)} %get-tuple-element.79), channel_id=1, source_target_pairs={{0,96},{16,112},{32,0},{48,16},{64,32},{80,48},{96,64},{112,80},{1... | collective-permute-start | bytes 786440 | tf_op jit(solution)/shard_map/ppermute | solution.py:472
  78.6 8.1 %last_step.1 = (f32[128,32,256]{2,1,0:T(8,128)}, f32[2,130,48,128]{3,2,1,0:T(8,128)S(1)}) custom-call(bf16[256,32,256]{2,1,0:T(8,128)(2,1)} %bitcast.7, bf16[256,32,256]{2,1,0:T(8,128)(2,1)} %bitcast.11, f32[2,128,32,128]{3,2,1,0:T(8,128)S(1)} %get-tuple-element.61.kept, ...), custom_call_target="tpu_custom_call", output_to_operand_aliasing={{1}: (7, {})} | custom-call | flops 20971520 | bytes 8388608 | tf_op jit(solution)/shard_map/last_step/pallas_call | solution.py:382
  86.7 0.0 collective-permute-done.12
  86.7 0.0 collective-permute-done.13
  86.7 0.0 collective-permute-done.14
  86.7 0.0 collective-permute-done.15
  86.7 0.1 add_add_fusion
  86.8 0.8 pad_maximum_fusion
  (1 shorter events, 0.0 us)
Async XLA Ops:
  7.1 14.7 %collective-permute-start = (f32[2,128,256]{2,1,0:T(8,128)S(1)}, f32[2,128,256]{2,1,0:T(8,128)S(1)}, u32[]{:S(2)}, u32[]{:S(2)}) collective-permute-start(f32[2,128,256]{2,1,0:T(8,128)S(1)} %get-tuple-element.41), channel_id=1, source_target_pairs={{0,4},{4,8},{8,12},{1,5},{5,9},{9,13},{2,6},{6,10},{10,14},{3,7},{... | collective-permute-start | bytes 786440 | tf_op jit(solution)/shard_map/ppermute | solution.py:438
  12.0 9.7 %collective-permute-start.1 = (f32[2,128,256]{2,1,0:T(8,128)S(1)}, f32[2,128,256]{2,1,0:T(8,128)S(1)}, u32[]{:S(2)}, u32[]{:S(2)}) collective-permute-start(f32[2,128,256]{2,1,0:T(8,128)S(1)} %get-tuple-element.42), channel_id=1, source_target_pairs={{4,0},{8,4},{12,8},{5,1},{9,5},{13,9},{6,2},{10,6},{14,10},{7,3},{... | collective-permute-start | bytes 786440 | tf_op jit(solution)/shard_map/ppermute | solution.py:438
  14.0 7.5 %collective-permute-start.2 = (f32[64,128]{1,0:T(8,128)S(1)}, f32[64,128]{1,0:T(8,128)S(1)}, u32[]{:S(2)}, u32[]{:S(2)}) collective-permute-start(f32[64,128]{1,0:T(8,128)S(1)} %get-tuple-element.43), channel_id=1, source_target_pairs={{0,1},{1,2},{2,3},{4,5},{5,6},{6,7},{8,9},{9,10},{10,11},{12,13},{... | collective-permute-start | bytes 98312 | tf_op jit(solution)/shard_map/ppermute | solution.py:438
  17.1 4.7 %collective-permute-start.3 = (f32[64,128]{1,0:T(8,128)S(1)}, f32[64,128]{1,0:T(8,128)S(1)}, u32[]{:S(2)}, u32[]{:S(2)}) collective-permute-start(f32[64,128]{1,0:T(8,128)S(1)} %get-tuple-element.44), channel_id=1, source_target_pairs={{1,0},{2,1},{3,2},{5,4},{6,5},{7,6},{9,8},{10,9},{11,10},{13,12},{... | collective-permute-start | bytes 98312 | tf_op jit(solution)/shard_map/ppermute | solution.py:438
  19.0 2.7 %copy-start = (f32[8]{0:T(128)S(1)}, f32[8]{0:T(128)}, u32[]{:S(2)}) copy-start(f32[8]{0:T(128)} %refs_1_.5) | copy-start | bytes 100
  26.8 47.8 %collective-permute-start.11 = (f32[32,32,256]{2,1,0:T(8,128)S(1)}, f32[32,32,256]{2,1,0:T(8,128)S(1)}, u32[]{:S(2)}, u32[]{:S(2)}) collective-permute-start(f32[32,32,256]{2,1,0:T(8,128)S(1)} %get-tuple-element.72), channel_id=1, source_target_pairs={{0,16},{16,0},{32,48},{48,32},{64,80},{80,64},{96,112},{112,96},{1... | collective-permute-start | bytes 3145736 | tf_op jit(solution)/shard_map/ppermute | solution.py:472
  36.9 37.9 %collective-permute-start.8 = (f32[16,32,256]{2,1,0:T(8,128)S(1)}, f32[16,32,256]{2,1,0:T(8,128)S(1)}, u32[]{:S(2)}, u32[]{:S(2)}) collective-permute-start(f32[16,32,256]{2,1,0:T(8,128)S(1)} %get-tuple-element.68), channel_id=1, source_target_pairs={{0,64},{16,80},{32,96},{48,112},{64,0},{80,16},{96,32},{112,48},{1... | collective-permute-start | bytes 1572872 | tf_op jit(solution)/shard_map/ppermute | solution.py:472
  39.9 34.9 %collective-permute-start.9 = (f32[16,32,256]{2,1,0:T(8,128)S(1)}, f32[16,32,256]{2,1,0:T(8,128)S(1)}, u32[]{:S(2)}, u32[]{:S(2)}) collective-permute-start(f32[16,32,256]{2,1,0:T(8,128)S(1)} %get-tuple-element.69), channel_id=1, source_target_pairs={{0,32},{16,48},{32,64},{48,80},{64,96},{80,112},{96,0},{112,16},{1... | collective-permute-start | bytes 1572872 | tf_op jit(solution)/shard_map/ppermute | solution.py:472
  40.3 34.5 %collective-permute-start.10 = (f32[16,32,256]{2,1,0:T(8,128)S(1)}, f32[16,32,256]{2,1,0:T(8,128)S(1)}, u32[]{:S(2)}, u32[]{:S(2)}) collective-permute-start(f32[16,32,256]{2,1,0:T(8,128)S(1)} %get-tuple-element.70), channel_id=1, source_target_pairs={{0,96},{16,112},{32,0},{48,16},{64,32},{80,48},{96,64},{112,80},{1... | collective-permute-start | bytes 1572872 | tf_op jit(solution)/shard_map/ppermute | solution.py:472
  49.3 4.6 %collective-permute-start.6 = (f32[32,128]{1,0:T(8,128)S(1)}, f32[32,128]{1,0:T(8,128)S(1)}, u32[]{:S(2)}, u32[]{:S(2)}) collective-permute-start(f32[32,128]{1,0:T(8,128)S(1)} %get-tuple-element.64), channel_id=1, source_target_pairs={{0,1},{1,2},{2,3},{4,5},{5,6},{6,7},{8,9},{9,10},{10,11},{12,13},{... | collective-permute-start | bytes 49160 | tf_op jit(solution)/shard_map/ppermute | solution.py:438
  54.0 5.3 %collective-permute-start.7 = (f32[32,128]{1,0:T(8,128)S(1)}, f32[32,128]{1,0:T(8,128)S(1)}, u32[]{:S(2)}, u32[]{:S(2)}) collective-permute-start(f32[32,128]{1,0:T(8,128)S(1)} %get-tuple-element.65), channel_id=1, source_target_pairs={{1,0},{2,1},{3,2},{5,4},{6,5},{7,6},{9,8},{10,9},{11,10},{13,12},{... | collective-permute-start | bytes 49160 | tf_op jit(solution)/shard_map/ppermute | solution.py:438
  59.3 8.3 %collective-permute-start.4 = (f32[128,256]{1,0:T(8,128)S(1)}, f32[128,256]{1,0:T(8,128)S(1)}, u32[]{:S(2)}, u32[]{:S(2)}) collective-permute-start(f32[128,256]{1,0:T(8,128)S(1)} %get-tuple-element.62), channel_id=1, source_target_pairs={{0,4},{4,8},{8,12},{1,5},{5,9},{9,13},{2,6},{6,10},{10,14},{3,7},{... | collective-permute-start | bytes 393224 | tf_op jit(solution)/shard_map/ppermute | solution.py:438
  67.6 7.0 %collective-permute-start.5 = (f32[128,256]{1,0:T(8,128)S(1)}, f32[128,256]{1,0:T(8,128)S(1)}, u32[]{:S(2)}, u32[]{:S(2)}) collective-permute-start(f32[128,256]{1,0:T(8,128)S(1)} %get-tuple-element.63), channel_id=1, source_target_pairs={{4,0},{8,4},{12,8},{5,1},{9,5},{13,9},{6,2},{10,6},{14,10},{7,3},{... | collective-permute-start | bytes 393224 | tf_op jit(solution)/shard_map/ppermute | solution.py:438
  74.7 12.0 %collective-permute-start.13 = (f32[8,32,256]{2,1,0:T(8,128)S(1)}, f32[8,32,256]{2,1,0:T(8,128)S(1)}, u32[]{:S(2)}, u32[]{:S(2)}) collective-permute-start(f32[8,32,256]{2,1,0:T(8,128)S(1)} %get-tuple-element.77), channel_id=1, source_target_pairs={{0,64},{16,80},{32,96},{48,112},{64,0},{80,16},{96,32},{112,48},{1... | collective-permute-start | bytes 786440 | tf_op jit(solution)/shard_map/ppermute | solution.py:472
  74.9 11.7 %collective-permute-start.12 = (f32[8,32,256]{2,1,0:T(8,128)S(1)}, f32[8,32,256]{2,1,0:T(8,128)S(1)}, u32[]{:S(2)}, u32[]{:S(2)}) collective-permute-start(f32[8,32,256]{2,1,0:T(8,128)S(1)} %get-tuple-element.76), channel_id=1, source_target_pairs={{0,16},{16,0},{32,48},{48,32},{64,80},{80,64},{96,112},{112,96},{1... | collective-permute-start | bytes 786440 | tf_op jit(solution)/shard_map/ppermute | solution.py:472
  75.9 10.8 %collective-permute-start.14 = (f32[8,32,256]{2,1,0:T(8,128)S(1)}, f32[8,32,256]{2,1,0:T(8,128)S(1)}, u32[]{:S(2)}, u32[]{:S(2)}) collective-permute-start(f32[8,32,256]{2,1,0:T(8,128)S(1)} %get-tuple-element.78), channel_id=1, source_target_pairs={{0,32},{16,48},{32,64},{48,80},{64,96},{80,112},{96,0},{112,16},{1... | collective-permute-start | bytes 786440 | tf_op jit(solution)/shard_map/ppermute | solution.py:472
  76.2 10.6 %collective-permute-start.15 = (f32[8,32,256]{2,1,0:T(8,128)S(1)}, f32[8,32,256]{2,1,0:T(8,128)S(1)}, u32[]{:S(2)}, u32[]{:S(2)}) collective-permute-start(f32[8,32,256]{2,1,0:T(8,128)S(1)} %get-tuple-element.79), channel_id=1, source_target_pairs={{0,96},{16,112},{32,0},{48,16},{64,32},{80,48},{96,64},{112,80},{1... | collective-permute-start | bytes 786440 | tf_op jit(solution)/shard_map/ppermute | solution.py:472

commit v4 on v3

--- a/solution.py
+++ b/solution.py
@@ -429,6 +429,32 @@
     )(*parts, *after)
 
 
+def join_kernel(unroll, low, high, low_got, high_got, low_out, high_out):
+    planes = low_got.shape[0]
+
+    def body(i, carry):
+        return carry, [
+            (out, (((part + turned) % 2) * planes + i,), base[planes + i] if part else base[i] + got[i])
+            for base, got, out, turned in ((low, low_got, low_out, 0), (high, high_got, high_out, 1))
+            for part in (0, 1)
+        ]
+
+    over(planes, unroll, body)
+
+
+def join(low, high, low_got, high_got, unroll=2):
+    size = low.size
+    return pl.pallas_call(
+        functools.partial(join_kernel, unroll),
+        in_specs=[VMEM] * 4,
+        out_specs=[VMEM] * 2,
+        out_shape=[jax.ShapeDtypeStruct(low.shape, F32)] * 2,
+        compiler_params=pltpu.CompilerParams(vmem_limit_bytes=VMEM_LIMIT),
+        cost_estimate=pl.CostEstimate(flops=size, bytes_accessed=4 * size, transcendentals=0),
+        name="join",
+    )(low, high, low_got, high_got)
+
+
 def exchange(y_low, y_high, z_low, z_high):
     received = []
     for axis, low, high in (("gy", y_low, y_high), ("gz", z_low, z_high)):
@@ -450,9 +476,10 @@
 
 def orders(ring):
     cross = [(turn, 1, 1) for turn in range(ring)]
-    along = [(turn, swap, 0) for turn in (2, 1, 3) for swap in (1, 0)]
+    far = [(2, 1, 0), (2, 0, 0)]
+    near = [(1, 1, 0), (1, 0, 0), (3, 0, 0), (3, 1, 0)]
     own = [(0, 1, 0), (0, 0, 0)] + [(turn, 0, 1) for turn in range(ring)]
-    return cross, along, own
+    return cross, far, near, own
 
 
 def shards(ring, adjoint_final, concentration, observed, capacity, pore_mask, feed_index, feed_affinity):
@@ -480,14 +507,19 @@
     state = (masked, weigh(wide))
     state, (cross,) = stage(scalars, fields, halo, state, at[0], (4,), planes, UNROLL, "cross")
     crossed = send(cross, 0, 1)
-    state, along = stage(scalars, fields, halo, state, at[1], (2, 2, 2), planes, UNROLL, "along")
-    parts_p = [send(value, turn, 0) for value, turn in zip(along, (2, 1, 3))]
-    (_, kept, next_adjoint, *next_faces), (own_p, own_q) = stage(scalars, fields, halo, state, at[2], (2, 4), planes, UNROLL, "own")
+    state, (far_s, far_k) = stage(scalars, fields, halo, state, at[1], (1, 1), planes, UNROLL, "far")
+    got_s, got_k = send(far_s, 1, 0), send(far_k, 3, 0)
+    state, (up, down) = stage(scalars, fields, halo, state, at[2], (2, 2), planes, UNROLL, "near")
+    up, down = join(up, down, got_s, got_k)
+    from_low, from_high = send(up, 1, 0), send(down, 3, 0)
+    (_, kept, next_adjoint, *next_faces), (own_p, own_q) = stage(
+        scalars, fields, halo, state, at[3], (2, 4), planes, UNROLL, "own"
+    )
     face_halo = exchange(*next_faces)
 
     totals_q = add([own_q, crossed], face_halo, ring, "add_q")
     parts_q = [send(totals_q[turn], turn, 0) for turn in (2, 1, 3)]
-    total_s, total_k = add([own_p, *parts_p], totals_q[:1], 2, "add_p")
+    total_s, total_k = add([own_p, from_low, from_high], totals_q[:1], 2, "add_p")
     last_p = send(total_s, 0, 1)
     adjoint_first = last_step(next_adjoint, kept, filled, seen, face_halo, total_k)
 

time: 88.5 us -> 83.8 us (0.947)
  waiting for transfers between devices: 12.1 us -> 6.1 us
  Pallas kernels: 35.7 us -> 37.2 us
    ppermute x8, waiting for transfers between devices: 12.1 us -> 3.72 us  [exchange(): received += [lax.ppermute(high, axis, up), lax.ppermute(low, axis, down)]]
    ppermute x8 -> x9, waiting for transfers between devices: 0.02 us -> 2.38 us  [send(): return lax.ppermute(value, 'exp', perm)]
    pallas_call x3 -> x4, Pallas kernels: 18.5 us -> 19.9 us  [stage(): pl.pallas_call(functools.partial(stage_kernel, places, counts, planes, un...]
    ppermute x8, starting transfers between devices: 24.6 us -> 23.3 us  [exchange(): received += [lax.ppermute(high, axis, up), lax.ppermute(low, axis, down)]]
    ppermute x8 -> x9, starting transfers between devices: 12.8 us -> 14 us  [send(): return lax.ppermute(value, 'exp', perm)]
  transfers between devices with their start and end apart: 16 -> 17, of which waited for: 5 -> 4; matrix products, arithmetic and copies ran while one was open for 0% -> 0% of each run, Pallas kernels for 28% -> 31%
where the time goes in v4:
time: 83.8 us; the launch traced here: 83 us
  starting transfers between devices  37.3 us (45%)
  Pallas kernels  37.2 us (44%)
  waiting for transfers between devices  6.1 us (7%)
  between operations  1.5 us (2%)
  other arithmetic  0.94 us (1%)
    ppermute x8, starting transfers between devices, exchange(): received += [lax.ppermute(high, axis, up), lax.ppermute(low, axis, down)]  23.3 us
    pallas_call x4, Pallas kernels, stage(): pl.pallas_call(functools.partial(stage_kernel, places, counts, planes, un...  19.9 us
    ppermute x9, starting transfers between devices, send(): return lax.ppermute(value, 'exp', perm)  14 us
    pallas_call x1, Pallas kernels, last_step(): pl.pallas_call(functools.partial(last_kernel, planes, unroll), in_specs=[...  8.08 us
    pallas_call x1, Pallas kernels, faces(): pl.pallas_call(functools.partial(faces_kernel, planes, unroll), in_specs=...  6.45 us
    ppermute x8, waiting for transfers between devices, exchange(): received += [lax.ppermute(high, axis, up), lax.ppermute(low, axis, down)]  3.72 us
    pallas_call x1, Pallas kernels, weigh(): pl.pallas_call(functools.partial(weigh_kernel, unroll), in_specs=[VMEM],...  2.45 us
    ppermute x9, waiting for transfers between devices, send(): return lax.ppermute(value, 'exp', perm)  2.38 us
  transfers between devices with their start and end apart: 17, of which 4 were waited for; matrix products, arithmetic and copies ran while one was open for 0% of the time, Pallas kernels for 31%

profile of v4, /device:TPU:1, one launch (start us, length us, event | category | flops | bytes accessed | tf_op | source)
XLA Modules:
  0.0 83.0 jit_solution(10189949678574292549)
XLA Ops:
  0.6 6.5 %faces.1 = (f32[2,130,48,128]{3,2,1,0:T(8,128)S(1)}, f32[2,130,48,128]{3,2,1,0:T(8,128)S(1)}, f32[2,128,256]{2,1,0:T(8,128)S(1)}, f32[2,128,256]{2,1,0:T(8,128)S...) custom-call(f32[128,32,256]{2,1,0:T(8,128)} %bitcast.14, s32[128,32,256]{2,1,0:T(8,128)} %pore_hbm.1), custom_call_target="tpu_custom_call" | custom-call | flops 4194304 | bytes 8388608 | tf_op jit(solution)/shard_map/faces/pallas_call | solution.py:163
  7.1 0.0 copy-start
  7.1 4.9 %collective-permute-start = (f32[2,128,256]{2,1,0:T(8,128)S(1)}, f32[2,128,256]{2,1,0:T(8,128)S(1)}, u32[]{:S(2)}, u32[]{:S(2)}) collective-permute-start(f32[2,128,256]{2,1,0:T(8,128)S(1)} %get-tuple-element.51), channel_id=1, source_target_pairs={{0,4},{4,8},{8,12},{1,5},{5,9},{9,13},{2,6},{6,10},{10,14},{3,7},{... | collective-permute-start | bytes 786440 | tf_op jit(solution)/shard_map/ppermute | solution.py:464
  12.0 1.9 %collective-permute-start.1 = (f32[2,128,256]{2,1,0:T(8,128)S(1)}, f32[2,128,256]{2,1,0:T(8,128)S(1)}, u32[]{:S(2)}, u32[]{:S(2)}) collective-permute-start(f32[2,128,256]{2,1,0:T(8,128)S(1)} %get-tuple-element.52), channel_id=1, source_target_pairs={{4,0},{8,4},{12,8},{5,1},{9,5},{13,9},{6,2},{10,6},{14,10},{7,3},{... | collective-permute-start | bytes 786440 | tf_op jit(solution)/shard_map/ppermute | solution.py:464
  14.0 3.1 %collective-permute-start.2 = (f32[64,128]{1,0:T(8,128)S(1)}, f32[64,128]{1,0:T(8,128)S(1)}, u32[]{:S(2)}, u32[]{:S(2)}) collective-permute-start(f32[64,128]{1,0:T(8,128)S(1)} %get-tuple-element.53), channel_id=1, source_target_pairs={{0,1},{1,2},{2,3},{4,5},{5,6},{6,7},{8,9},{9,10},{10,11},{12,13},{... | collective-permute-start | bytes 98312 | tf_op jit(solution)/shard_map/ppermute | solution.py:464
  17.1 1.3 %collective-permute-start.3 = (f32[64,128]{1,0:T(8,128)S(1)}, f32[64,128]{1,0:T(8,128)S(1)}, u32[]{:S(2)}, u32[]{:S(2)}) collective-permute-start(f32[64,128]{1,0:T(8,128)S(1)} %get-tuple-element.54), channel_id=1, source_target_pairs={{1,0},{2,1},{3,2},{5,4},{6,5},{7,6},{9,8},{10,9},{11,10},{13,12},{... | collective-permute-start | bytes 98312 | tf_op jit(solution)/shard_map/ppermute | solution.py:464
  19.0 2.4 %weigh.1.refs_10_ = f32[2,128,32,128]{3,2,1,0:T(8,128)S(1)} custom-call(f32[2,130,48,128]{3,2,1,0:T(8,128)S(1)} %get-tuple-element.56.wide), custom_call_target="tpu_custom_call" | custom-call | flops 12582912 | bytes 12582912 | tf_op jit(solution)/shard_map/weigh/pallas_call | solution.py:198
  21.5 0.0 collective-permute-done.2.refs_7_
  21.5 0.2 collective-permute-done.3.refs_8_
  21.8 0.0 collective-permute-done.refs_5_
  21.8 0.0 collective-permute-done.1.refs_6_
  21.8 0.0 copy-done
  21.8 5.0 %cross.1 = (f32[2,130,48,128]{3,2,1,0:T(8,128)S(1)}, f32[2,128,32,128]{3,2,1,0:T(8,128)S(1)}, f32[2,130,48,128]{3,2,1,0:T(8,128)S(1)}, f32[128,256]{1,0:T(8,128)...) custom-call(s32[1]{0:T(128)S(6)} %copy.57.refs_0_, ...), custom_call_target="tpu_custom_call", output_to_operand_aliasing={{0}: (9, {}), {1}: (10, {})} | custom-call | flops 10485760 | bytes 2621440 | tf_op jit(solution)/shard_map/cross/pallas_call | solution.py:312
  26.8 3.4 %collective-permute-start.12 = (f32[32,32,256]{2,1,0:T(8,128)S(1)}, f32[32,32,256]{2,1,0:T(8,128)S(1)}, u32[]{:S(2)}, u32[]{:S(2)}) collective-permute-start(f32[32,32,256]{2,1,0:T(8,128)S(1)} %get-tuple-element.92), channel_id=1, source_target_pairs={{0,16},{16,0},{32,48},{48,32},{64,80},{80,64},{96,112},{112,96},{1... | collective-permute-start | bytes 3145736 | tf_op jit(solution)/shard_map/ppermute | solution.py:499
  30.2 3.2 %far.1 = (f32[2,130,48,128]{3,2,1,0:T(8,128)S(1)}, f32[2,128,32,128]{3,2,1,0:T(8,128)S(1)}, f32[2,130,48,128]{3,2,1,0:T(8,128)S(1)}, f32[128,256]{1,0:T(8,128)S(...) custom-call(s32[1]{0:T(128)S(6)} %copy.57.refs_0_, ...), custom_call_target="tpu_custom_call", output_to_operand_aliasing={{0}: (9, {}), {1}: (10, {}), {2}: (11, {}), {3}: (12, {}), ... | custom-call | flops 5242880 | bytes 1310720 | tf_op jit(solution)/shard_map/far/pallas_call | solution.py:312
  33.4 1.4 %collective-permute-start.8 = (f32[8,32,256]{2,1,0:T(8,128)S(1)}, f32[8,32,256]{2,1,0:T(8,128)S(1)}, u32[]{:S(2)}, u32[]{:S(2)}) collective-permute-start(f32[8,32,256]{2,1,0:T(8,128)S(1)} %get-tuple-element.87), channel_id=1, source_target_pairs={{0,32},{16,48},{32,64},{48,80},{64,96},{80,112},{96,0},{112,16},{1... | collective-permute-start | bytes 786440 | tf_op jit(solution)/shard_map/ppermute | solution.py:499
  34.7 1.5 %collective-permute-start.9 = (f32[8,32,256]{2,1,0:T(8,128)S(1)}, f32[8,32,256]{2,1,0:T(8,128)S(1)}, u32[]{:S(2)}, u32[]{:S(2)}) collective-permute-start(f32[8,32,256]{2,1,0:T(8,128)S(1)} %get-tuple-element.88), channel_id=1, source_target_pairs={{0,96},{16,112},{32,0},{48,16},{64,32},{80,48},{96,64},{112,80},{1... | collective-permute-start | bytes 786440 | tf_op jit(solution)/shard_map/ppermute | solution.py:499
  36.3 5.0 %near.1 = (f32[2,130,48,128]{3,2,1,0:T(8,128)S(1)}, f32[2,128,32,128]{3,2,1,0:T(8,128)S(1)}, f32[2,130,48,128]{3,2,1,0:T(8,128)S(1)}, f32[128,256]{1,0:T(8,128)S...) custom-call(s32[1]{0:T(128)S(6)} %copy.57.refs_0_, ...), custom_call_target="tpu_custom_call", output_to_operand_aliasing={{0}: (9, {}), {1}: (10, {}), {2}: (11, {}), {3}: (12, {}), ... | custom-call | flops 10485760 | bytes 2621440 | tf_op jit(solution)/shard_map/near/pallas_call | solution.py:312
  41.2 1.7 %collective-permute-done.8.low_got = f32[8,32,256]{2,1,0:T(8,128)S(1)} collective-permute-done((f32[8,32,256]{2,1,0:T(8,128)S(1)}, f32[8,32,256]{2,1,0:T(8,128)S(1)}, u32[]{:S(2)}, u32[]{:S(2)}) %collective-permute-start.8) | collective-permute-done | bytes 262176 | tf_op jit(solution)/shard_map/ppermute | solution.py:499
  42.9 0.0 collective-permute-done.9.high_got
  42.9 0.1 join.1
  43.0 1.1 %collective-permute-start.10 = (f32[16,32,256]{2,1,0:T(8,128)S(1)}, f32[16,32,256]{2,1,0:T(8,128)S(1)}, u32[]{:S(2)}, u32[]{:S(2)}) collective-permute-start(f32[16,32,256]{2,1,0:T(8,128)S(1)} %get-tuple-element.89), channel_id=1, source_target_pairs={{0,32},{16,48},{32,64},{48,80},{64,96},{80,112},{96,0},{112,16},{1... | collective-permute-start | bytes 1572872 | tf_op jit(solution)/shard_map/ppermute | solution.py:499
  44.2 1.8 %collective-permute-start.11 = (f32[16,32,256]{2,1,0:T(8,128)S(1)}, f32[16,32,256]{2,1,0:T(8,128)S(1)}, u32[]{:S(2)}, u32[]{:S(2)}) collective-permute-start(f32[16,32,256]{2,1,0:T(8,128)S(1)} %get-tuple-element.90), channel_id=1, source_target_pairs={{0,96},{16,112},{32,0},{48,16},{64,32},{80,48},{96,64},{112,80},{1... | collective-permute-start | bytes 1572872 | tf_op jit(solution)/shard_map/ppermute | solution.py:499
  45.9 6.8 %own.1 = (f32[2,130,48,128]{3,2,1,0:T(8,128)S(1)}, f32[2,128,32,128]{3,2,1,0:T(8,128)S(1)}, f32[2,130,48,128]{3,2,1,0:T(8,128)S(1)}, f32[128,256]{1,0:T(8,128)S(...) custom-call(s32[1]{0:T(128)S(6)} %copy.57.refs_0_, ...), custom_call_target="tpu_custom_call", output_to_operand_aliasing={{0}: (9, {}), {1}: (10, {}), {2}: (11, {}), {3}: (12, {}), ... | custom-call | flops 15728640 | bytes 3932160 | tf_op jit(solution)/shard_map/own/pallas_call | solution.py:312
  52.7 3.7 %collective-permute-start.6 = (f32[32,128]{1,0:T(8,128)S(1)}, f32[32,128]{1,0:T(8,128)S(1)}, u32[]{:S(2)}, u32[]{:S(2)}) collective-permute-start(f32[32,128]{1,0:T(8,128)S(1)} %get-tuple-element.81), channel_id=1, source_target_pairs={{0,1},{1,2},{2,3},{4,5},{5,6},{6,7},{8,9},{9,10},{10,11},{12,13},{... | collective-permute-start | bytes 49160 | tf_op jit(solution)/shard_map/ppermute | solution.py:464
  56.4 1.3 %collective-permute-start.7 = (f32[32,128]{1,0:T(8,128)S(1)}, f32[32,128]{1,0:T(8,128)S(1)}, u32[]{:S(2)}, u32[]{:S(2)}) collective-permute-start(f32[32,128]{1,0:T(8,128)S(1)} %get-tuple-element.82), channel_id=1, source_target_pairs={{1,0},{2,1},{3,2},{5,4},{6,5},{7,6},{9,8},{10,9},{11,10},{13,12},{... | collective-permute-start | bytes 49160 | tf_op jit(solution)/shard_map/ppermute | solution.py:464
  57.7 0.0 collective-permute-done.6.refs_4_.z_low
  57.7 3.7 %collective-permute-start.4 = (f32[128,256]{1,0:T(8,128)S(1)}, f32[128,256]{1,0:T(8,128)S(1)}, u32[]{:S(2)}, u32[]{:S(2)}) collective-permute-start(f32[128,256]{1,0:T(8,128)S(1)} %get-tuple-element.79), channel_id=1, source_target_pairs={{0,4},{4,8},{8,12},{1,5},{5,9},{9,13},{2,6},{6,10},{10,14},{3,7},{... | collective-permute-start | bytes 393224 | tf_op jit(solution)/shard_map/ppermute | solution.py:464
  61.4 0.0 collective-permute-done.7.refs_5_.z_high
  61.4 3.4 %collective-permute-start.5 = (f32[128,256]{1,0:T(8,128)S(1)}, f32[128,256]{1,0:T(8,128)S(1)}, u32[]{:S(2)}, u32[]{:S(2)}) collective-permute-start(f32[128,256]{1,0:T(8,128)S(1)} %get-tuple-element.80), channel_id=1, source_target_pairs={{4,0},{8,4},{12,8},{5,1},{9,5},{13,9},{6,2},{10,6},{14,10},{7,3},{... | collective-permute-start | bytes 393224 | tf_op jit(solution)/shard_map/ppermute | solution.py:464
  64.8 0.0 collective-permute-done.4.refs_2_.y_low
  64.8 3.5 %collective-permute-done.5.refs_3_.y_high = f32[128,256]{1,0:T(8,128)S(1)} collective-permute-done((f32[128,256]{1,0:T(8,128)S(1)}, f32[128,256]{1,0:T(8,128)S(1)}, u32[]{:S(2)}, u32[]{:S(2)}) %collective-permute-start.5) | collective-permute-done | bytes 131104 | tf_op jit(solution)/shard_map/ppermute | solution.py:464
  68.3 0.0 collective-permute-done.12.refs_1_
  68.3 0.1 add_q.1
  68.4 1.2 %collective-permute-start.14 = (f32[8,32,256]{2,1,0:T(8,128)S(1)}, f32[8,32,256]{2,1,0:T(8,128)S(1)}, u32[]{:S(2)}, u32[]{:S(2)}) collective-permute-start(f32[8,32,256]{2,1,0:T(8,128)S(1)} %get-tuple-element.97), channel_id=1, source_target_pairs={{0,64},{16,80},{32,96},{48,112},{64,0},{80,16},{96,32},{112,48},{1... | collective-permute-start | bytes 786440 | tf_op jit(solution)/shard_map/ppermute | solution.py:499
  69.6 0.0 collective-permute-done.10.refs_1_
  69.6 0.0 collective-permute-done.11.refs_2_
  69.6 0.1 add_p.1
  69.7 1.0 %collective-permute-start.13 = (f32[8,32,256]{2,1,0:T(8,128)S(1)}, f32[8,32,256]{2,1,0:T(8,128)S(1)}, u32[]{:S(2)}, u32[]{:S(2)}) collective-permute-start(f32[8,32,256]{2,1,0:T(8,128)S(1)} %get-tuple-element.96), channel_id=1, source_target_pairs={{0,16},{16,0},{32,48},{48,32},{64,80},{80,64},{96,112},{112,96},{1... | collective-permute-start | bytes 786440 | tf_op jit(solution)/shard_map/ppermute | solution.py:499
  70.6 0.5 collective-permute-start.15
  71.2 2.1 %collective-permute-start.16 = (f32[8,32,256]{2,1,0:T(8,128)S(1)}, f32[8,32,256]{2,1,0:T(8,128)S(1)}, u32[]{:S(2)}, u32[]{:S(2)}) collective-permute-start(f32[8,32,256]{2,1,0:T(8,128)S(1)} %get-tuple-element.99), channel_id=1, source_target_pairs={{0,96},{16,112},{32,0},{48,16},{64,32},{80,48},{96,64},{112,80},{1... | collective-permute-start | bytes 786440 | tf_op jit(solution)/shard_map/ppermute | solution.py:499
  73.3 8.1 %last_step.1 = (f32[128,32,256]{2,1,0:T(8,128)}, f32[2,130,48,128]{3,2,1,0:T(8,128)S(1)}) custom-call(bf16[256,32,256]{2,1,0:T(8,128)(2,1)} %bitcast.8, bf16[256,32,256]{2,1,0:T(8,128)(2,1)} %bitcast.13, f32[2,128,32,128]{3,2,1,0:T(8,128)S(1)} %get-tuple-element.78.kept, ...), custom_call_target="tpu_custom_call", output_to_operand_aliasing={{1}: (7, {})} | custom-call | flops 20971520 | bytes 8388608 | tf_op jit(solution)/shard_map/last_step/pallas_call | solution.py:382
  81.4 0.0 collective-permute-done.13
  81.5 0.0 collective-permute-done.14
  81.5 0.6 collective-permute-done.15
  82.1 0.0 collective-permute-done.16
  82.1 0.1 add_add_fusion
  82.2 0.8 %pad_maximum_fusion = f32[16,32,256]{2,1,0:T(8,128)} fusion(f32[8,32,256]{2,1,0:T(8,128)S(1)} %add_add_fusion, f32[8,32,256]{2,1,0:T(8,128)S(1)} %add.12), kind=kLoop, calls=%fused_computation | loop fusion | flops 131072 | bytes 1048576 | tf_op jit(solution)/shard_map/concatenate | solution.py:527
  (1 shorter events, 0.0 us)
Async XLA Ops:
  7.1 14.7 %copy-start = (f32[8]{0:T(128)S(1)}, f32[8]{0:T(128)}, u32[]{:S(2)}) copy-start(f32[8]{0:T(128)} %refs_1_.7) | copy-start | bytes 100
  7.1 14.7 %collective-permute-start = (f32[2,128,256]{2,1,0:T(8,128)S(1)}, f32[2,128,256]{2,1,0:T(8,128)S(1)}, u32[]{:S(2)}, u32[]{:S(2)}) collective-permute-start(f32[2,128,256]{2,1,0:T(8,128)S(1)} %get-tuple-element.51), channel_id=1, source_target_pairs={{0,4},{4,8},{8,12},{1,5},{5,9},{9,13},{2,6},{6,10},{10,14},{3,7},{... | collective-permute-start | bytes 786440 | tf_op jit(solution)/shard_map/ppermute | solution.py:464
  12.0 9.7 %collective-permute-start.1 = (f32[2,128,256]{2,1,0:T(8,128)S(1)}, f32[2,128,256]{2,1,0:T(8,128)S(1)}, u32[]{:S(2)}, u32[]{:S(2)}) collective-permute-start(f32[2,128,256]{2,1,0:T(8,128)S(1)} %get-tuple-element.52), channel_id=1, source_target_pairs={{4,0},{8,4},{12,8},{5,1},{9,5},{13,9},{6,2},{10,6},{14,10},{7,3},{... | collective-permute-start | bytes 786440 | tf_op jit(solution)/shard_map/ppermute | solution.py:464
  14.0 7.5 %collective-permute-start.2 = (f32[64,128]{1,0:T(8,128)S(1)}, f32[64,128]{1,0:T(8,128)S(1)}, u32[]{:S(2)}, u32[]{:S(2)}) collective-permute-start(f32[64,128]{1,0:T(8,128)S(1)} %get-tuple-element.53), channel_id=1, source_target_pairs={{0,1},{1,2},{2,3},{4,5},{5,6},{6,7},{8,9},{9,10},{10,11},{12,13},{... | collective-permute-start | bytes 98312 | tf_op jit(solution)/shard_map/ppermute | solution.py:464
  17.1 4.7 %collective-permute-start.3 = (f32[64,128]{1,0:T(8,128)S(1)}, f32[64,128]{1,0:T(8,128)S(1)}, u32[]{:S(2)}, u32[]{:S(2)}) collective-permute-start(f32[64,128]{1,0:T(8,128)S(1)} %get-tuple-element.54), channel_id=1, source_target_pairs={{1,0},{2,1},{3,2},{5,4},{6,5},{7,6},{9,8},{10,9},{11,10},{13,12},{... | collective-permute-start | bytes 98312 | tf_op jit(solution)/shard_map/ppermute | solution.py:464
  26.8 41.5 %collective-permute-start.12 = (f32[32,32,256]{2,1,0:T(8,128)S(1)}, f32[32,32,256]{2,1,0:T(8,128)S(1)}, u32[]{:S(2)}, u32[]{:S(2)}) collective-permute-start(f32[32,32,256]{2,1,0:T(8,128)S(1)} %get-tuple-element.92), channel_id=1, source_target_pairs={{0,16},{16,0},{32,48},{48,32},{64,80},{80,64},{96,112},{112,96},{1... | collective-permute-start | bytes 3145736 | tf_op jit(solution)/shard_map/ppermute | solution.py:499
  33.4 9.6 %collective-permute-start.8 = (f32[8,32,256]{2,1,0:T(8,128)S(1)}, f32[8,32,256]{2,1,0:T(8,128)S(1)}, u32[]{:S(2)}, u32[]{:S(2)}) collective-permute-start(f32[8,32,256]{2,1,0:T(8,128)S(1)} %get-tuple-element.87), channel_id=1, source_target_pairs={{0,32},{16,48},{32,64},{48,80},{64,96},{80,112},{96,0},{112,16},{1... | collective-permute-start | bytes 786440 | tf_op jit(solution)/shard_map/ppermute | solution.py:499
  34.7 8.2 %collective-permute-start.9 = (f32[8,32,256]{2,1,0:T(8,128)S(1)}, f32[8,32,256]{2,1,0:T(8,128)S(1)}, u32[]{:S(2)}, u32[]{:S(2)}) collective-permute-start(f32[8,32,256]{2,1,0:T(8,128)S(1)} %get-tuple-element.88), channel_id=1, source_target_pairs={{0,96},{16,112},{32,0},{48,16},{64,32},{80,48},{96,64},{112,80},{1... | collective-permute-start | bytes 786440 | tf_op jit(solution)/shard_map/ppermute | solution.py:499
  43.0 26.6 %collective-permute-start.10 = (f32[16,32,256]{2,1,0:T(8,128)S(1)}, f32[16,32,256]{2,1,0:T(8,128)S(1)}, u32[]{:S(2)}, u32[]{:S(2)}) collective-permute-start(f32[16,32,256]{2,1,0:T(8,128)S(1)} %get-tuple-element.89), channel_id=1, source_target_pairs={{0,32},{16,48},{32,64},{48,80},{64,96},{80,112},{96,0},{112,16},{1... | collective-permute-start | bytes 1572872 | tf_op jit(solution)/shard_map/ppermute | solution.py:499
  44.2 25.4 %collective-permute-start.11 = (f32[16,32,256]{2,1,0:T(8,128)S(1)}, f32[16,32,256]{2,1,0:T(8,128)S(1)}, u32[]{:S(2)}, u32[]{:S(2)}) collective-permute-start(f32[16,32,256]{2,1,0:T(8,128)S(1)} %get-tuple-element.90), channel_id=1, source_target_pairs={{0,96},{16,112},{32,0},{48,16},{64,32},{80,48},{96,64},{112,80},{1... | collective-permute-start | bytes 1572872 | tf_op jit(solution)/shard_map/ppermute | solution.py:499
  52.7 5.0 %collective-permute-start.6 = (f32[32,128]{1,0:T(8,128)S(1)}, f32[32,128]{1,0:T(8,128)S(1)}, u32[]{:S(2)}, u32[]{:S(2)}) collective-permute-start(f32[32,128]{1,0:T(8,128)S(1)} %get-tuple-element.81), channel_id=1, source_target_pairs={{0,1},{1,2},{2,3},{4,5},{5,6},{6,7},{8,9},{9,10},{10,11},{12,13},{... | collective-permute-start | bytes 49160 | tf_op jit(solution)/shard_map/ppermute | solution.py:464
  56.4 5.0 %collective-permute-start.7 = (f32[32,128]{1,0:T(8,128)S(1)}, f32[32,128]{1,0:T(8,128)S(1)}, u32[]{:S(2)}, u32[]{:S(2)}) collective-permute-start(f32[32,128]{1,0:T(8,128)S(1)} %get-tuple-element.82), channel_id=1, source_target_pairs={{1,0},{2,1},{3,2},{5,4},{6,5},{7,6},{9,8},{10,9},{11,10},{13,12},{... | collective-permute-start | bytes 49160 | tf_op jit(solution)/shard_map/ppermute | solution.py:464
  57.7 7.1 %collective-permute-start.4 = (f32[128,256]{1,0:T(8,128)S(1)}, f32[128,256]{1,0:T(8,128)S(1)}, u32[]{:S(2)}, u32[]{:S(2)}) collective-permute-start(f32[128,256]{1,0:T(8,128)S(1)} %get-tuple-element.79), channel_id=1, source_target_pairs={{0,4},{4,8},{8,12},{1,5},{5,9},{9,13},{2,6},{6,10},{10,14},{3,7},{... | collective-permute-start | bytes 393224 | tf_op jit(solution)/shard_map/ppermute | solution.py:464
  61.4 6.8 %collective-permute-start.5 = (f32[128,256]{1,0:T(8,128)S(1)}, f32[128,256]{1,0:T(8,128)S(1)}, u32[]{:S(2)}, u32[]{:S(2)}) collective-permute-start(f32[128,256]{1,0:T(8,128)S(1)} %get-tuple-element.80), channel_id=1, source_target_pairs={{4,0},{8,4},{12,8},{5,1},{9,5},{13,9},{6,2},{10,6},{14,10},{7,3},{... | collective-permute-start | bytes 393224 | tf_op jit(solution)/shard_map/ppermute | solution.py:464
  68.4 13.1 %collective-permute-start.14 = (f32[8,32,256]{2,1,0:T(8,128)S(1)}, f32[8,32,256]{2,1,0:T(8,128)S(1)}, u32[]{:S(2)}, u32[]{:S(2)}) collective-permute-start(f32[8,32,256]{2,1,0:T(8,128)S(1)} %get-tuple-element.97), channel_id=1, source_target_pairs={{0,64},{16,80},{32,96},{48,112},{64,0},{80,16},{96,32},{112,48},{1... | collective-permute-start | bytes 786440 | tf_op jit(solution)/shard_map/ppermute | solution.py:499
  69.7 11.7 %collective-permute-start.13 = (f32[8,32,256]{2,1,0:T(8,128)S(1)}, f32[8,32,256]{2,1,0:T(8,128)S(1)}, u32[]{:S(2)}, u32[]{:S(2)}) collective-permute-start(f32[8,32,256]{2,1,0:T(8,128)S(1)} %get-tuple-element.96), channel_id=1, source_target_pairs={{0,16},{16,0},{32,48},{48,32},{64,80},{80,64},{96,112},{112,96},{1... | collective-permute-start | bytes 786440 | tf_op jit(solution)/shard_map/ppermute | solution.py:499
  70.6 11.5 %collective-permute-start.15 = (f32[8,32,256]{2,1,0:T(8,128)S(1)}, f32[8,32,256]{2,1,0:T(8,128)S(1)}, u32[]{:S(2)}, u32[]{:S(2)}) collective-permute-start(f32[8,32,256]{2,1,0:T(8,128)S(1)} %get-tuple-element.98), channel_id=1, source_target_pairs={{0,32},{16,48},{32,64},{48,80},{64,96},{80,112},{96,0},{112,16},{1... | collective-permute-start | bytes 786440 | tf_op jit(solution)/shard_map/ppermute | solution.py:499
  71.2 10.9 %collective-permute-start.16 = (f32[8,32,256]{2,1,0:T(8,128)S(1)}, f32[8,32,256]{2,1,0:T(8,128)S(1)}, u32[]{:S(2)}, u32[]{:S(2)}) collective-permute-start(f32[8,32,256]{2,1,0:T(8,128)S(1)} %get-tuple-element.99), channel_id=1, source_target_pairs={{0,96},{16,112},{32,0},{48,16},{64,32},{80,48},{96,64},{112,80},{1... | collective-permute-start | bytes 786440 | tf_op jit(solution)/shard_map/ppermute | solution.py:499

commit v5 on v4

--- a/solution.py
+++ b/solution.py
@@ -57,13 +57,22 @@
     return (nz // LANES, nx + 2, ny + 2 * ROWS, LANES)
 
 
+def rows_of(array, x, row):
+    rows = array.shape[2]
+    return pl.ds(x * rows + row, ROWS, stride=rows)
+
+
+def flat_rows(array):
+    count, planes, rows, lanes = array.shape
+    return array.reshape(count, planes * rows, lanes)
+
+
 def halo_rows(wide, x, low, high):
     ny = wide.shape[2] - 2 * ROWS
-    stores = []
+    flat = flat_rows(wide)
     for h in range(wide.shape[0]):
-        stores.append((wide, (h, x + 1, slice(ROWS - 1, ROWS)), low[:, run(h)]))
-        stores.append((wide, (h, x + 1, slice(ROWS + ny, ROWS + ny + 1)), high[:, run(h)]))
-    return stores
+        flat[h, rows_of(wide, x + 1, ROWS - 1), :] = low[:, run(h)]
+        flat[h, rows_of(wide, x + 1, ROWS + ny), :] = high[:, run(h)]
 
 
 def face_rows(wide, x, row):
@@ -95,7 +104,7 @@
     return centre, sums
 
 
-def rotating(steps, copies, body):
+def rotating(steps, copies, body, ahead=lambda t: None):
     for copy in copies(0, 0):
         copy.start()
     for t in range(steps):
@@ -103,6 +112,7 @@
         if t + 1 < steps:
             for copy in copies(t + 1, 1 - slot):
                 copy.start()
+        ahead(t)
         for copy in copies(t, slot):
             copy.wait()
         body(t, slot)
@@ -236,23 +246,19 @@
 
     targets = [(out, k) for out, n in zip(outs, counts) for k in range(n)]
 
-    def body(t, slot):
+    def ahead(t):
         start = starts[t]
-        grad, block = targets[t]
-        m_low, p_low = z_low[:ny], 0.1 * z_low[ny:]
-        m_high, p_high = z_high[:ny], 0.1 * z_high[ny:]
-
-        def ends(i, carry):
-            x = start + i
-            row = pl.ds(x, 1)
-            stores = halo_rows(masked, x, y_low[0, row, :], y_high[0, row, :])
-            low, high = 0.1 * y_low[1, row, :], 0.1 * y_high[1, row, :]
-            for h in range(count):
-                for rows, value in ((slice(0, 1), low), (slice(ny - 1, ny), high)):
-                    stores.append((kept, (h, x, rows), kept[h, x, rows, :] - value[:, run(h)]))
-            return carry, stores
-
-        over(planes, planes, ends)
+        m_low, m_high = z_low[:ny], z_high[:ny]
+
+        flat = flat_rows(kept)
+        for at in range(0, planes, ROWS):
+            x = pl.multiple_of(start + at, ROWS)
+            halo_rows(masked, x, y_low[0, pl.ds(x, ROWS), :], y_high[0, pl.ds(x, ROWS), :])
+            for row, side in ((0, y_low), (ny - 1, y_high)):
+                taken = 0.1 * side[1, pl.ds(x, ROWS), :]
+                for h in range(count):
+                    index = rows_of(kept, x, row)
+                    flat[h, index, :] = flat[h, index, :] - taken[:, run(h)]
 
         def gather(i, carry):
             x = start + i
@@ -260,6 +266,11 @@
             return carry, [(inflow, (h, i), 0.1 * sums[h]) for h in range(count)]
 
         over(planes, unroll[0], gather)
+
+    def body(t, slot):
+        start = starts[t]
+        grad, block = targets[t]
+        p_low, p_high = 0.1 * z_low[ny:], 0.1 * z_high[ny:]
 
         def plane(i, carry):
             low, high = carry
@@ -296,7 +307,7 @@
             store_rows(out_y_low, start + at, face_rows(adj, start + at, 0))
             store_rows(out_y_high, start + at, face_rows(adj, start + at, ny - 1))
 
-    rotating(sum(counts), copies, body)
+    rotating(sum(counts), copies, body, ahead)
 
 
 def stage(scalars, fields, halo, state, places, counts, planes, unroll, name):
@@ -330,7 +341,7 @@
     return results[:7], results[7:]
 
 
-def last_kernel(planes, unroll, f_hbm, o_hbm, kept, y_low, y_high, z_low, z_high, _, _after, out_hbm, adj, filled, seen, out, sem, out_sem):
+def last_kernel(planes, unroll, f_hbm, o_hbm, kept, y_low, y_high, z_low, z_high, _, _after, out_hbm, adj, filled, seen, out, inflow, sem, out_sem):
     count, nx, ny, _ = kept.shape
     lane = lax.broadcasted_iota(jnp.int32, (ny, LANES), 1)
     steps = nx // planes
@@ -345,37 +356,42 @@
     def writing(t):
         return pltpu.make_async_copy(out.at[t % 2], out_hbm.at[pl.ds(t * planes, planes)], out_sem.at[t % 2])
 
+    def ahead(t):
+        for x in range(t * planes, (t + 1) * planes, ROWS):
+            halo_rows(adj, x, y_low[pl.ds(x, ROWS), :], y_high[pl.ds(x, ROWS), :])
+
+        def gather(i, carry):
+            x = t * planes + i
+            low, high = lane_to(z_low[...], x, 0), lane_to(z_high[...], x, LANES - 1)
+            _, sums = weighted(adj, x + 1, lane, low, high)
+            return carry, [(inflow, (h, i), 0.1 * sums[h]) for h in range(count)]
+
+        over(planes, planes, gather)
+
     def body(t, slot):
         if t >= 2:
             writing(t - 2).wait()
 
-        def ends(i, carry):
-            x = t * planes + i
-            row = pl.ds(x, 1)
-            return carry, halo_rows(adj, x, y_low[row, :], y_high[row, :])
-
-        over(planes, planes, ends)
-
         def plane(i, carry):
             x = t * planes + i
-            centre, sums = weighted(adj, x + 1, lane, lane_to(z_low[...], x, 0), lane_to(z_high[...], x, LANES - 1))
             stores = []
             for h in range(count):
                 weight = kept[h, x]
+                centre = adj[h, x + 1, ROWS : ROWS + ny, :]
                 source = filled[slot, i, :, run(h)].astype(F32) - seen[slot, i, :, run(h)].astype(F32)
-                value = centre[h] * weight + (0.1 * sums[h] + source)
+                value = centre * weight + (inflow[h, i] + source)
                 stores.append((out, (slot, i, slice(None), run(h)), jnp.where(weight == SOLID, 0.0, value)))
             return carry, stores
 
         over(planes, unroll, plane)
         writing(t).start()
 
-    rotating(steps, copies, body)
+    rotating(steps, copies, body, ahead)
     writing(steps - 2).wait()
     writing(steps - 1).wait()
 
 
-def last_step(adjoint, kept, filled, seen, halo, after, planes=16, unroll=16):
+def last_step(adjoint, kept, filled, seen, halo, after, planes=16, unroll=8):
     count, nx, ny, lanes = kept.shape
     nz = count * lanes
     voxels = nx * ny * nz
@@ -388,6 +404,7 @@
             pltpu.VMEM((2, planes, ny, nz), jnp.bfloat16),
             pltpu.VMEM((2, planes, ny, nz), jnp.bfloat16),
             pltpu.VMEM((2, planes, ny, nz), F32),
+            pltpu.VMEM((count, planes, ny, lanes), F32),
             pltpu.SemaphoreType.DMA((2, 2)),
             pltpu.SemaphoreType.DMA((2,)),
         ],
@@ -479,7 +496,7 @@
     far = [(2, 1, 0), (2, 0, 0)]
     near = [(1, 1, 0), (1, 0, 0), (3, 0, 0), (3, 1, 0)]
     own = [(0, 1, 0), (0, 0, 0)] + [(turn, 0, 1) for turn in range(ring)]
-    return cross, far, near, own
+    return cross + far, near + own
 
 
 def shards(ring, adjoint_final, concentration, observed, capacity, pore_mask, feed_index, feed_affinity):
@@ -505,16 +522,14 @@
     masked, wide, *outer = faces(adjoint, pore_mask)
     halo = exchange(*outer)
     state = (masked, weigh(wide))
-    state, (cross,) = stage(scalars, fields, halo, state, at[0], (4,), planes, UNROLL, "cross")
+    state, (cross, far_s, far_k) = stage(scalars, fields, halo, state, at[0], (4, 1, 1), planes, UNROLL, "early")
     crossed = send(cross, 0, 1)
-    state, (far_s, far_k) = stage(scalars, fields, halo, state, at[1], (1, 1), planes, UNROLL, "far")
     got_s, got_k = send(far_s, 1, 0), send(far_k, 3, 0)
-    state, (up, down) = stage(scalars, fields, halo, state, at[2], (2, 2), planes, UNROLL, "near")
+    (_, kept, next_adjoint, *next_faces), (up, down, own_p, own_q) = stage(
+        scalars, fields, halo, state, at[1], (2, 2, 2, 4), planes, UNROLL, "late"
+    )
     up, down = join(up, down, got_s, got_k)
     from_low, from_high = send(up, 1, 0), send(down, 3, 0)
-    (_, kept, next_adjoint, *next_faces), (own_p, own_q) = stage(
-        scalars, fields, halo, state, at[3], (2, 4), planes, UNROLL, "own"
-    )
     face_halo = exchange(*next_faces)
 
     totals_q = add([own_q, crossed], face_halo, ring, "add_q")

time: 83.8 us -> 79.3 us (0.946)
  Pallas kernels: 37.2 us -> 33.8 us
  waiting for transfers between devices: 6.1 us -> 5.17 us
    pallas_call x4 -> x2, Pallas kernels: 19.9 us -> 16.8 us  [stage(): pl.pallas_call(functools.partial(stage_kernel, places, counts, planes, un...]
    ppermute x9, waiting for transfers between devices: 2.38 us -> 0.03 us  [send(): return lax.ppermute(value, 'exp', perm)]
    ppermute x8, waiting for transfers between devices: 3.72 us -> 5.14 us  [exchange(): received += [lax.ppermute(high, axis, up), lax.ppermute(low, axis, down)]]
    ppermute x9, starting transfers between devices: 14 us -> 13.1 us  [send(): return lax.ppermute(value, 'exp', perm)]
  transfers between devices with their start and end apart: 17 -> 17, of which waited for: 4 -> 2; matrix products, arithmetic and copies ran while one was open for 0% -> 0% of each run, Pallas kernels for 31% -> 26%
where the time goes in v5:
time: 79.3 us; the launch traced here: 78.2 us
  starting transfers between devices  36.8 us (46%)
  Pallas kernels  33.8 us (43%)
  waiting for transfers between devices  5.17 us (7%)
  between operations  1.51 us (2%)
  other arithmetic  0.94 us (1%)
    ppermute x8, starting transfers between devices, exchange(): received += [lax.ppermute(high, axis, up), lax.ppermute(low, axis, down)]  23.8 us
    pallas_call x2, Pallas kernels, stage(): pl.pallas_call(functools.partial(stage_kernel, places, counts, planes, un...  16.8 us
    ppermute x9, starting transfers between devices, send(): return lax.ppermute(value, 'exp', perm)  13.1 us
    pallas_call x1, Pallas kernels, last_step(): pl.pallas_call(functools.partial(last_kernel, planes, unroll), in_specs=[...  7.72 us
    pallas_call x1, Pallas kernels, faces(): pl.pallas_call(functools.partial(faces_kernel, planes, unroll), in_specs=...  6.45 us
    ppermute x8, waiting for transfers between devices, exchange(): received += [lax.ppermute(high, axis, up), lax.ppermute(low, axis, down)]  5.14 us
    pallas_call x1, Pallas kernels, weigh(): pl.pallas_call(functools.partial(weigh_kernel, unroll), in_specs=[VMEM],...  2.45 us
  transfers between devices with their start and end apart: 17, of which 2 were waited for; matrix products, arithmetic and copies ran while one was open for 0% of the time, Pallas kernels for 26%

profile of v5, /device:TPU:1, one launch (start us, length us, event | category | flops | bytes accessed | tf_op | source)
XLA Modules:
  0.0 78.2 jit_solution(15077077584466582021)
XLA Ops:
  0.6 6.4 %faces.1 = (f32[2,130,48,128]{3,2,1,0:T(8,128)S(1)}, f32[2,130,48,128]{3,2,1,0:T(8,128)S(1)}, f32[2,128,256]{2,1,0:T(8,128)S(1)}, f32[2,128,256]{2,1,0:T(8,128)S...) custom-call(f32[128,32,256]{2,1,0:T(8,128)} %bitcast.10, s32[128,32,256]{2,1,0:T(8,128)} %pore_hbm.1), custom_call_target="tpu_custom_call" | custom-call | flops 4194304 | bytes 8388608 | tf_op jit(solution)/shard_map/faces/pallas_call | solution.py:173
  7.1 4.9 %collective-permute-start = (f32[2,128,256]{2,1,0:T(8,128)S(1)}, f32[2,128,256]{2,1,0:T(8,128)S(1)}, u32[]{:S(2)}, u32[]{:S(2)}) collective-permute-start(f32[2,128,256]{2,1,0:T(8,128)S(1)} %get-tuple-element.37), channel_id=1, source_target_pairs={{0,4},{4,8},{8,12},{1,5},{5,9},{9,13},{2,6},{6,10},{10,14},{3,7},{... | collective-permute-start | bytes 786440 | tf_op jit(solution)/shard_map/ppermute | solution.py:481
  12.0 1.9 %collective-permute-start.1 = (f32[2,128,256]{2,1,0:T(8,128)S(1)}, f32[2,128,256]{2,1,0:T(8,128)S(1)}, u32[]{:S(2)}, u32[]{:S(2)}) collective-permute-start(f32[2,128,256]{2,1,0:T(8,128)S(1)} %get-tuple-element.38), channel_id=1, source_target_pairs={{4,0},{8,4},{12,8},{5,1},{9,5},{13,9},{6,2},{10,6},{14,10},{7,3},{... | collective-permute-start | bytes 786440 | tf_op jit(solution)/shard_map/ppermute | solution.py:481
  14.0 3.1 %collective-permute-start.2 = (f32[64,128]{1,0:T(8,128)S(1)}, f32[64,128]{1,0:T(8,128)S(1)}, u32[]{:S(2)}, u32[]{:S(2)}) collective-permute-start(f32[64,128]{1,0:T(8,128)S(1)} %get-tuple-element.39), channel_id=1, source_target_pairs={{0,1},{1,2},{2,3},{4,5},{5,6},{6,7},{8,9},{9,10},{10,11},{12,13},{... | collective-permute-start | bytes 98312 | tf_op jit(solution)/shard_map/ppermute | solution.py:481
  17.1 1.3 %collective-permute-start.3 = (f32[64,128]{1,0:T(8,128)S(1)}, f32[64,128]{1,0:T(8,128)S(1)}, u32[]{:S(2)}, u32[]{:S(2)}) collective-permute-start(f32[64,128]{1,0:T(8,128)S(1)} %get-tuple-element.40), channel_id=1, source_target_pairs={{1,0},{2,1},{3,2},{5,4},{6,5},{7,6},{9,8},{10,9},{11,10},{13,12},{... | collective-permute-start | bytes 98312 | tf_op jit(solution)/shard_map/ppermute | solution.py:481
  19.0 0.0 copy-start
  19.0 2.4 %weigh.1.refs_10_ = f32[2,128,32,128]{3,2,1,0:T(8,128)S(1)} custom-call(f32[2,130,48,128]{3,2,1,0:T(8,128)S(1)} %get-tuple-element.42.wide), custom_call_target="tpu_custom_call" | custom-call | flops 12582912 | bytes 12582912 | tf_op jit(solution)/shard_map/weigh/pallas_call | solution.py:208
  21.5 0.0 collective-permute-done.2.refs_7_
  21.5 0.2 collective-permute-done.3.refs_8_
  21.7 0.0 collective-permute-done.refs_5_
  21.7 0.0 collective-permute-done.1.refs_6_
  21.7 0.0 copy-done
  21.8 6.7 %early.1 = (f32[2,130,48,128]{3,2,1,0:T(8,128)S(1)}, f32[2,128,32,128]{3,2,1,0:T(8,128)S(1)}, f32[2,130,48,128]{3,2,1,0:T(8,128)S(1)}, f32[128,256]{1,0:T(8,128)...) custom-call(s32[1]{0:T(128)S(6)} %copy.29.refs_0_, ...), custom_call_target="tpu_custom_call", output_to_operand_aliasing={{0}: (9, {}), {1}: (10, {})} | custom-call | flops 15728640 | bytes 3932160 | tf_op jit(solution)/shard_map/early/pallas_call | solution.py:323
  28.4 3.4 %collective-permute-start.12 = (f32[32,32,256]{2,1,0:T(8,128)S(1)}, f32[32,32,256]{2,1,0:T(8,128)S(1)}, u32[]{:S(2)}, u32[]{:S(2)}) collective-permute-start(f32[32,32,256]{2,1,0:T(8,128)S(1)} %get-tuple-element.64), channel_id=1, source_target_pairs={{0,16},{16,0},{32,48},{48,32},{64,80},{80,64},{96,112},{112,96},{1... | collective-permute-start | bytes 3145736 | tf_op jit(solution)/shard_map/ppermute | solution.py:516
  31.8 1.3 %collective-permute-start.8 = (f32[8,32,256]{2,1,0:T(8,128)S(1)}, f32[8,32,256]{2,1,0:T(8,128)S(1)}, u32[]{:S(2)}, u32[]{:S(2)}) collective-permute-start(f32[8,32,256]{2,1,0:T(8,128)S(1)} %get-tuple-element.59), channel_id=1, source_target_pairs={{0,32},{16,48},{32,64},{48,80},{64,96},{80,112},{96,0},{112,16},{1... | collective-permute-start | bytes 786440 | tf_op jit(solution)/shard_map/ppermute | solution.py:516
  33.1 1.4 %collective-permute-start.9 = (f32[8,32,256]{2,1,0:T(8,128)S(1)}, f32[8,32,256]{2,1,0:T(8,128)S(1)}, u32[]{:S(2)}, u32[]{:S(2)}) collective-permute-start(f32[8,32,256]{2,1,0:T(8,128)S(1)} %get-tuple-element.60), channel_id=1, source_target_pairs={{0,96},{16,112},{32,0},{48,16},{64,32},{80,48},{96,64},{112,80},{1... | collective-permute-start | bytes 786440 | tf_op jit(solution)/shard_map/ppermute | solution.py:516
  34.6 10.2 %late.1 = (f32[2,130,48,128]{3,2,1,0:T(8,128)S(1)}, f32[2,128,32,128]{3,2,1,0:T(8,128)S(1)}, f32[2,130,48,128]{3,2,1,0:T(8,128)S(1)}, f32[128,256]{1,0:T(8,128)S...) custom-call(s32[1]{0:T(128)S(6)} %copy.29.refs_0_, ...), custom_call_target="tpu_custom_call", output_to_operand_aliasing={{0}: (9, {}), {1}: (10, {}), {2}: (11, {}), {3}: (12, {}), ... | custom-call | flops 26214400 | bytes 6553600 | tf_op jit(solution)/shard_map/late/pallas_call | solution.py:323
  44.7 0.0 collective-permute-done.8.low_got
  44.7 0.0 collective-permute-done.9.high_got
  44.8 0.1 join.1
  44.9 0.1 collective-permute-start.10
  45.0 2.7 %collective-permute-start.11 = (f32[16,32,256]{2,1,0:T(8,128)S(1)}, f32[16,32,256]{2,1,0:T(8,128)S(1)}, u32[]{:S(2)}, u32[]{:S(2)}) collective-permute-start(f32[16,32,256]{2,1,0:T(8,128)S(1)} %get-tuple-element.62), channel_id=1, source_target_pairs={{0,96},{16,112},{32,0},{48,16},{64,32},{80,48},{96,64},{112,80},{1... | collective-permute-start | bytes 1572872 | tf_op jit(solution)/shard_map/ppermute | solution.py:516
  47.6 3.8 %collective-permute-start.6 = (f32[32,128]{1,0:T(8,128)S(1)}, f32[32,128]{1,0:T(8,128)S(1)}, u32[]{:S(2)}, u32[]{:S(2)}) collective-permute-start(f32[32,128]{1,0:T(8,128)S(1)} %get-tuple-element.53), channel_id=1, source_target_pairs={{0,1},{1,2},{2,3},{4,5},{5,6},{6,7},{8,9},{9,10},{10,11},{12,13},{... | collective-permute-start | bytes 49160 | tf_op jit(solution)/shard_map/ppermute | solution.py:481
  51.4 1.3 %collective-permute-start.7 = (f32[32,128]{1,0:T(8,128)S(1)}, f32[32,128]{1,0:T(8,128)S(1)}, u32[]{:S(2)}, u32[]{:S(2)}) collective-permute-start(f32[32,128]{1,0:T(8,128)S(1)} %get-tuple-element.54), channel_id=1, source_target_pairs={{1,0},{2,1},{3,2},{5,4},{6,5},{7,6},{9,8},{10,9},{11,10},{13,12},{... | collective-permute-start | bytes 49160 | tf_op jit(solution)/shard_map/ppermute | solution.py:481
  52.7 0.0 collective-permute-done.6.refs_4_.z_low
  52.7 5.5 %collective-permute-start.4 = (f32[128,256]{1,0:T(8,128)S(1)}, f32[128,256]{1,0:T(8,128)S(1)}, u32[]{:S(2)}, u32[]{:S(2)}) collective-permute-start(f32[128,256]{1,0:T(8,128)S(1)} %get-tuple-element.51), channel_id=1, source_target_pairs={{0,4},{4,8},{8,12},{1,5},{5,9},{9,13},{2,6},{6,10},{10,14},{3,7},{... | collective-permute-start | bytes 393224 | tf_op jit(solution)/shard_map/ppermute | solution.py:481
  58.2 0.0 collective-permute-done.7.refs_5_.z_high
  58.2 1.9 %collective-permute-start.5 = (f32[128,256]{1,0:T(8,128)S(1)}, f32[128,256]{1,0:T(8,128)S(1)}, u32[]{:S(2)}, u32[]{:S(2)}) collective-permute-start(f32[128,256]{1,0:T(8,128)S(1)} %get-tuple-element.52), channel_id=1, source_target_pairs={{4,0},{8,4},{12,8},{5,1},{9,5},{13,9},{6,2},{10,6},{14,10},{7,3},{... | collective-permute-start | bytes 393224 | tf_op jit(solution)/shard_map/ppermute | solution.py:481
  60.2 0.0 collective-permute-done.4.refs_2_.y_low
  60.2 4.9 %collective-permute-done.5.refs_3_.y_high = f32[128,256]{1,0:T(8,128)S(1)} collective-permute-done((f32[128,256]{1,0:T(8,128)S(1)}, f32[128,256]{1,0:T(8,128)S(1)}, u32[]{:S(2)}, u32[]{:S(2)}) %collective-permute-start.5) | collective-permute-done | bytes 131104 | tf_op jit(solution)/shard_map/ppermute | solution.py:481
  65.1 0.0 collective-permute-done.12.refs_1_
  65.1 0.1 add_q.1
  65.2 0.6 collective-permute-start.14
  65.8 0.0 collective-permute-done.10.refs_1_
  65.8 0.0 collective-permute-done.11.refs_2_
  65.8 0.1 add_p.1
  65.9 1.0 %collective-permute-start.13 = (f32[8,32,256]{2,1,0:T(8,128)S(1)}, f32[8,32,256]{2,1,0:T(8,128)S(1)}, u32[]{:S(2)}, u32[]{:S(2)}) collective-permute-start(f32[8,32,256]{2,1,0:T(8,128)S(1)} %get-tuple-element.68), channel_id=1, source_target_pairs={{0,16},{16,0},{32,48},{48,32},{64,80},{80,64},{96,112},{112,96},{1... | collective-permute-start | bytes 786440 | tf_op jit(solution)/shard_map/ppermute | solution.py:516
  66.8 0.4 collective-permute-start.15
  67.2 2.3 %collective-permute-start.16 = (f32[8,32,256]{2,1,0:T(8,128)S(1)}, f32[8,32,256]{2,1,0:T(8,128)S(1)}, u32[]{:S(2)}, u32[]{:S(2)}) collective-permute-start(f32[8,32,256]{2,1,0:T(8,128)S(1)} %get-tuple-element.71), channel_id=1, source_target_pairs={{0,96},{16,112},{32,0},{48,16},{64,32},{80,48},{96,64},{112,80},{1... | collective-permute-start | bytes 786440 | tf_op jit(solution)/shard_map/ppermute | solution.py:516
  69.5 7.7 %last_step.1 = (f32[128,32,256]{2,1,0:T(8,128)}, f32[2,130,48,128]{3,2,1,0:T(8,128)S(1)}) custom-call(bf16[256,32,256]{2,1,0:T(8,128)(2,1)} %bitcast.6, bf16[256,32,256]{2,1,0:T(8,128)(2,1)} %bitcast.9, f32[2,128,32,128]{3,2,1,0:T(8,128)S(1)} %get-tuple-element.50.kept, ...), custom_call_target="tpu_custom_call", output_to_operand_aliasing={{1}: (7, {})} | custom-call | flops 20971520 | bytes 8388608 | tf_op jit(solution)/shard_map/last_step/pallas_call | solution.py:398
  77.2 0.0 collective-permute-done.13
  77.3 0.0 collective-permute-done.14
  77.3 0.0 collective-permute-done.15
  77.3 0.0 collective-permute-done.16
  77.3 0.1 add_add_fusion
  77.4 0.8 %pad_maximum_fusion = f32[16,32,256]{2,1,0:T(8,128)} fusion(f32[8,32,256]{2,1,0:T(8,128)S(1)} %add_add_fusion, f32[8,32,256]{2,1,0:T(8,128)S(1)} %add.12), kind=kLoop, calls=%fused_computation | loop fusion | flops 131072 | bytes 1048576 | tf_op jit(solution)/shard_map/concatenate | solution.py:542
  (1 shorter events, 0.0 us)
Async XLA Ops:
  7.1 14.7 %collective-permute-start = (f32[2,128,256]{2,1,0:T(8,128)S(1)}, f32[2,128,256]{2,1,0:T(8,128)S(1)}, u32[]{:S(2)}, u32[]{:S(2)}) collective-permute-start(f32[2,128,256]{2,1,0:T(8,128)S(1)} %get-tuple-element.37), channel_id=1, source_target_pairs={{0,4},{4,8},{8,12},{1,5},{5,9},{9,13},{2,6},{6,10},{10,14},{3,7},{... | collective-permute-start | bytes 786440 | tf_op jit(solution)/shard_map/ppermute | solution.py:481
  12.0 9.7 %collective-permute-start.1 = (f32[2,128,256]{2,1,0:T(8,128)S(1)}, f32[2,128,256]{2,1,0:T(8,128)S(1)}, u32[]{:S(2)}, u32[]{:S(2)}) collective-permute-start(f32[2,128,256]{2,1,0:T(8,128)S(1)} %get-tuple-element.38), channel_id=1, source_target_pairs={{4,0},{8,4},{12,8},{5,1},{9,5},{13,9},{6,2},{10,6},{14,10},{7,3},{... | collective-permute-start | bytes 786440 | tf_op jit(solution)/shard_map/ppermute | solution.py:481
  14.0 7.5 %collective-permute-start.2 = (f32[64,128]{1,0:T(8,128)S(1)}, f32[64,128]{1,0:T(8,128)S(1)}, u32[]{:S(2)}, u32[]{:S(2)}) collective-permute-start(f32[64,128]{1,0:T(8,128)S(1)} %get-tuple-element.39), channel_id=1, source_target_pairs={{0,1},{1,2},{2,3},{4,5},{5,6},{6,7},{8,9},{9,10},{10,11},{12,13},{... | collective-permute-start | bytes 98312 | tf_op jit(solution)/shard_map/ppermute | solution.py:481
  17.1 4.7 %collective-permute-start.3 = (f32[64,128]{1,0:T(8,128)S(1)}, f32[64,128]{1,0:T(8,128)S(1)}, u32[]{:S(2)}, u32[]{:S(2)}) collective-permute-start(f32[64,128]{1,0:T(8,128)S(1)} %get-tuple-element.40), channel_id=1, source_target_pairs={{1,0},{2,1},{3,2},{5,4},{6,5},{7,6},{9,8},{10,9},{11,10},{13,12},{... | collective-permute-start | bytes 98312 | tf_op jit(solution)/shard_map/ppermute | solution.py:481
  19.0 2.7 %copy-start = (f32[8]{0:T(128)S(1)}, f32[8]{0:T(128)}, u32[]{:S(2)}) copy-start(f32[8]{0:T(128)} %refs_1_.3) | copy-start | bytes 100
  28.4 36.6 %collective-permute-start.12 = (f32[32,32,256]{2,1,0:T(8,128)S(1)}, f32[32,32,256]{2,1,0:T(8,128)S(1)}, u32[]{:S(2)}, u32[]{:S(2)}) collective-permute-start(f32[32,32,256]{2,1,0:T(8,128)S(1)} %get-tuple-element.64), channel_id=1, source_target_pairs={{0,16},{16,0},{32,48},{48,32},{64,80},{80,64},{96,112},{112,96},{1... | collective-permute-start | bytes 3145736 | tf_op jit(solution)/shard_map/ppermute | solution.py:516
  31.8 12.9 %collective-permute-start.8 = (f32[8,32,256]{2,1,0:T(8,128)S(1)}, f32[8,32,256]{2,1,0:T(8,128)S(1)}, u32[]{:S(2)}, u32[]{:S(2)}) collective-permute-start(f32[8,32,256]{2,1,0:T(8,128)S(1)} %get-tuple-element.59), channel_id=1, source_target_pairs={{0,32},{16,48},{32,64},{48,80},{64,96},{80,112},{96,0},{112,16},{1... | collective-permute-start | bytes 786440 | tf_op jit(solution)/shard_map/ppermute | solution.py:516
  33.1 11.6 %collective-permute-start.9 = (f32[8,32,256]{2,1,0:T(8,128)S(1)}, f32[8,32,256]{2,1,0:T(8,128)S(1)}, u32[]{:S(2)}, u32[]{:S(2)}) collective-permute-start(f32[8,32,256]{2,1,0:T(8,128)S(1)} %get-tuple-element.60), channel_id=1, source_target_pairs={{0,96},{16,112},{32,0},{48,16},{64,32},{80,48},{96,64},{112,80},{1... | collective-permute-start | bytes 786440 | tf_op jit(solution)/shard_map/ppermute | solution.py:516
  44.9 20.9 %collective-permute-start.10 = (f32[16,32,256]{2,1,0:T(8,128)S(1)}, f32[16,32,256]{2,1,0:T(8,128)S(1)}, u32[]{:S(2)}, u32[]{:S(2)}) collective-permute-start(f32[16,32,256]{2,1,0:T(8,128)S(1)} %get-tuple-element.61), channel_id=1, source_target_pairs={{0,32},{16,48},{32,64},{48,80},{64,96},{80,112},{96,0},{112,16},{1... | collective-permute-start | bytes 1572872 | tf_op jit(solution)/shard_map/ppermute | solution.py:516
  45.0 20.8 %collective-permute-start.11 = (f32[16,32,256]{2,1,0:T(8,128)S(1)}, f32[16,32,256]{2,1,0:T(8,128)S(1)}, u32[]{:S(2)}, u32[]{:S(2)}) collective-permute-start(f32[16,32,256]{2,1,0:T(8,128)S(1)} %get-tuple-element.62), channel_id=1, source_target_pairs={{0,96},{16,112},{32,0},{48,16},{64,32},{80,48},{96,64},{112,80},{1... | collective-permute-start | bytes 1572872 | tf_op jit(solution)/shard_map/ppermute | solution.py:516
  47.6 5.1 %collective-permute-start.6 = (f32[32,128]{1,0:T(8,128)S(1)}, f32[32,128]{1,0:T(8,128)S(1)}, u32[]{:S(2)}, u32[]{:S(2)}) collective-permute-start(f32[32,128]{1,0:T(8,128)S(1)} %get-tuple-element.53), channel_id=1, source_target_pairs={{0,1},{1,2},{2,3},{4,5},{5,6},{6,7},{8,9},{9,10},{10,11},{12,13},{... | collective-permute-start | bytes 49160 | tf_op jit(solution)/shard_map/ppermute | solution.py:481
  51.4 6.8 %collective-permute-start.7 = (f32[32,128]{1,0:T(8,128)S(1)}, f32[32,128]{1,0:T(8,128)S(1)}, u32[]{:S(2)}, u32[]{:S(2)}) collective-permute-start(f32[32,128]{1,0:T(8,128)S(1)} %get-tuple-element.54), channel_id=1, source_target_pairs={{1,0},{2,1},{3,2},{5,4},{6,5},{7,6},{9,8},{10,9},{11,10},{13,12},{... | collective-permute-start | bytes 49160 | tf_op jit(solution)/shard_map/ppermute | solution.py:481
  52.7 7.5 %collective-permute-start.4 = (f32[128,256]{1,0:T(8,128)S(1)}, f32[128,256]{1,0:T(8,128)S(1)}, u32[]{:S(2)}, u32[]{:S(2)}) collective-permute-start(f32[128,256]{1,0:T(8,128)S(1)} %get-tuple-element.51), channel_id=1, source_target_pairs={{0,4},{4,8},{8,12},{1,5},{5,9},{9,13},{2,6},{6,10},{10,14},{3,7},{... | collective-permute-start | bytes 393224 | tf_op jit(solution)/shard_map/ppermute | solution.py:481
  58.2 6.8 %collective-permute-start.5 = (f32[128,256]{1,0:T(8,128)S(1)}, f32[128,256]{1,0:T(8,128)S(1)}, u32[]{:S(2)}, u32[]{:S(2)}) collective-permute-start(f32[128,256]{1,0:T(8,128)S(1)} %get-tuple-element.52), channel_id=1, source_target_pairs={{4,0},{8,4},{12,8},{5,1},{9,5},{13,9},{6,2},{10,6},{14,10},{7,3},{... | collective-permute-start | bytes 393224 | tf_op jit(solution)/shard_map/ppermute | solution.py:481
  65.2 12.1 %collective-permute-start.14 = (f32[8,32,256]{2,1,0:T(8,128)S(1)}, f32[8,32,256]{2,1,0:T(8,128)S(1)}, u32[]{:S(2)}, u32[]{:S(2)}) collective-permute-start(f32[8,32,256]{2,1,0:T(8,128)S(1)} %get-tuple-element.69), channel_id=1, source_target_pairs={{0,64},{16,80},{32,96},{48,112},{64,0},{80,16},{96,32},{112,48},{1... | collective-permute-start | bytes 786440 | tf_op jit(solution)/shard_map/ppermute | solution.py:516
  65.9 11.4 %collective-permute-start.13 = (f32[8,32,256]{2,1,0:T(8,128)S(1)}, f32[8,32,256]{2,1,0:T(8,128)S(1)}, u32[]{:S(2)}, u32[]{:S(2)}) collective-permute-start(f32[8,32,256]{2,1,0:T(8,128)S(1)} %get-tuple-element.68), channel_id=1, source_target_pairs={{0,16},{16,0},{32,48},{48,32},{64,80},{80,64},{96,112},{112,96},{1... | collective-permute-start | bytes 786440 | tf_op jit(solution)/shard_map/ppermute | solution.py:516
  66.8 10.5 %collective-permute-start.15 = (f32[8,32,256]{2,1,0:T(8,128)S(1)}, f32[8,32,256]{2,1,0:T(8,128)S(1)}, u32[]{:S(2)}, u32[]{:S(2)}) collective-permute-start(f32[8,32,256]{2,1,0:T(8,128)S(1)} %get-tuple-element.70), channel_id=1, source_target_pairs={{0,32},{16,48},{32,64},{48,80},{64,96},{80,112},{96,0},{112,16},{1... | collective-permute-start | bytes 786440 | tf_op jit(solution)/shard_map/ppermute | solution.py:516
  67.2 10.1 %collective-permute-start.16 = (f32[8,32,256]{2,1,0:T(8,128)S(1)}, f32[8,32,256]{2,1,0:T(8,128)S(1)}, u32[]{:S(2)}, u32[]{:S(2)}) collective-permute-start(f32[8,32,256]{2,1,0:T(8,128)S(1)} %get-tuple-element.71), channel_id=1, source_target_pairs={{0,96},{16,112},{32,0},{48,16},{64,32},{80,48},{96,64},{112,80},{1... | collective-permute-start | bytes 786440 | tf_op jit(solution)/shard_map/ppermute | solution.py:516

commit v6 on v5

--- a/solution.py
+++ b/solution.py
@@ -24,6 +24,24 @@
     if isinstance(shift, int):
         return pltpu.roll(values, shift % LANES, 1)
     return pltpu.roll(values, lax.rem(shift + LANES, LANES), 1)
+
+
+def columns(low, high, x, lane):
+    return lane_to(jnp.where(lane == x, low, high), x, 0)
+
+
+def collect(values, x, lane, low, high):
+    before = (x - 1) % LANES if isinstance(x, int) else lax.rem(x + LANES - 1, LANES)
+    ends = lane_to(jnp.where(lane == 0, values[0], values[-1]), 0, x)
+    return jnp.where(lane == x, ends, low), jnp.where(lane == before, ends, high)
+
+
+def one_back(values):
+    return pltpu.roll(values, LANES - 1, 1)
+
+
+def one_on(values):
+    return pltpu.roll(values, 1, 1)
 
 
 def in_hbm(*arrays):
@@ -139,23 +157,22 @@
     def body(t, slot):
         def load(i, carry):
             x = t * planes + i
-            here = lane == x
             out = list(carry)
-            stores = []
+            stores, values = [], ([], [])
             for h in range(count):
                 pores = pore[slot, i, :, run(h)].astype(F32)
                 for part, (array, value) in enumerate(((masked, adj[slot, i, :, run(h)] * pores), (wide, pores))):
                     stores.append((array, (h, x + 1, slice(ROWS, ROWS + ny)), value))
-                    if h == 0:
-                        out[part] = jnp.where(here, lane_to(value, 0, x), out[part])
-                    if h == count - 1:
-                        out[2 + part] = jnp.where(here, lane_to(value, LANES - 1, x), out[2 + part])
+                    values[part].append(value)
                 for rows in (slice(0, ROWS), slice(ROWS + ny, 2 * ROWS + ny)):
                     stores.append((wide, (h, x + 1, rows), jnp.zeros((ROWS, LANES), F32)))
+            for part in range(2):
+                out[part], out[2 + part] = collect(values[part], x, lane, out[part], out[2 + part])
             return tuple(out), stores
 
-        parts = (z_low[:ny], z_low[ny:], z_high[:ny], z_high[ny:])
-        z_low[:ny], z_low[ny:], z_high[:ny], z_high[ny:] = over(planes, unroll, load, parts)
+        parts = (z_low[:ny], z_low[ny:], one_back(z_high[:ny]), one_back(z_high[ny:]))
+        z_low[:ny], z_low[ny:], m_high, p_high = over(planes, unroll, load, parts)
+        z_high[:ny], z_high[ny:] = one_on(m_high), one_on(p_high)
 
         for x in range(t * planes, (t + 1) * planes, ROWS):
             for part, array in enumerate((masked, wide)):
@@ -248,7 +265,7 @@
 
     def ahead(t):
         start = starts[t]
-        m_low, m_high = z_low[:ny], z_high[:ny]
+        m_low, m_high = z_low[:ny], one_back(z_high[:ny])
 
         flat = flat_rows(kept)
         for at in range(0, planes, ROWS):
@@ -262,7 +279,8 @@
 
         def gather(i, carry):
             x = start + i
-            _, sums = weighted(masked, x + 1, lane, lane_to(m_low, x, 0), lane_to(m_high, x, LANES - 1))
+            beside = columns(m_low, m_high, x, lane)
+            _, sums = weighted(masked, x + 1, lane, beside, beside)
             return carry, [(inflow, (h, i), 0.1 * sums[h]) for h in range(count)]
 
         over(planes, unroll[0], gather)
@@ -270,12 +288,13 @@
     def body(t, slot):
         start = starts[t]
         grad, block = targets[t]
-        p_low, p_high = 0.1 * z_low[ny:], 0.1 * z_high[ny:]
+        p_low, p_high = 0.1 * z_low[ny:], one_back(0.1 * z_high[ny:])
 
         def plane(i, carry):
             low, high = carry
             x = start + i
-            stores = []
+            beside = columns(p_low, p_high, x, lane)
+            stores, values = [], []
             for h in range(count):
                 centre = masked[h, x + 1, ROWS : ROWS + ny, :]
                 filled = late_f[slot, i, :, run(h)].astype(F32)
@@ -285,9 +304,9 @@
                 early_r = pl.reciprocal(-inverse - early, approx=True)
                 weight = kept[h, x]
                 if h == 0:
-                    weight = weight - jnp.where(lane == 0, lane_to(p_low, x, 0), 0.0)
+                    weight = weight - jnp.where(lane == 0, beside, 0.0)
                 if h == count - 1:
-                    weight = weight - jnp.where(lane == LANES - 1, lane_to(p_high, x, LANES - 1), 0.0)
+                    weight = weight - jnp.where(lane == LANES - 1, beside, 0.0)
                 pore = weight != SOLID
                 uptake = cap[slot, i, :, run(h)] * inverse
                 updated = centre * (weight - uptake * (late_r * late_r)) + (inflow[h, i] + source)
@@ -296,13 +315,11 @@
                 term = (filled * late_r) * centre + (early * early_r) * updated
                 stores.append((grad, (block * planes + i, slice(None), run(h)), term))
                 stores.append((adj, (h, x + 1, slice(ROWS, ROWS + ny)), updated))
-                if h == 0:
-                    low = jnp.where(lane == x, lane_to(updated, 0, x), low)
-                if h == count - 1:
-                    high = jnp.where(lane == x, lane_to(updated, LANES - 1, x), high)
-            return (low, high), stores
-
-        out_z_low[...], out_z_high[...] = over(planes, unroll[1], plane, (out_z_low[...], out_z_high[...]))
+                values.append(updated)
+            return collect(values, x, lane, low, high), stores
+
+        out_z_low[...], high = over(planes, unroll[1], plane, (out_z_low[...], one_back(out_z_high[...])))
+        out_z_high[...] = one_on(high)
         for at in range(0, planes, ROWS):
             store_rows(out_y_low, start + at, face_rows(adj, start + at, 0))
             store_rows(out_y_high, start + at, face_rows(adj, start + at, ny - 1))
@@ -359,11 +376,12 @@
     def ahead(t):
         for x in range(t * planes, (t + 1) * planes, ROWS):
             halo_rows(adj, x, y_low[pl.ds(x, ROWS), :], y_high[pl.ds(x, ROWS), :])
+        m_low, m_high = z_low[...], one_back(z_high[...])
 
         def gather(i, carry):
             x = t * planes + i
-            low, high = lane_to(z_low[...], x, 0), lane_to(z_high[...], x, LANES - 1)
-            _, sums = weighted(adj, x + 1, lane, low, high)
+            beside = columns(m_low, m_high, x, lane)
+            _, sums = weighted(adj, x + 1, lane, beside, beside)
             return carry, [(inflow, (h, i), 0.1 * sums[h]) for h in range(count)]
 
         over(planes, planes, gather)
@@ -532,7 +550,7 @@
     from_low, from_high = send(up, 1, 0), send(down, 3, 0)
     face_halo = exchange(*next_faces)
 
-    totals_q = add([own_q, crossed], face_halo, ring, "add_q")
+    totals_q = add([own_q, crossed], face_halo[:1] + face_halo[2:], ring, "add_q")
     parts_q = [send(totals_q[turn], turn, 0) for turn in (2, 1, 3)]
     total_s, total_k = add([own_p, from_low, from_high], totals_q[:1], 2, "add_p")
     last_p = send(total_s, 0, 1)

time: 79.3 us -> 84 us (1.059)
  waiting for transfers between devices: 5.17 us -> 10 us
    ppermute x8, waiting for transfers between devices: 5.14 us -> 10 us  [exchange(): received += [lax.ppermute(high, axis, up), lax.ppermute(low, axis, down)]]
  transfers between devices with their start and end apart: 17 -> 17, of which waited for: 2 -> 4; matrix products, arithmetic and copies ran while one was open for 0% -> 0% of each run, Pallas kernels for 26% -> 25%
where the time goes in v6:
time: 84 us; the launch traced here: 83.2 us
  starting transfers between devices  36.6 us (44%)
  Pallas kernels  34.1 us (41%)
  waiting for transfers between devices  10 us (12%)
  between operations  1.5 us (2%)
  other arithmetic  0.94 us (1%)
    ppermute x8, starting transfers between devices, exchange(): received += [lax.ppermute(high, axis, up), lax.ppermute(low, axis, down)]  23.4 us
    pallas_call x2, Pallas kernels, stage(): pl.pallas_call(functools.partial(stage_kernel, places, counts, planes, un...  17.4 us
    ppermute x9, starting transfers between devices, send(): return lax.ppermute(value, 'exp', perm)  13.3 us
    ppermute x8, waiting for transfers between devices, exchange(): received += [lax.ppermute(high, axis, up), lax.ppermute(low, axis, down)]  10 us
    pallas_call x1, Pallas kernels, last_step(): pl.pallas_call(functools.partial(last_kernel, planes, unroll), in_specs=[...  7.76 us
    pallas_call x1, Pallas kernels, faces(): pl.pallas_call(functools.partial(faces_kernel, planes, unroll), in_specs=...  6.19 us
    pallas_call x1, Pallas kernels, weigh(): pl.pallas_call(functools.partial(weigh_kernel, unroll), in_specs=[VMEM],...  2.45 us
  transfers between devices with their start and end apart: 17, of which 4 were waited for; matrix products, arithmetic and copies ran while one was open for 0% of the time, Pallas kernels for 25%

profile of v6, /device:TPU:1, one launch (start us, length us, event | category | flops | bytes accessed | tf_op | source)
XLA Modules:
  0.0 83.2 jit_solution(2059442913857901499)
XLA Ops:
  0.6 6.2 %faces.1 = (f32[2,130,48,128]{3,2,1,0:T(8,128)S(1)}, f32[2,130,48,128]{3,2,1,0:T(8,128)S(1)}, f32[2,128,256]{2,1,0:T(8,128)S(1)}, f32[2,128,256]{2,1,0:T(8,128)S...) custom-call(f32[128,32,256]{2,1,0:T(8,128)} %bitcast.10, s32[128,32,256]{2,1,0:T(8,128)} %pore_hbm.1), custom_call_target="tpu_custom_call" | custom-call | flops 4194304 | bytes 8388608 | tf_op jit(solution)/shard_map/faces/pallas_call | solution.py:190
  6.8 4.9 %collective-permute-start = (f32[2,128,256]{2,1,0:T(8,128)S(1)}, f32[2,128,256]{2,1,0:T(8,128)S(1)}, u32[]{:S(2)}, u32[]{:S(2)}) collective-permute-start(f32[2,128,256]{2,1,0:T(8,128)S(1)} %get-tuple-element.37), channel_id=1, source_target_pairs={{0,4},{4,8},{8,12},{1,5},{5,9},{9,13},{2,6},{6,10},{10,14},{3,7},{... | collective-permute-start | bytes 786440 | tf_op jit(solution)/shard_map/ppermute | solution.py:499
  11.8 1.9 %collective-permute-start.1 = (f32[2,128,256]{2,1,0:T(8,128)S(1)}, f32[2,128,256]{2,1,0:T(8,128)S(1)}, u32[]{:S(2)}, u32[]{:S(2)}) collective-permute-start(f32[2,128,256]{2,1,0:T(8,128)S(1)} %get-tuple-element.38), channel_id=1, source_target_pairs={{4,0},{8,4},{12,8},{5,1},{9,5},{13,9},{6,2},{10,6},{14,10},{7,3},{... | collective-permute-start | bytes 786440 | tf_op jit(solution)/shard_map/ppermute | solution.py:499
  13.7 3.1 %collective-permute-start.2 = (f32[64,128]{1,0:T(8,128)S(1)}, f32[64,128]{1,0:T(8,128)S(1)}, u32[]{:S(2)}, u32[]{:S(2)}) collective-permute-start(f32[64,128]{1,0:T(8,128)S(1)} %get-tuple-element.39), channel_id=1, source_target_pairs={{0,1},{1,2},{2,3},{4,5},{5,6},{6,7},{8,9},{9,10},{10,11},{12,13},{... | collective-permute-start | bytes 98312 | tf_op jit(solution)/shard_map/ppermute | solution.py:499
  16.8 1.3 %collective-permute-start.3 = (f32[64,128]{1,0:T(8,128)S(1)}, f32[64,128]{1,0:T(8,128)S(1)}, u32[]{:S(2)}, u32[]{:S(2)}) collective-permute-start(f32[64,128]{1,0:T(8,128)S(1)} %get-tuple-element.40), channel_id=1, source_target_pairs={{1,0},{2,1},{3,2},{5,4},{6,5},{7,6},{9,8},{10,9},{11,10},{13,12},{... | collective-permute-start | bytes 98312 | tf_op jit(solution)/shard_map/ppermute | solution.py:499
  18.8 0.0 copy-start
  18.8 2.4 %weigh.1.refs_10_ = f32[2,128,32,128]{3,2,1,0:T(8,128)S(1)} custom-call(f32[2,130,48,128]{3,2,1,0:T(8,128)S(1)} %get-tuple-element.42.wide), custom_call_target="tpu_custom_call" | custom-call | flops 12582912 | bytes 12582912 | tf_op jit(solution)/shard_map/weigh/pallas_call | solution.py:225
  21.2 0.0 collective-permute-done.2.refs_7_
  21.3 0.2 collective-permute-done.3.refs_8_
  21.5 0.0 collective-permute-done.refs_5_
  21.5 0.0 collective-permute-done.1.refs_6_
  21.5 0.0 copy-done
  21.5 6.9 %early.1 = (f32[2,130,48,128]{3,2,1,0:T(8,128)S(1)}, f32[2,128,32,128]{3,2,1,0:T(8,128)S(1)}, f32[2,130,48,128]{3,2,1,0:T(8,128)S(1)}, f32[128,256]{1,0:T(8,128)...) custom-call(s32[1]{0:T(128)S(6)} %copy.29.refs_0_, ...), custom_call_target="tpu_custom_call", output_to_operand_aliasing={{0}: (9, {}), {1}: (10, {})} | custom-call | flops 15728640 | bytes 3932160 | tf_op jit(solution)/shard_map/early/pallas_call | solution.py:340
  28.4 3.4 %collective-permute-start.12 = (f32[32,32,256]{2,1,0:T(8,128)S(1)}, f32[32,32,256]{2,1,0:T(8,128)S(1)}, u32[]{:S(2)}, u32[]{:S(2)}) collective-permute-start(f32[32,32,256]{2,1,0:T(8,128)S(1)} %get-tuple-element.64), channel_id=1, source_target_pairs={{0,16},{16,0},{32,48},{48,32},{64,80},{80,64},{96,112},{112,96},{1... | collective-permute-start | bytes 3145736 | tf_op jit(solution)/shard_map/ppermute | solution.py:534
  31.7 1.3 %collective-permute-start.8 = (f32[8,32,256]{2,1,0:T(8,128)S(1)}, f32[8,32,256]{2,1,0:T(8,128)S(1)}, u32[]{:S(2)}, u32[]{:S(2)}) collective-permute-start(f32[8,32,256]{2,1,0:T(8,128)S(1)} %get-tuple-element.59), channel_id=1, source_target_pairs={{0,32},{16,48},{32,64},{48,80},{64,96},{80,112},{96,0},{112,16},{1... | collective-permute-start | bytes 786440 | tf_op jit(solution)/shard_map/ppermute | solution.py:534
  33.0 1.4 %collective-permute-start.9 = (f32[8,32,256]{2,1,0:T(8,128)S(1)}, f32[8,32,256]{2,1,0:T(8,128)S(1)}, u32[]{:S(2)}, u32[]{:S(2)}) collective-permute-start(f32[8,32,256]{2,1,0:T(8,128)S(1)} %get-tuple-element.60), channel_id=1, source_target_pairs={{0,96},{16,112},{32,0},{48,16},{64,32},{80,48},{96,64},{112,80},{1... | collective-permute-start | bytes 786440 | tf_op jit(solution)/shard_map/ppermute | solution.py:534
  34.5 10.5 %late.1 = (f32[2,130,48,128]{3,2,1,0:T(8,128)S(1)}, f32[2,128,32,128]{3,2,1,0:T(8,128)S(1)}, f32[2,130,48,128]{3,2,1,0:T(8,128)S(1)}, f32[128,256]{1,0:T(8,128)S...) custom-call(s32[1]{0:T(128)S(6)} %copy.29.refs_0_, ...), custom_call_target="tpu_custom_call", output_to_operand_aliasing={{0}: (9, {}), {1}: (10, {}), {2}: (11, {}), {3}: (12, {}), ... | custom-call | flops 26214400 | bytes 6553600 | tf_op jit(solution)/shard_map/late/pallas_call | solution.py:340
  45.0 0.0 collective-permute-done.8.low_got
  45.0 0.0 collective-permute-done.9.high_got
  45.0 0.1 join.1
  45.1 0.1 collective-permute-start.10
  45.2 2.7 %collective-permute-start.11 = (f32[16,32,256]{2,1,0:T(8,128)S(1)}, f32[16,32,256]{2,1,0:T(8,128)S(1)}, u32[]{:S(2)}, u32[]{:S(2)}) collective-permute-start(f32[16,32,256]{2,1,0:T(8,128)S(1)} %get-tuple-element.62), channel_id=1, source_target_pairs={{0,96},{16,112},{32,0},{48,16},{64,32},{80,48},{96,64},{112,80},{1... | collective-permute-start | bytes 1572872 | tf_op jit(solution)/shard_map/ppermute | solution.py:534
  47.9 5.8 %collective-permute-start.4 = (f32[128,256]{1,0:T(8,128)S(1)}, f32[128,256]{1,0:T(8,128)S(1)}, u32[]{:S(2)}, u32[]{:S(2)}) collective-permute-start(f32[128,256]{1,0:T(8,128)S(1)} %get-tuple-element.51), channel_id=1, source_target_pairs={{0,4},{4,8},{8,12},{1,5},{5,9},{9,13},{2,6},{6,10},{10,14},{3,7},{... | collective-permute-start | bytes 393224 | tf_op jit(solution)/shard_map/ppermute | solution.py:499
  53.7 3.1 %collective-permute-start.6 = (f32[32,128]{1,0:T(8,128)S(1)}, f32[32,128]{1,0:T(8,128)S(1)}, u32[]{:S(2)}, u32[]{:S(2)}) collective-permute-start(f32[32,128]{1,0:T(8,128)S(1)} %get-tuple-element.53), channel_id=1, source_target_pairs={{0,1},{1,2},{2,3},{4,5},{5,6},{6,7},{8,9},{9,10},{10,11},{12,13},{... | collective-permute-start | bytes 49160 | tf_op jit(solution)/shard_map/ppermute | solution.py:499
  56.8 0.9 %collective-permute-done.6.refs_3_.z_low = f32[32,128]{1,0:T(8,128)S(1)} collective-permute-done((f32[32,128]{1,0:T(8,128)S(1)}, f32[32,128]{1,0:T(8,128)S(1)}, u32[]{:S(2)}, u32[]{:S(2)}) %collective-permute-start.6) | collective-permute-done | bytes 16416 | tf_op jit(solution)/shard_map/ppermute | solution.py:499
  57.7 1.3 %collective-permute-start.7 = (f32[32,128]{1,0:T(8,128)S(1)}, f32[32,128]{1,0:T(8,128)S(1)}, u32[]{:S(2)}, u32[]{:S(2)}) collective-permute-start(f32[32,128]{1,0:T(8,128)S(1)} %get-tuple-element.54), channel_id=1, source_target_pairs={{1,0},{2,1},{3,2},{5,4},{6,5},{7,6},{9,8},{10,9},{11,10},{13,12},{... | collective-permute-start | bytes 49160 | tf_op jit(solution)/shard_map/ppermute | solution.py:499
  59.0 3.7 %collective-permute-done.7.refs_4_.z_high = f32[32,128]{1,0:T(8,128)S(1)} collective-permute-done((f32[32,128]{1,0:T(8,128)S(1)}, f32[32,128]{1,0:T(8,128)S(1)}, u32[]{:S(2)}, u32[]{:S(2)}) %collective-permute-start.7) | collective-permute-done | bytes 16416 | tf_op jit(solution)/shard_map/ppermute | solution.py:499
  62.7 0.0 collective-permute-done.4.refs_2_.y_low
  62.7 0.0 collective-permute-done.12.refs_1_
  62.7 0.1 add_q.1
  62.8 0.8 collective-permute-start.14
  63.6 0.0 collective-permute-done.10.refs_1_
  63.6 0.0 collective-permute-done.11.refs_2_
  63.6 0.1 add_p.1
  63.7 1.0 %collective-permute-start.13 = (f32[8,32,256]{2,1,0:T(8,128)S(1)}, f32[8,32,256]{2,1,0:T(8,128)S(1)}, u32[]{:S(2)}, u32[]{:S(2)}) collective-permute-start(f32[8,32,256]{2,1,0:T(8,128)S(1)} %get-tuple-element.68), channel_id=1, source_target_pairs={{0,16},{16,0},{32,48},{48,32},{64,80},{80,64},{96,112},{112,96},{1... | collective-permute-start | bytes 786440 | tf_op jit(solution)/shard_map/ppermute | solution.py:534
  64.6 0.4 collective-permute-start.15
  65.0 2.3 %collective-permute-start.16 = (f32[8,32,256]{2,1,0:T(8,128)S(1)}, f32[8,32,256]{2,1,0:T(8,128)S(1)}, u32[]{:S(2)}, u32[]{:S(2)}) collective-permute-start(f32[8,32,256]{2,1,0:T(8,128)S(1)} %get-tuple-element.71), channel_id=1, source_target_pairs={{0,96},{16,112},{32,0},{48,16},{64,32},{80,48},{96,64},{112,80},{1... | collective-permute-start | bytes 786440 | tf_op jit(solution)/shard_map/ppermute | solution.py:534
  67.3 1.9 %collective-permute-start.5 = (f32[128,256]{1,0:T(8,128)S(1)}, f32[128,256]{1,0:T(8,128)S(1)}, u32[]{:S(2)}, u32[]{:S(2)}) collective-permute-start(f32[128,256]{1,0:T(8,128)S(1)} %get-tuple-element.52), channel_id=1, source_target_pairs={{4,0},{8,4},{12,8},{5,1},{9,5},{13,9},{6,2},{10,6},{14,10},{7,3},{... | collective-permute-start | bytes 393224 | tf_op jit(solution)/shard_map/ppermute | solution.py:499
  69.2 5.2 %collective-permute-done.5.y_high = f32[128,256]{1,0:T(8,128)S(1)} collective-permute-done((f32[128,256]{1,0:T(8,128)S(1)}, f32[128,256]{1,0:T(8,128)S(1)}, u32[]{:S(2)}, u32[]{:S(2)}) %collective-permute-start.5) | collective-permute-done | bytes 131104 | tf_op jit(solution)/shard_map/ppermute | solution.py:499
  74.4 7.8 %last_step.1 = (f32[128,32,256]{2,1,0:T(8,128)}, f32[2,130,48,128]{3,2,1,0:T(8,128)S(1)}) custom-call(bf16[256,32,256]{2,1,0:T(8,128)(2,1)} %bitcast.6, bf16[256,32,256]{2,1,0:T(8,128)(2,1)} %bitcast.9, f32[2,128,32,128]{3,2,1,0:T(8,128)S(1)} %get-tuple-element.50.kept, ...), custom_call_target="tpu_custom_call", output_to_operand_aliasing={{1}: (7, {})} | custom-call | flops 20971520 | bytes 8388608 | tf_op jit(solution)/shard_map/last_step/pallas_call | solution.py:416
  82.2 0.0 collective-permute-done.13
  82.2 0.0 collective-permute-done.14
  82.2 0.0 collective-permute-done.15
  82.3 0.0 collective-permute-done.16
  82.3 0.1 add_add_fusion
  82.3 0.8 %pad_maximum_fusion = f32[16,32,256]{2,1,0:T(8,128)} fusion(f32[8,32,256]{2,1,0:T(8,128)S(1)} %add_add_fusion, f32[8,32,256]{2,1,0:T(8,128)S(1)} %add.12), kind=kLoop, calls=%fused_computation | loop fusion | flops 131072 | bytes 1048576 | tf_op jit(solution)/shard_map/concatenate | solution.py:560
  (1 shorter events, 0.0 us)
Async XLA Ops:
  6.8 14.7 %collective-permute-start = (f32[2,128,256]{2,1,0:T(8,128)S(1)}, f32[2,128,256]{2,1,0:T(8,128)S(1)}, u32[]{:S(2)}, u32[]{:S(2)}) collective-permute-start(f32[2,128,256]{2,1,0:T(8,128)S(1)} %get-tuple-element.37), channel_id=1, source_target_pairs={{0,4},{4,8},{8,12},{1,5},{5,9},{9,13},{2,6},{6,10},{10,14},{3,7},{... | collective-permute-start | bytes 786440 | tf_op jit(solution)/shard_map/ppermute | solution.py:499
  11.8 9.7 %collective-permute-start.1 = (f32[2,128,256]{2,1,0:T(8,128)S(1)}, f32[2,128,256]{2,1,0:T(8,128)S(1)}, u32[]{:S(2)}, u32[]{:S(2)}) collective-permute-start(f32[2,128,256]{2,1,0:T(8,128)S(1)} %get-tuple-element.38), channel_id=1, source_target_pairs={{4,0},{8,4},{12,8},{5,1},{9,5},{13,9},{6,2},{10,6},{14,10},{7,3},{... | collective-permute-start | bytes 786440 | tf_op jit(solution)/shard_map/ppermute | solution.py:499
  13.7 7.5 %collective-permute-start.2 = (f32[64,128]{1,0:T(8,128)S(1)}, f32[64,128]{1,0:T(8,128)S(1)}, u32[]{:S(2)}, u32[]{:S(2)}) collective-permute-start(f32[64,128]{1,0:T(8,128)S(1)} %get-tuple-element.39), channel_id=1, source_target_pairs={{0,1},{1,2},{2,3},{4,5},{5,6},{6,7},{8,9},{9,10},{10,11},{12,13},{... | collective-permute-start | bytes 98312 | tf_op jit(solution)/shard_map/ppermute | solution.py:499
  16.8 4.7 %collective-permute-start.3 = (f32[64,128]{1,0:T(8,128)S(1)}, f32[64,128]{1,0:T(8,128)S(1)}, u32[]{:S(2)}, u32[]{:S(2)}) collective-permute-start(f32[64,128]{1,0:T(8,128)S(1)} %get-tuple-element.40), channel_id=1, source_target_pairs={{1,0},{2,1},{3,2},{5,4},{6,5},{7,6},{9,8},{10,9},{11,10},{13,12},{... | collective-permute-start | bytes 98312 | tf_op jit(solution)/shard_map/ppermute | solution.py:499
  18.8 2.7 %copy-start = (f32[8]{0:T(128)S(1)}, f32[8]{0:T(128)}, u32[]{:S(2)}) copy-start(f32[8]{0:T(128)} %refs_1_.3) | copy-start | bytes 100
  28.4 34.3 %collective-permute-start.12 = (f32[32,32,256]{2,1,0:T(8,128)S(1)}, f32[32,32,256]{2,1,0:T(8,128)S(1)}, u32[]{:S(2)}, u32[]{:S(2)}) collective-permute-start(f32[32,32,256]{2,1,0:T(8,128)S(1)} %get-tuple-element.64), channel_id=1, source_target_pairs={{0,16},{16,0},{32,48},{48,32},{64,80},{80,64},{96,112},{112,96},{1... | collective-permute-start | bytes 3145736 | tf_op jit(solution)/shard_map/ppermute | solution.py:534
  31.7 13.3 %collective-permute-start.8 = (f32[8,32,256]{2,1,0:T(8,128)S(1)}, f32[8,32,256]{2,1,0:T(8,128)S(1)}, u32[]{:S(2)}, u32[]{:S(2)}) collective-permute-start(f32[8,32,256]{2,1,0:T(8,128)S(1)} %get-tuple-element.59), channel_id=1, source_target_pairs={{0,32},{16,48},{32,64},{48,80},{64,96},{80,112},{96,0},{112,16},{1... | collective-permute-start | bytes 786440 | tf_op jit(solution)/shard_map/ppermute | solution.py:534
  33.0 12.0 %collective-permute-start.9 = (f32[8,32,256]{2,1,0:T(8,128)S(1)}, f32[8,32,256]{2,1,0:T(8,128)S(1)}, u32[]{:S(2)}, u32[]{:S(2)}) collective-permute-start(f32[8,32,256]{2,1,0:T(8,128)S(1)} %get-tuple-element.60), channel_id=1, source_target_pairs={{0,96},{16,112},{32,0},{48,16},{64,32},{80,48},{96,64},{112,80},{1... | collective-permute-start | bytes 786440 | tf_op jit(solution)/shard_map/ppermute | solution.py:534
  45.1 18.4 %collective-permute-start.10 = (f32[16,32,256]{2,1,0:T(8,128)S(1)}, f32[16,32,256]{2,1,0:T(8,128)S(1)}, u32[]{:S(2)}, u32[]{:S(2)}) collective-permute-start(f32[16,32,256]{2,1,0:T(8,128)S(1)} %get-tuple-element.61), channel_id=1, source_target_pairs={{0,32},{16,48},{32,64},{48,80},{64,96},{80,112},{96,0},{112,16},{1... | collective-permute-start | bytes 1572872 | tf_op jit(solution)/shard_map/ppermute | solution.py:534
  45.2 18.4 %collective-permute-start.11 = (f32[16,32,256]{2,1,0:T(8,128)S(1)}, f32[16,32,256]{2,1,0:T(8,128)S(1)}, u32[]{:S(2)}, u32[]{:S(2)}) collective-permute-start(f32[16,32,256]{2,1,0:T(8,128)S(1)} %get-tuple-element.62), channel_id=1, source_target_pairs={{0,96},{16,112},{32,0},{48,16},{64,32},{80,48},{96,64},{112,80},{1... | collective-permute-start | bytes 1572872 | tf_op jit(solution)/shard_map/ppermute | solution.py:534
  47.9 14.8 %collective-permute-start.4 = (f32[128,256]{1,0:T(8,128)S(1)}, f32[128,256]{1,0:T(8,128)S(1)}, u32[]{:S(2)}, u32[]{:S(2)}) collective-permute-start(f32[128,256]{1,0:T(8,128)S(1)} %get-tuple-element.51), channel_id=1, source_target_pairs={{0,4},{4,8},{8,12},{1,5},{5,9},{9,13},{2,6},{6,10},{10,14},{3,7},{... | collective-permute-start | bytes 393224 | tf_op jit(solution)/shard_map/ppermute | solution.py:499
  53.7 4.0 %collective-permute-start.6 = (f32[32,128]{1,0:T(8,128)S(1)}, f32[32,128]{1,0:T(8,128)S(1)}, u32[]{:S(2)}, u32[]{:S(2)}) collective-permute-start(f32[32,128]{1,0:T(8,128)S(1)} %get-tuple-element.53), channel_id=1, source_target_pairs={{0,1},{1,2},{2,3},{4,5},{5,6},{6,7},{8,9},{9,10},{10,11},{12,13},{... | collective-permute-start | bytes 49160 | tf_op jit(solution)/shard_map/ppermute | solution.py:499
  57.7 5.0 %collective-permute-start.7 = (f32[32,128]{1,0:T(8,128)S(1)}, f32[32,128]{1,0:T(8,128)S(1)}, u32[]{:S(2)}, u32[]{:S(2)}) collective-permute-start(f32[32,128]{1,0:T(8,128)S(1)} %get-tuple-element.54), channel_id=1, source_target_pairs={{1,0},{2,1},{3,2},{5,4},{6,5},{7,6},{9,8},{10,9},{11,10},{13,12},{... | collective-permute-start | bytes 49160 | tf_op jit(solution)/shard_map/ppermute | solution.py:499
  62.8 19.4 %collective-permute-start.14 = (f32[8,32,256]{2,1,0:T(8,128)S(1)}, f32[8,32,256]{2,1,0:T(8,128)S(1)}, u32[]{:S(2)}, u32[]{:S(2)}) collective-permute-start(f32[8,32,256]{2,1,0:T(8,128)S(1)} %get-tuple-element.69), channel_id=1, source_target_pairs={{0,64},{16,80},{32,96},{48,112},{64,0},{80,16},{96,32},{112,48},{1... | collective-permute-start | bytes 786440 | tf_op jit(solution)/shard_map/ppermute | solution.py:534
  63.7 18.5 %collective-permute-start.13 = (f32[8,32,256]{2,1,0:T(8,128)S(1)}, f32[8,32,256]{2,1,0:T(8,128)S(1)}, u32[]{:S(2)}, u32[]{:S(2)}) collective-permute-start(f32[8,32,256]{2,1,0:T(8,128)S(1)} %get-tuple-element.68), channel_id=1, source_target_pairs={{0,16},{16,0},{32,48},{48,32},{64,80},{80,64},{96,112},{112,96},{1... | collective-permute-start | bytes 786440 | tf_op jit(solution)/shard_map/ppermute | solution.py:534
  64.6 17.6 %collective-permute-start.15 = (f32[8,32,256]{2,1,0:T(8,128)S(1)}, f32[8,32,256]{2,1,0:T(8,128)S(1)}, u32[]{:S(2)}, u32[]{:S(2)}) collective-permute-start(f32[8,32,256]{2,1,0:T(8,128)S(1)} %get-tuple-element.70), channel_id=1, source_target_pairs={{0,32},{16,48},{32,64},{48,80},{64,96},{80,112},{96,0},{112,16},{1... | collective-permute-start | bytes 786440 | tf_op jit(solution)/shard_map/ppermute | solution.py:534
  65.0 17.2 %collective-permute-start.16 = (f32[8,32,256]{2,1,0:T(8,128)S(1)}, f32[8,32,256]{2,1,0:T(8,128)S(1)}, u32[]{:S(2)}, u32[]{:S(2)}) collective-permute-start(f32[8,32,256]{2,1,0:T(8,128)S(1)} %get-tuple-element.71), channel_id=1, source_target_pairs={{0,96},{16,112},{32,0},{48,16},{64,32},{80,48},{96,64},{112,80},{1... | collective-permute-start | bytes 786440 | tf_op jit(solution)/shard_map/ppermute | solution.py:534
  67.3 7.1 %collective-permute-start.5 = (f32[128,256]{1,0:T(8,128)S(1)}, f32[128,256]{1,0:T(8,128)S(1)}, u32[]{:S(2)}, u32[]{:S(2)}) collective-permute-start(f32[128,256]{1,0:T(8,128)S(1)} %get-tuple-element.52), channel_id=1, source_target_pairs={{4,0},{8,4},{12,8},{5,1},{9,5},{13,9},{6,2},{10,6},{14,10},{7,3},{... | collective-permute-start | bytes 393224 | tf_op jit(solution)/shard_map/ppermute | solution.py:499
